TPU v7x, 512 devices: a whole 4x8x8 slice. The times are simulated.
512 devices in a mesh: dp: 8 (over y_hi, core), ep: 64 (over y_lo, x, z).
Axes of the slice: x: 4, y: 8 (y_hi: 4, y_lo: 2; y = y_hi * 2 + y_lo), z: 8, core: 2. Of those that a mesh axis runs over, the one named last changes fastest.
Arguments:
- latent_cache: bfloat16 [64, 16, 512, 576], P('ep', 'dp'), may hold values from -6 to 6
- lengths: int32 [64, 16], P(None, 'dp'), may hold values from 2 to 512
- new_home: int32 [64, 16], P(None, 'dp'), may hold values from 0 to 63, as said below
- queries: bfloat16 [2, 64, 16, 128, 576], P(None, 'ep', 'dp'), may hold values from -32 to 32
- new_latent: bfloat16 [2, 64, 16, 576], P(None, 'ep', 'dp'), may hold values from -6 to 6
- hidden: bfloat16 [2, 64, 16, 3584], P(None, 'ep', 'dp'), may hold values from -6 to 6
- routes: int32 [2, 64, 16, 8], P(None, 'ep', 'dp'), may hold values from 0 to 63, all different within a row; in each aligned block of 16 rows (0 to 15, 16 to 31, ..., all dimensions but the last counted through in order) at most 4 rows name the same one
- route_logits: bfloat16 [2, 64, 16, 8], P(None, 'ep', 'dp'), may hold values from -8 to 8
- w_gate: bfloat16 [64, 3584, 1024], P('ep', None, 'dp'), may hold values from -0.09375 to 0.09375
- w_up: bfloat16 [64, 3584, 1024], P('ep', None, 'dp'), may hold values from -0.09375 to 0.09375
- w_down: bfloat16 [64, 1024, 3584], P('ep', 'dp'), may hold values from -0.1875 to 0.1875
Outputs:
- attended: bfloat16 [2, 64, 16, 128, 512], P(None, 'ep', 'dp')
- moe_out: bfloat16 [2, 64, 16, 3584], P(None, 'ep', 'dp')
Inputs may be any that keep to these rules, and one draw needn't show every extreme that they name: `routes`: in each step, the 16 requests of one ep index name any one expert in at most 4 of their choices, and this bound is reached. For each request index c, new_home[., c] exchanges exactly two ep indices and leaves every other one in place, so new_home[new_home[e, c], c] == e; the two indices lie 64 // 2 apart for even c and 1 apart (modulo 64) for odd c.
All inputs are finite; a program needn't handle non-finite values.
Results may differ from a plain program's by a relative error of at most 0.0057.
Values may be sent and summed in bfloat16 or wider, within the bound.
No kernel may reach another device: no remote copies, remote signals or barrier semaphores. Data moves between devices by JAX's collectives and lax.ppermute only.
A program may use at most 128 MiB of HBM per device.

v0:
```python
import math

import jax
import jax.numpy as jnp
from jax import lax
from jax.sharding import Mesh
from jax.sharding import PartitionSpec as P

KV_RANK = 512
HEAD_QK = 192
EP = ("ep_0", "ep_1", "ep_2")


def broadcast_by_axis(x, axes, root):
    x = jnp.where(lax.axis_index(axes) == root, x, jnp.zeros_like(x))
    for axis in axes:
        x = lax.psum(x, axis)
    return x


def joined_along(tiles, dim):
    shape = list(tiles.shape[1:])
    shape[dim] *= tiles.shape[0]
    return jnp.moveaxis(tiles, 0, dim).reshape(shape)


def from_everyone(x, axis):
    copies = jnp.broadcast_to(x, (lax.axis_size(axis), *x.shape))
    return lax.all_to_all(copies, axis, split_axis=0, concat_axis=0, tiled=True)


def collect(x, axis, dim):
    return joined_along(from_everyone(x, axis), dim)


def in_blocks(x, dim, size):
    shape = x.shape
    tiles = x.reshape(*shape[:dim], size, shape[dim] // size, *shape[dim + 1 :])
    return jnp.moveaxis(tiles, dim, 0)


def summed_on_arrival(x, axis, dim):
    tiles = in_blocks(x, dim, lax.axis_size(axis))
    arrived = lax.all_to_all(tiles, axis, split_axis=0, concat_axis=0, tiled=True)
    return arrived.sum(axis=0)


def attend(query_rows, cache_rows, fresh_rows, length, softmax_scale):
    step_count, head_count, lat_width = query_rows.shape
    flat_query = query_rows.reshape(step_count * head_count, lat_width)
    total_keys = cache_rows.shape[0]
    key_block = math.gcd(128, total_keys)
    block_count = (length + key_block - 1) // key_block

    def score_block(block_index, buffer):
        key_rows = lax.dynamic_slice_in_dim(cache_rows, block_index * key_block, key_block, 0)
        block_scores = (
            jnp.dot(flat_query, key_rows.T, preferred_element_type=jnp.float32) * softmax_scale
        )
        key_place = block_index * key_block + jnp.arange(key_block, dtype=jnp.int32)
        block_scores = jnp.where(key_place[None, :] < length, block_scores, -jnp.inf)
        return lax.dynamic_update_slice_in_dim(buffer, block_scores, block_index * key_block, 1)

    empty_scores = jnp.full((step_count * head_count, total_keys), -jnp.inf, jnp.float32)
    cache_scores = lax.fori_loop(0, block_count, score_block, empty_scores)
    fresh_scores = (
        jnp.dot(flat_query, fresh_rows.T, preferred_element_type=jnp.float32) * softmax_scale
    )
    row_step = jnp.arange(step_count * head_count, dtype=jnp.int32) // head_count
    fresh_step = jnp.arange(step_count, dtype=jnp.int32)
    fresh_scores = jnp.where(fresh_step[None, :] <= row_step[:, None], fresh_scores, -jnp.inf)
    row_max = jnp.maximum(jnp.max(cache_scores, 1), jnp.max(fresh_scores, 1))[:, None]
    cache_weights = jnp.exp(cache_scores - row_max)
    fresh_weights = jnp.exp(fresh_scores - row_max)
    row_total = jnp.sum(cache_weights, 1, keepdims=True) + jnp.sum(fresh_weights, 1, keepdims=True)
    cache_probs = (cache_weights / row_total).astype(jnp.bfloat16)
    fresh_probs = (fresh_weights / row_total).astype(jnp.bfloat16)

    def value_block(block_index, value_sum):
        key_rows = lax.dynamic_slice_in_dim(cache_rows, block_index * key_block, key_block, 0)
        prob_block = lax.dynamic_slice_in_dim(cache_probs, block_index * key_block, key_block, 1)
        return value_sum + jnp.dot(
            prob_block, key_rows[:, :KV_RANK], preferred_element_type=jnp.float32
        )

    start_sum = jnp.dot(fresh_probs, fresh_rows[:, :KV_RANK], preferred_element_type=jnp.float32)
    value_sum = lax.fori_loop(0, block_count, value_block, start_sum)
    return value_sum.astype(jnp.bfloat16).reshape(step_count, head_count, KV_RANK)


def shards(
    latent_cache,
    lengths,
    new_home,
    queries,
    new_latent,
    hidden,
    routes,
    route_logits,
    w_gate,
    w_up,
    w_down,
):
    expert_count = lax.axis_size(EP)
    own_rank = lax.axis_index(EP)
    rank_ids = jnp.arange(expert_count, dtype=jnp.int32)
    softmax_scale = HEAD_QK ** (-0.5)
    step_count = queries.shape[0]
    attended_rows = []
    for request in range(latent_cache.shape[1]):
        home_ranks = new_home[:, request]
        anchor = home_ranks[own_rank]
        first_sender = jnp.argmax(home_ranks != rank_ids)
        second_sender = home_ranks[first_sender]
        own_cache = latent_cache[0, request]
        own_query = queries[:, 0, request]
        own_fresh = new_latent[:, 0, request]
        computed = attend(
            own_query, own_cache, own_fresh, lengths[own_rank, request], softmax_scale
        )
        result = computed
        for sender in (first_sender, second_sender):
            arrived = broadcast_by_axis(computed, EP, sender)
            result = jnp.where((anchor == sender) & (anchor != own_rank), arrived, result)
        attended_rows.append(result)
    attended = jnp.stack(attended_rows, 1)[:, None]
    gathered = (
        collect(hidden[:, 0], "dp", 1),
        collect(routes[:, 0], "dp", 1),
        collect(route_logits[:, 0], "dp", 1),
    )
    col_hidden, col_routes, col_logits = gathered
    column_rows = col_hidden.shape[1]
    top_count = routes.shape[3]
    model_width = hidden.shape[3]
    capacity = max(2, 2 * column_rows * top_count // expert_count)
    sigmoid_part = jax.nn.sigmoid(col_logits.astype(jnp.float32))
    gate_weights = 2.5 * sigmoid_part / jnp.sum(sigmoid_part, -1, keepdims=True)
    slot_ids = jnp.arange(expert_count * capacity, dtype=jnp.int32)

    def dispatch_plan(step_routes):
        flat_routes = step_routes.reshape(-1)
        onehot = (flat_routes[:, None] == rank_ids[None, :]).astype(jnp.int32)
        earlier = jnp.sum(jnp.cumsum(onehot, 0) * onehot, 1) - 1
        return flat_routes * capacity + earlier

    def build_buffer(step_hidden, placed):
        chosen = placed.reshape(column_rows, top_count)[None, :, :] == slot_ids[:, None, None]
        selector = jnp.any(chosen, 2).astype(jnp.bfloat16)
        filled = jnp.dot(selector, step_hidden, preferred_element_type=jnp.float32).astype(
            jnp.bfloat16
        )
        return filled.reshape(expert_count, capacity, model_width)

    def combine(returned, placed, step_gates):
        flat_out = returned.reshape(expert_count * capacity, model_width)
        picked = jnp.take(flat_out, placed, axis=0).astype(jnp.float32)
        weighted = picked * step_gates.reshape(-1)[:, None]
        return jnp.sum(weighted.reshape(column_rows, top_count, model_width), 1)

    placements = [dispatch_plan(col_routes[number]) for number in range(step_count)]
    buffers = [build_buffer(col_hidden[number], placements[number]) for number in range(step_count)]
    joined = jnp.concatenate(buffers, 1)
    received = lax.all_to_all(joined, EP, split_axis=0, concat_axis=0, tiled=True)
    source_count, item_count, _ = received.shape
    flat_rows = received.reshape(source_count * item_count, model_width)
    gate_part = jnp.dot(flat_rows, w_gate[0], preferred_element_type=jnp.float32)
    up_part = jnp.dot(flat_rows, w_up[0], preferred_element_type=jnp.float32)
    hidden_units = (jax.nn.silu(gate_part) * up_part).astype(jnp.bfloat16)
    partial_value = jnp.dot(hidden_units, w_down[0], preferred_element_type=jnp.float32).astype(
        jnp.bfloat16
    )
    returned_all = lax.all_to_all(
        partial_value.reshape(source_count, item_count, model_width),
        EP,
        split_axis=0,
        concat_axis=0,
        tiled=True,
    )
    returned_list = [
        returned_all[:, number * capacity : (number + 1) * capacity] for number in range(step_count)
    ]
    partials = jnp.stack(
        [
            combine(returned_list[number], placements[number], gate_weights[number])
            for number in range(step_count)
        ],
        0,
    )
    summed = summed_on_arrival(partials, "dp", 1)
    moe_out = summed.astype(jnp.bfloat16)[:, None]
    return (attended, moe_out)


def solution(mesh):
    torus = Mesh(mesh.devices.reshape(mesh.shape["dp"], 2, 4, 8), ("dp", "ep_0", "ep_1", "ep_2"))
    placed = (
        P(EP, "dp", None, None),
        P(None, "dp"),
        P(None, "dp"),
        P(None, EP, "dp", None, None),
        P(None, EP, "dp", None),
        P(None, EP, "dp", None),
        P(None, EP, "dp", None),
        P(None, EP, "dp", None),
        P(EP, None, "dp"),
        P(EP, None, "dp"),
        P(EP, "dp", None),
    )
    return jax.shard_map(
        shards,
        mesh=torus,
        in_specs=placed,
        out_specs=(P(None, EP, "dp", None, None), P(None, EP, "dp", None)),
        check_vma=False,
    )
```

profile of v0, /device:TPU:1, one launch (start us, length us, event | category | flops | bytes accessed | tf_op | source)
XLA Modules:
  0.0 410.7 jit_solution(6807647515131898374)
XLA Ops:
  7.2 0.8 broadcast_in_dim.66
  7.9 16.3 %all_to_all.30 = s32[8,2,2,8]{3,2,1,0:T(2,128)S(1)} all-to-all(s32[8,2,2,8]{3,2,1,0:T(2,128)S(1)} %broadcast_in_dim.66), channel_id=1, replica_groups=mesh['dp'=8,'ep_0'=2,'ep_1'=4,'ep_2'=8] {'dp'}, dimensions={0} | all-to-all | bytes 2048 | tf_op jit(solution)/shard_map/all_to_all | solution.py:29
  24.2 1.6 broadcast_in_dim.67
  25.8 4.0 all-to-all-start.1
  31.4 8.7 %all-to-all-done.1 = bf16[8,2,2,3584]{3,2,1,0:T(2,128)(2,1)S(1)} async-done(((bf16[8,2,2,3584]{3,2,1,0:T(2,128)(2,1)}), bf16[8,2,2,3584]{3,2,1,0:T(2,128)(2,1)S(1)}, u32[]{:S(2)}, u32[]{:S(2)}) %all-to-all-start.1) | async-done | bytes 229408 | tf_op jit(solution)/shard_map/all_to_all | solution.py:29
  40.2 1.9 convolution_convert_fusion.2
  42.2 3.1 reshape.164
  45.4 1.9 convolution_convert_fusion.1
  47.3 4.1 reshape.165
  51.4 5.1 %pad_maximum_fusion = bf16[64,8,3584]{2,1,0:T(8,128)(2,1)} fusion(bf16[64,4,3584]{2,1,0:T(4,128)(2,1)} %reshape.165, bf16[64,4,3584]{2,1,0:T(4,128)(2,1)S(1)} %reshape.164), kind=kLoop, calls=%fused_computation.28 | loop fusion | flops 7340032 | bytes 7340032 | tf_op jit(solution)/shard_map/concatenate | solution.py:163
  56.5 12.1 %all-to-all-start.2 = ((bf16[64,8,3584]{2,1,0:T(8,128)(2,1)}), bf16[64,8,3584]{2,1,0:T(8,128)(2,1)}, u32[]{:S(2)}, u32[]{:S(2)}) async-start(bf16[64,8,3584]{2,1,0:T(8,128)(2,1)} %pad_maximum_fusion), calls=%async_computation.2 | async-start | bytes 7340032 | tf_op jit(solution)/shard_map/all_to_all | solution.py:164
  68.6 0.7 compare_reduce_fusion
  71.2 0.7 constant_dynamic-slice_fusion.1
  72.6 0.7 compare_reduce_fusion.1
  76.7 0.9 fusion.61
  77.6 0.3 copy.74
  77.9 0.8 fusion.62
  79.0 0.9 while.40
  79.0 0.7 add_compare_fusion.4
  81.0 71.5 %all-to-all-done.2 = bf16[64,8,3584]{2,1,0:T(8,128)(2,1)} async-done(((bf16[64,8,3584]{2,1,0:T(8,128)(2,1)}), bf16[64,8,3584]{2,1,0:T(8,128)(2,1)}, u32[]{:S(2)}, u32[]{:S(2)}) %all-to-all-start.2) | async-done | bytes 3670048 | tf_op jit(solution)/shard_map/all_to_all | solution.py:164
  152.5 0.6 broadcast_in_dim.68
  153.1 7.4 %all-to-all-start.4 = ((bf16[8,2,2,8]{3,2,1,0:T(2,128)(2,1)}), bf16[8,2,2,8]{3,2,1,0:T(2,128)(2,1)S(1)}, u32[]{:S(2)}, u32[]{:S(2)}) async-start(bf16[8,2,2,8]{3,2,1,0:T(2,128)(2,1)} %broadcast_in_dim.68), calls=%async_computation.4 | async-start | bytes 16384 | tf_op jit(solution)/shard_map/all_to_all | solution.py:29
  160.5 3.4 fusion.19
  163.9 8.1 %fusion.16 = bf16[64,8,3584]{2,1,0:T(8,128)(2,1)} fusion(bf16[1,128,3584]{2,1,0:T(8,128)(2,1)S(1)} %copy-done, bf16[64,8,3584]{2,1,0:T(8,128)(2,1)} %all-to-all-done.2, bf16[1,3584,128]{2,1,0:T(8,128)(2,1)} %param.30, f32[512,128]{1,0:T(8,128)S(1)} %fusion.19), kind=kOutput, calls=%fused_computation.25 | convolution fusion | flops 941752320 | bytes 9437184 | tf_op jit(solution)/shard_map/dot_general | solution.py:170
  172.0 7.4 %all-to-all-start.3 = ((bf16[64,8,3584]{2,1,0:T(8,128)(2,1)}), bf16[64,8,3584]{2,1,0:T(8,128)(2,1)}, u32[]{:S(2)}, u32[]{:S(2)}) async-start(bf16[64,8,3584]{2,1,0:T(8,128)(2,1)} %fusion.16), calls=%async_computation.3 | async-start | bytes 7340032 | tf_op jit(solution)/shard_map/all_to_all | solution.py:173
  179.4 0.3 fusion.51
  180.7 0.6 constant_dynamic-slice_fusion.4
  182.0 0.3 copy.75
  182.6 1.0 while.42
  182.6 0.7 add_compare_fusion.5
  184.4 0.3 fusion.49
  185.8 0.8 broadcast_select_fusion.2
  186.7 0.8 broadcast_select_fusion
  187.6 73.7 %all-reduce.11.cloned.1.call-done = (bf16[2,128,512]{2,1,0:T(8,128)(2,1)}, bf16[2,128,512]{2,1,0:T(8,128)(2,1)}, bf16[2,128,512]{2,1,0:T(8,128)(2,1)}, bf16[2,128,512]{2,1,0:T(8,128)(2,1)}) async-done(((bf16[2,128,512]{2,1,0:T(8,128)(2,1)}, bf16[2,128,512]{2,1,0:T(8,128)(2,1)}, bf16[2,128,512]{2,1,0:T(8,128)(2,1)}, bf16[2,128,512]{2,1,0:T(8,128)(2,1)}), (bf16[2,128,512]{2,1,0:T(8,128)(2,1)}, ...) | async-done | bytes 1048592 | tf_op jit(solution)/shard_map/psum | solution.py:17
  261.9 57.9 %all-reduce.9.cloned.1.call-done = (bf16[2,128,512]{2,1,0:T(8,128)(2,1)}, bf16[2,128,512]{2,1,0:T(8,128)(2,1)}, bf16[2,128,512]{2,1,0:T(8,128)(2,1)}, bf16[2,128,512]{2,1,0:T(8,128)(2,1)}) async-done(((bf16[2,128,512]{2,1,0:T(8,128)(2,1)}, bf16[2,128,512]{2,1,0:T(8,128)(2,1)}, bf16[2,128,512]{2,1,0:T(8,128)(2,1)}, bf16[2,128,512]{2,1,0:T(8,128)(2,1)}), (bf16[2,128,512]{2,1,0:T(8,128)(2,1)}, ...) | async-done | bytes 1048592 | tf_op jit(solution)/shard_map/psum | solution.py:17
  319.9 6.4 %fusion.60 = (bf16[64,4,3584]{2,1,0:T(4,128)(2,1)}, bf16[64,4,3584]{2,1,0:T(4,128)(2,1)}) fusion(bf16[64,8,3584]{2,1,0:T(8,128)(2,1)} %all-to-all-done.3), kind=kLoop, calls=%fused_computation.119 | loop fusion | bytes 7340032 | tf_op jit(solution)/shard_map/slice | solution.py:181
  326.3 2.9 reshape.168
  329.2 2.0 gather_fusion
  331.3 1.9 bitcast_reduce_fusion.1
  333.2 0.8 stack.21
  334.0 2.9 reshape.170
  337.0 2.1 gather_fusion.1
  339.0 1.9 bitcast_reduce_fusion
  341.1 1.9 maximum_bitcast_fusion.1
  343.0 8.6 %all-to-all-start.5 = ((f32[8,2,2,3584]{3,2,1,0:T(2,128)}), f32[8,2,2,3584]{3,2,1,0:T(2,128)S(1)}, u32[]{:S(2)}, u32[]{:S(2)}) async-start(f32[8,2,2,3584]{3,2,1,0:T(2,128)} %maximum_bitcast_fusion.1), calls=%async_computation.5 | async-start | bytes 917504 | tf_op jit(solution)/shard_map/all_to_all | solution.py:44
  358.1 44.4 %all-reduce.7.cloned.1.call-done = (bf16[2,128,512]{2,1,0:T(8,128)(2,1)}, bf16[2,128,512]{2,1,0:T(8,128)(2,1)}, bf16[2,128,512]{2,1,0:T(8,128)(2,1)}, bf16[2,128,512]{2,1,0:T(8,128)(2,1)}) async-done(((bf16[2,128,512]{2,1,0:T(8,128)(2,1)}, bf16[2,128,512]{2,1,0:T(8,128)(2,1)}, bf16[2,128,512]{2,1,0:T(8,128)(2,1)}, bf16[2,128,512]{2,1,0:T(8,128)(2,1)}), (bf16[2,128,512]{2,1,0:T(8,128)(2,1)}, ...) | async-done | bytes 1048592 | tf_op jit(solution)/shard_map/psum | solution.py:17
  402.6 0.8 maximum_bitcast_fusion
  403.4 0.8 reduce_sum.99
  (93 shorter events, 6.7 us)
Async XLA Ops:
  7.2 156.7 %copy-start = (bf16[1,128,3584]{2,1,0:T(8,128)(2,1)S(1)}, bf16[1,128,3584]{2,1,0:T(8,128)(2,1)}, u32[]{:S(2)}) copy-start(bf16[1,128,3584]{2,1,0:T(8,128)(2,1)} %param.31) | copy-start | bytes 2752516
  25.8 14.2 %all-to-all-start.1 = ((bf16[8,2,2,3584]{3,2,1,0:T(2,128)(2,1)}), bf16[8,2,2,3584]{3,2,1,0:T(2,128)(2,1)S(1)}, u32[]{:S(2)}, u32[]{:S(2)}) async-start(bf16[8,2,2,3584]{3,2,1,0:T(2,128)(2,1)} %broadcast_in_dim.67), calls=%async_computation.1 | async-start | bytes 458752 | tf_op jit(solution)/shard_map/all_to_all | solution.py:29
  56.5 12.1 %copy-start.8 = (s32[64,2]{0,1:T(2,128)S(1)}, s32[64,2]{0,1:T(2,128)}, u32[]{:S(2)}) copy-start(s32[64,2]{0,1:T(2,128)} %param.23) | copy-start | bytes 1540
  56.5 14.8 %copy-start.6 = (s32[64,2]{0,1:T(2,128)S(1)}, s32[64,2]{0,1:T(2,128)}, u32[]{:S(2)}) copy-start(s32[64,2]{0,1:T(2,128)} %param.22) | copy-start | bytes 1540
  56.5 20.2 %copy-start.2 = (bf16[1,2,512,576]{2,3,1,0:T(8,128)(2,1)S(1)}, bf16[1,2,512,576]{2,3,1,0:T(8,128)(2,1)}, u32[]{:S(2)}) copy-start(bf16[1,2,512,576]{2,3,1,0:T(8,128)(2,1)} %param.21) | copy-start | bytes 3538948
  56.5 96.0 %all-to-all-start.2 = ((bf16[64,8,3584]{2,1,0:T(8,128)(2,1)}), bf16[64,8,3584]{2,1,0:T(8,128)(2,1)}, u32[]{:S(2)}, u32[]{:S(2)}) async-start(bf16[64,8,3584]{2,1,0:T(8,128)(2,1)} %pad_maximum_fusion), calls=%async_computation.2 | async-start | bytes 7340032 | tf_op jit(solution)/shard_map/all_to_all | solution.py:164
  71.9 6.0 %copy-start.4 = (bf16[2,1,2,128,576]{3,4,2,1,0:T(8,128)(2,1)S(1)}, bf16[2,1,2,128,576]{3,4,2,1,0:T(8,128)(2,1)}, u32[]{:S(2)}) copy-start(bf16[2,1,2,128,576]{3,4,2,1,0:T(8,128)(2,1)} %param.24) | copy-start | bytes 1769476
  78.9 1.3 copy-start.5
  79.9 72.6 %copy-start.7 = (bf16[2,1,2,8]{3,2,1,0:T(2,128)(2,1)S(1)}, bf16[2,1,2,8]{3,2,1,0:T(2,128)(2,1)}, u32[]{:S(2)}) copy-start(bf16[2,1,2,8]{3,2,1,0:T(2,128)(2,1)} %param.28) | copy-start | bytes 196
  153.1 18.9 %all-to-all-start.4 = ((bf16[8,2,2,8]{3,2,1,0:T(2,128)(2,1)}), bf16[8,2,2,8]{3,2,1,0:T(2,128)(2,1)S(1)}, u32[]{:S(2)}, u32[]{:S(2)}) async-start(bf16[8,2,2,8]{3,2,1,0:T(2,128)(2,1)} %broadcast_in_dim.68), calls=%async_computation.4 | async-start | bytes 16384 | tf_op jit(solution)/shard_map/all_to_all | solution.py:29
  172.0 147.9 %all-to-all-start.3 = ((bf16[64,8,3584]{2,1,0:T(8,128)(2,1)}), bf16[64,8,3584]{2,1,0:T(8,128)(2,1)}, u32[]{:S(2)}, u32[]{:S(2)}) async-start(bf16[64,8,3584]{2,1,0:T(8,128)(2,1)} %fusion.16), calls=%async_computation.3 | async-start | bytes 7340032 | tf_op jit(solution)/shard_map/all_to_all | solution.py:173
  179.3 81.9 %all-reduce.11.cloned.1.call-start = ((), (), s32[]{:S(2)}) async-start(), calls=%async_computation.8 | async-start | bytes 2097152 | tf_op jit(solution)/shard_map/psum | solution.py:17
  179.7 2.4 copy-start.1
  180.0 2.4 copy-start.3
  187.5 132.3 %all-reduce.9.cloned.1.call-start = ((), (), s32[]{:S(2)}) async-start(), calls=%async_computation.7 | async-start | bytes 2097152 | tf_op jit(solution)/shard_map/psum | solution.py:17
  261.3 141.2 %all-reduce.7.cloned.1.call-start = ((), (), s32[]{:S(2)}) async-start(), calls=%async_computation.6 | async-start | bytes 2097152 | tf_op jit(solution)/shard_map/psum | solution.py:17
  343.0 60.4 %all-to-all-start.5 = ((f32[8,2,2,3584]{3,2,1,0:T(2,128)}), f32[8,2,2,3584]{3,2,1,0:T(2,128)S(1)}, u32[]{:S(2)}, u32[]{:S(2)}) async-start(f32[8,2,2,3584]{3,2,1,0:T(2,128)} %maximum_bitcast_fusion.1), calls=%async_computation.5 | async-start | bytes 917504 | tf_op jit(solution)/shard_map/all_to_all | solution.py:44
Sparse Core Ops, SparseCore 0:
  187.6 73.5 all-reduce.10
  264.0 55.8 all-reduce.8
  322.4 79.9 all-reduce.6
where the time goes:
time: 416 us; the launch traced here: 411 us
  waiting for transfers between devices  256 us (62%)
  starting transfers between devices  39.6 us (10%)
  local copies, waits for them, and re-layouts  33 us (8%)
  between operations  28.7 us (7%)
  other arithmetic  19.5 us (5%)
  matrix products  17.3 us (4%)
  blocking collectives  16.3 us (4%)
    psum x3, waiting for transfers between devices, broadcast_by_axis(): x = lax.psum(x, axis)  176 us
    all_to_all x1, waiting for transfers between devices, shards(): lax.all_to_all(joined, EP, split_axis=0, concat_axis=0, tiled=True)  71.5 us
    all_to_all x1, blocking collectives, from_everyone(): return lax.all_to_all(copies, axis, split_axis=0, concat_axis=0, tiled=True)  16.3 us
    all_to_all x1, starting transfers between devices, shards(): lax.all_to_all(joined, EP, split_axis=0, concat_axis=0, tiled=True)  12.1 us
    all_to_all x2, starting transfers between devices, from_everyone(): return lax.all_to_all(copies, axis, split_axis=0, concat_axis=0, tiled=True)  11.4 us
    all_to_all x2, waiting for transfers between devices, from_everyone(): return lax.all_to_all(copies, axis, split_axis=0, concat_axis=0, tiled=True)  8.65 us
    all_to_all x1, starting transfers between devices, summed_on_arrival(): lax.all_to_all(tiles, axis, split_axis=0, concat_axis=0, tiled=True)  8.59 us
  transfers between devices with their start and end apart: 8, of which 5 were waited for; matrix products, arithmetic and copies ran while one was open for 12% of the time, Pallas kernels for 0%

commit v1 on v0

v1 whole, which is shorter than its diff:
```python
import functools

import jax
import jax.numpy as jnp
from jax import lax
from jax.experimental import pallas as pl
from jax.experimental.pallas import tpu as pltpu
from jax.sharding import Mesh
from jax.sharding import PartitionSpec as P

KV_RANK = 512
HEAD_QK = 192
CAP = 4
EP = ("yl", "x", "z")
DP = ("yh", "c")
BF = jnp.bfloat16
F32 = jnp.float32
PARAMS = pltpu.CompilerParams(vmem_limit_bytes=48 * 1024 * 1024)


def dot(a, b, dims=((1,), (0,))):
    return lax.dot_general(a, b, (dims, ((), ())), preferred_element_type=F32)


def iota(shape, dim):
    return lax.broadcasted_iota(jnp.int32, shape, dim)


def vmem(n):
    return [pl.BlockSpec(memory_space=pltpu.VMEM)] * n


def attend_kernel(len_ref, query_ref, cache_ref, fresh_ref, out0_ref, out1_ref, keys_ref):
    steps, _, requests, heads, width = query_ref.shape
    cached = cache_ref.shape[2]
    total = keys_ref.shape[0]
    rows = steps * heads
    column = iota((rows, total), 1)
    row_step = iota((rows, total), 0) // heads
    for request, out_ref in zip(range(requests), (out0_ref, out1_ref)):
        keys_ref[:cached] = cache_ref[0, request]
        place = iota((total - cached, width), 0)
        tail = jnp.zeros((total - cached, width), F32)
        for step in range(steps):
            row = fresh_ref[step, 0, request : request + 1, :].astype(F32)
            tail = jnp.where(place == step, row, tail)
        keys_ref[cached:] = tail.astype(BF)
        query = query_ref[:, 0, request].reshape(rows, width)
        keys = keys_ref[...]
        scores = dot(query, keys, ((1,), (1,))) * (HEAD_QK**-0.5)
        old = column < len_ref[request]
        new = (column >= cached) & (column - cached <= row_step)
        scores = jnp.where(old | new, scores, -jnp.inf)
        weights = jnp.exp(scores - jnp.max(scores, 1, keepdims=True))
        probs = (weights / jnp.sum(weights, 1, keepdims=True)).astype(BF)
        served = dot(probs, keys[:, :KV_RANK]).astype(BF)
        out_ref[...] = served.reshape(steps, heads, KV_RANK)


def attend(length, queries, cache, fresh):
    steps, _, _, heads, width = queries.shape
    out = jax.ShapeDtypeStruct((steps, heads, KV_RANK), BF)
    return pl.pallas_call(
        attend_kernel,
        out_shape=(out, out),
        in_specs=[pl.BlockSpec(memory_space=pltpu.SMEM), *vmem(3)],
        out_specs=tuple(vmem(2)),
        scratch_shapes=[pltpu.VMEM((cache.shape[2] + 128, width), BF)],
        compiler_params=PARAMS,
        name="attend",
    )(length, queries, cache, fresh)


def dispatch_kernel(tokens_ref, send_ref, mix_ref):
    rows = tokens_ref.shape[0]
    slots, half = send_ref.shape
    width = 2 * half
    tail = tokens_ref[:, width:].astype(F32)
    top = tail.shape[1] // 2
    sigmoid = jax.nn.sigmoid(tail[:, top:])
    gates = 2.5 * sigmoid / jnp.sum(sigmoid, 1, keepdims=True)
    slot = iota((rows, slots), 1)
    expert = (slot // 8).astype(F32)
    named = jnp.zeros((rows, slots), F32)
    gate = jnp.zeros((rows, slots), F32)
    for k in range(top):
        hit = tail[:, k : k + 1] == expert
        named = jnp.where(hit, 1.0, named)
        gate = jnp.where(hit, gates[:, k : k + 1], gate)
    before = (iota((rows, rows), 1) < iota((rows, rows), 0)).astype(F32)
    earlier = dot(before.astype(BF), named.astype(BF))
    chosen = (named > 0) & (earlier == (slot % 4).astype(F32))
    left = chosen & (slot % 8 < 4)
    right = chosen & (slot % 8 >= 4)
    picks = (left.astype(F32).astype(BF), right.astype(F32).astype(BF))
    over_rows = ((0,), (0,))
    send = dot(picks[0], tokens_ref[:, :half], over_rows)
    send = send + dot(picks[1], tokens_ref[:, half:width], over_rows)
    send_ref[...] = send.astype(BF)
    high = gate.astype(BF).astype(F32)
    low = gate - high
    mix = [jnp.where(side, part, 0.0) for part in (high, low) for side in (left, right)]
    mix_ref[...] = jnp.concatenate(mix, 0).astype(BF)


def dispatch(tokens, slots, half):
    return pl.pallas_call(
        dispatch_kernel,
        out_shape=(
            jax.ShapeDtypeStruct((slots, half), BF),
            jax.ShapeDtypeStruct((4 * tokens.shape[0], slots), BF),
        ),
        in_specs=vmem(1),
        out_specs=tuple(vmem(2)),
        compiler_params=PARAMS,
        name="dispatch",
    )(tokens)


def hidden_kernel(rows_ref, own_ref, peer_ref, out_ref):
    slots, half = rows_ref.shape
    units = own_ref.shape[1] // 2
    rows = rows_ref[...]
    parts = []
    for ref in (own_ref, peer_ref):
        upper = dot(rows, ref[:half])
        lower = dot(rows, ref[half:])
        both = upper + pltpu.roll(lower, slots - 4, 0)
        gate, up = both[:, :units], both[:, units:]
        parts.append(gate / (1.0 + jnp.exp(-gate)) * up)
    value = jnp.concatenate(parts, 1)
    value = jnp.where(iota(value.shape, 0) % 8 < 4, value, 0.0).astype(BF)
    row, slot = iota((slots // 2, slots), 0), iota((slots // 2, slots), 1)
    pick = (slot == row // 4 * 8 + row % 4).astype(F32).astype(BF)
    out_ref[...] = dot(pick, value).astype(BF)


def hidden_units(rows, own, peer):
    return pl.pallas_call(
        hidden_kernel,
        out_shape=jax.ShapeDtypeStruct((rows.shape[0] // 2, own.shape[1]), BF),
        in_specs=vmem(3),
        out_specs=vmem(1)[0],
        compiler_params=PARAMS,
        name="hidden_units",
    )(rows, own, peer)


def down_kernel(h0, h1, h2, h3, own_ref, peer_ref, out_ref):
    slots, part = out_ref.shape
    total = None
    for number, ref in enumerate((h0, h1, h2, h3)):
        weights = jnp.concatenate([own_ref[number], peer_ref[number]], 0)
        term = dot(ref[...], weights)
        total = term if total is None else total + term
    value = total.astype(BF)
    rest = value.shape[1] - part
    slot, row = iota((slots, slots // 2), 0), iota((slots, slots // 2), 1)
    match = slot // 8 * 4 + slot % 4 == row
    left = (match & (slot % 8 < 4)).astype(F32).astype(BF)
    right = (match & (slot % 8 >= 4)).astype(F32).astype(BF)
    first, second = dot(left, value[:, :part]), dot(right, value[:, part:])
    out_ref[:, :rest] = (first[:, :rest] + second).astype(BF)
    out_ref[:, rest:] = first[:, rest:].astype(BF)


def down(hs, own, peer, part):
    rows = hs[0].shape[0]
    return pl.pallas_call(
        down_kernel,
        out_shape=jax.ShapeDtypeStruct((2 * rows, part), BF),
        in_specs=vmem(6),
        out_specs=vmem(1)[0],
        compiler_params=PARAMS,
        name="down",
    )(*hs, own, peer)


def combine_kernel(mix_ref, back_ref, out_ref):
    rows = mix_ref.shape[0] // 4
    part = back_ref.shape[1]
    rest = out_ref.shape[1] - part
    value = dot(mix_ref[...], back_ref[...])
    value = value[: 2 * rows] + value[2 * rows :]
    out_ref[:, :part] = value[:rows].astype(BF)
    out_ref[:, part:] = value[rows:, :rest].astype(BF)


def combine(mix, back, width):
    return pl.pallas_call(
        combine_kernel,
        out_shape=jax.ShapeDtypeStruct((mix.shape[0] // 4, width), BF),
        in_specs=vmem(2),
        out_specs=vmem(1)[0],
        compiler_params=PARAMS,
        name="combine",
    )(mix, back)


def exchange(x, axes):
    return lax.all_to_all(x, axes, split_axis=0, concat_axis=0, tiled=True)


def shifted(x, axes, by):
    size = lax.axis_size(axes)
    return lax.ppermute(x, axes, [(i, (i + by) % size) for i in range(size)])


def shards(
    latent_cache,
    lengths,
    new_home,
    queries,
    new_latent,
    hidden,
    routes,
    route_logits,
    w_gate,
    w_up,
    w_down,
):
    experts = lax.axis_size(EP)
    yh_size = lax.axis_size("yh")
    own_rank = lax.axis_index(EP)
    yh = lax.axis_index("yh")
    steps, _, requests, width = hidden.shape
    half = width // 2
    chunk = width // yh_size
    part = (chunk // 2 + 127) // 128 * 128
    slots = experts * 2 * CAP

    packed = jnp.concatenate([hidden, routes.astype(BF), route_logits], -1)[:, 0]
    packed = jnp.broadcast_to(packed[None], (yh_size, *packed.shape))
    tokens = exchange(packed.reshape(-1, *packed.shape[2:]), DP)
    tokens = tokens.reshape(-1, tokens.shape[-1])
    send, mix = dispatch(tokens, slots, half)
    arrived = exchange(send.reshape(experts, 2 * CAP, half), EP).reshape(slots, half)

    own_w = jnp.concatenate([w_gate[0], w_up[0]], 1)
    peer_w = shifted(own_w, "c", 1)
    down_blocks = [
        lax.dynamic_slice_in_dim(w_down[0], (yh + s) % yh_size * chunk, chunk, 1)
        for s in range(yh_size)
    ]
    own_down = jnp.stack([shifted(x, "yh", s) if s else x for s, x in enumerate(down_blocks)])
    peer_down = shifted(own_down, "c", 1)

    served0, served1 = attend(lengths[own_rank], queries, latent_cache, new_latent)
    far = shifted(served0, EP, experts // 2)
    lower = shifted(served1, EP, 1)
    upper = shifted(served1, EP, -1)
    home = new_home[own_rank]
    result0 = jnp.where(home[0] == own_rank, served0, far)
    result1 = jnp.where(
        home[1] == own_rank,
        served1,
        jnp.where(home[1] == (own_rank + 1) % experts, upper, lower),
    )
    attended = jnp.stack([result0, result1], 1)[:, None]

    h = hidden_units(arrived, own_w, peer_w)
    hs = [h, *(shifted(h, "yh", s) for s in range(1, yh_size))]
    out = down(hs, own_down, peer_down, part)
    back = exchange(out.reshape(experts, 2 * CAP, part), EP).reshape(slots, part)
    mixed = combine(mix, back, chunk)
    final = exchange(mixed.reshape(-1, requests, chunk), DP)
    final = final.reshape(yh_size, steps, requests, chunk).transpose(1, 2, 0, 3)
    moe_out = final.reshape(steps, 1, requests, width)
    return attended, moe_out


def solution(mesh):
    torus = Mesh(mesh.devices.reshape(4, 2, 2, 4, 8), ("yh", "c", "yl", "x", "z"))
    placed = (
        P(EP, DP, None, None),
        P(None, DP),
        P(None, DP),
        P(None, EP, DP, None, None),
        P(None, EP, DP, None),
        P(None, EP, DP, None),
        P(None, EP, DP, None),
        P(None, EP, DP, None),
        P(EP, None, DP),
        P(EP, None, DP),
        P(EP, DP, None),
    )
    return jax.shard_map(
        shards,
        mesh=torus,
        in_specs=placed,
        out_specs=(P(None, EP, DP, None, None), P(None, EP, DP, None)),
        check_vma=False,
    )
```

time: 416 us -> 166 us (0.40); the launches traced: 411 us -> 165 us
  waiting for transfers between devices: 256 us -> 48.8 us
  starting transfers between devices: 39.6 us -> 72.3 us
  between operations: 28.7 us -> 3.04 us
  local copies, waits for them, and re-layouts: 33 us -> 8.54 us
  matrix products: 17.3 us -> 0 us
  other arithmetic: 19.5 us -> 3.55 us
  Pallas kernels: 0 us -> 11.5 us
    psum x3 -> x0, waiting for transfers between devices: 176 us -> none  [broadcast_by_axis(): x = lax.psum(x, axis)]
    all_to_all x5 -> x3, waiting for transfers between devices: 80.2 us -> 6.31 us  [exchange(): return lax.all_to_all(x, axes, split_axis=0, concat_axis=0, tiled=True)]
    ppermute x0 -> x11, waiting for transfers between devices: none -> 42.5 us  [shifted(): return lax.ppermute(x, axes, [(i, (i + by) % size) for i in range(size)])]
    ppermute x0 -> x11, starting transfers between devices: none -> 41.1 us  [shifted(): return lax.ppermute(x, axes, [(i, (i + by) % size) for i in range(size)])]
    dot_general x12 -> x0, matrix products: 17.3 us -> none  [the longest x1 8.05 us: shards(): jnp.dot(hidden_units, w_down[0], preferred_element_type=jnp.float32)]
    reshape x4, local copies, waits for them, and re-layouts: 13.1 us -> 1.38 us  [the longest x1 0.65 us: shards(): final = exchange(mixed.reshape(-1, requests, chunk), DP)]
    pallas_call x0 -> x5, Pallas kernels: none -> 11.5 us  [the longest x1 4.39 us: hidden_units(): pl.pallas_call(hidden_kernel, out_shape=jax.ShapeDtypeStruct((rows.shape[...]
    all_to_all x5 -> x3, starting transfers between devices: 39.5 us -> 31.2 us  [exchange(): return lax.all_to_all(x, axes, split_axis=0, concat_axis=0, tiled=True)]
  transfers between devices with their start and end apart: 8 -> 14, of which waited for: 5 -> 7; matrix products, arithmetic and copies ran while one was open for 12% -> 5% of each run, Pallas kernels for 0% -> 4%
where the time goes in v1:
time: 166 us; the launch traced here: 165 us
  starting transfers between devices  72.3 us (44%)
  waiting for transfers between devices  48.8 us (29%)
  blocking collectives  17.1 us (10%)
  Pallas kernels  11.5 us (7%)
  local copies, waits for them, and re-layouts  8.54 us (5%)
  other arithmetic  3.55 us (2%)
  between operations  3.04 us (2%)
    ppermute x11, waiting for transfers between devices, shifted(): return lax.ppermute(x, axes, [(i, (i + by) % size) for i in range(size)])  42.5 us
    ppermute x11, starting transfers between devices, shifted(): return lax.ppermute(x, axes, [(i, (i + by) % size) for i in range(size)])  41.1 us
    all_to_all x3, starting transfers between devices, exchange(): return lax.all_to_all(x, axes, split_axis=0, concat_axis=0, tiled=True)  31.2 us
    all_to_all x1, blocking collectives, exchange(): return lax.all_to_all(x, axes, split_axis=0, concat_axis=0, tiled=True)  17.1 us
    all_to_all x3, waiting for transfers between devices, exchange(): return lax.all_to_all(x, axes, split_axis=0, concat_axis=0, tiled=True)  6.31 us
    pallas_call x1, Pallas kernels, hidden_units(): pl.pallas_call(hidden_kernel, out_shape=jax.ShapeDtypeStruct((rows.shape[...  4.39 us
    unnamed x15, local copies, waits for them, and re-layouts  4.1 us
  transfers between devices with their start and end apart: 14, of which 7 were waited for; matrix products, arithmetic and copies ran while one was open for 5% of the time, Pallas kernels for 4%

profile of v1, /device:TPU:1, one launch (start us, length us, event | category | flops | bytes accessed | tf_op | source)
XLA Modules:
  0.0 164.9 jit_solution(3634051817923358063)
XLA Ops:
  0.6 0.7 convert_element_type.3
  1.3 0.8 concatenate.6
  2.2 0.1 broadcast_in_dim.12
  2.2 17.1 %all_to_all.20 = bf16[8,2,3600]{2,1,0:T(2,128)(2,1)S(1)} all-to-all(bf16[8,2,3600]{2,1,0:T(2,128)(2,1)S(1)} %bitcast.34), channel_id=1, replica_groups=mesh['yh'=4,'c'=2,'yl'=2,'x'=4,'z'=8] {'yh','c'}, dimensions={0} | all-to-all | bytes 230400 | tf_op jit(solution)/shard_map/all_to_all | solution.py:201
  19.4 0.1 reshape.42.tokens_ref
  19.5 1.4 dispatch.1
  20.9 1.3 copy-done
  22.1 13.0 %all-to-all-start.1 = ((bf16[64,8,1792]{2,1,0:T(8,128)(2,1)}), bf16[64,8,1792]{2,1,0:T(8,128)(2,1)S(1)}, u32[]{:S(2)}, u32[]{:S(2)}) async-start(bf16[64,8,1792]{2,1,0:T(8,128)(2,1)} %bitcast.31), calls=%async_computation.1 | async-start | bytes 3670016 | tf_op jit(solution)/shard_map/all_to_all | solution.py:201
  35.1 2.6 %pad_maximum_fusion.own_ref = bf16[3584,256]{1,0:T(8,128)(2,1)} fusion(bf16[3584,128]{1,0:T(8,128)(2,1)S(1)} %bitcast.32, bf16[3584,128]{1,0:T(8,128)(2,1)} %bitcast.33), kind=kLoop, calls=%fused_computation | loop fusion | flops 3670016 | bytes 3670016 | tf_op jit(solution)/shard_map/concatenate | solution.py:239
  37.7 3.8 %collective-permute-start.3 = (bf16[3584,256]{1,0:T(8,128)(2,1)}, bf16[3584,256]{1,0:T(8,128)(2,1)}, u32[]{:S(2)}, u32[]{:S(2)}) collective-permute-start(bf16[3584,256]{1,0:T(8,128)(2,1)} %pad_maximum_fusion.own_ref), channel_id=1, source_target_pairs={{0,64},{64,0},{1,65},{65,1},{2,66},{66,2},{3,67},{67,3},{4,68},{68... | collective-permute-start | bytes 5505032 | tf_op jit(solution)/shard_map/ppermute | solution.py:206
  41.6 1.4 constant_dynamic-slice_fusion
  43.0 1.9 %collective-permute-start.9 = (bf16[128,896]{1,0:T(8,128)(2,1)S(1)}, bf16[128,896]{1,0:T(8,128)(2,1)S(1)}, u32[]{:S(2)}, u32[]{:S(2)}) collective-permute-start(bf16[128,896]{1,0:T(8,128)(2,1)S(1)} %get-tuple-element.14), channel_id=1, source_target_pairs={{0,384},{128,0},{256,128},{384,256},{1,385},{129,1},{257,129},{385... | collective-permute-start | bytes 688136 | tf_op jit(solution)/shard_map/ppermute | solution.py:206
  44.9 5.4 %collective-permute-start.8 = (bf16[128,896]{1,0:T(8,128)(2,1)S(1)}, bf16[128,896]{1,0:T(8,128)(2,1)S(1)}, u32[]{:S(2)}, u32[]{:S(2)}) collective-permute-start(bf16[128,896]{1,0:T(8,128)(2,1)S(1)} %get-tuple-element.15), channel_id=1, source_target_pairs={{0,256},{128,384},{256,0},{384,128},{1,257},{129,385},{257,1},{385... | collective-permute-start | bytes 688136 | tf_op jit(solution)/shard_map/ppermute | solution.py:206
  50.3 1.9 %collective-permute-start.7 = (bf16[128,896]{1,0:T(8,128)(2,1)S(1)}, bf16[128,896]{1,0:T(8,128)(2,1)S(1)}, u32[]{:S(2)}, u32[]{:S(2)}) collective-permute-start(bf16[128,896]{1,0:T(8,128)(2,1)S(1)} %get-tuple-element.13), channel_id=1, source_target_pairs={{0,128},{128,256},{256,384},{384,0},{1,129},{129,257},{257,385},{3... | collective-permute-start | bytes 688136 | tf_op jit(solution)/shard_map/ppermute | solution.py:206
  52.3 0.8 collective-permute-done.9
  53.0 16.4 %collective-permute-done.8 = bf16[128,896]{1,0:T(8,128)(2,1)S(1)} collective-permute-done((bf16[128,896]{1,0:T(8,128)(2,1)S(1)}, bf16[128,896]{1,0:T(8,128)(2,1)S(1)}, u32[]{:S(2)}, u32[]{:S(2)}) %collective-permute-start.8) | collective-permute-done | bytes 229408 | tf_op jit(solution)/shard_map/ppermute | solution.py:206
  69.4 7.5 %collective-permute-done.7 = bf16[128,896]{1,0:T(8,128)(2,1)S(1)} collective-permute-done((bf16[128,896]{1,0:T(8,128)(2,1)S(1)}, bf16[128,896]{1,0:T(8,128)(2,1)S(1)}, u32[]{:S(2)}, u32[]{:S(2)}) %collective-permute-start.7) | collective-permute-done | bytes 229408 | tf_op jit(solution)/shard_map/ppermute | solution.py:206
  76.9 0.1 pad_maximum_fusion.1.own_ref
  77.1 3.7 %collective-permute-start.10 = (bf16[4,128,896]{2,1,0:T(8,128)(2,1)S(1)}, bf16[4,128,896]{2,1,0:T(8,128)(2,1)}, u32[]{:S(2)}, u32[]{:S(2)}) collective-permute-start(bf16[4,128,896]{2,1,0:T(8,128)(2,1)S(1)} %pad_maximum_fusion.1.own_ref), channel_id=1, source_target_pairs={{0,64},{64,0},{1,65},{65,1},{2,66},{66,2},{3,67},{67,3},{4,68},{68... | collective-permute-start | bytes 2752520 | tf_op jit(solution)/shard_map/ppermute | solution.py:206
  80.7 0.0 collective-permute-done.3.peer_ref
  80.8 4.4 %hidden_units.1.h0 = bf16[256,256]{1,0:T(8,128)(2,1)S(1)} custom-call(bf16[512,1792]{1,0:T(8,128)(2,1)S(1)} %bitcast.29, bf16[3584,256]{1,0:T(8,128)(2,1)} %pad_maximum_fusion.own_ref, bf16[3584,256]{1,0:T(8,128)(2,1)} %collective-permute-done.3.peer_ref), custom_call_target="tpu_custom_call" | custom-call | tf_op jit(solution)/shard_map/hidden_units/pallas_call | solution.py:139
  85.1 0.0 copy-start.3
  85.2 3.7 %collective-permute-start.4 = (bf16[256,256]{1,0:T(8,128)(2,1)S(1)}, bf16[256,256]{1,0:T(8,128)(2,1)S(1)}, u32[]{:S(2)}, u32[]{:S(2)}) collective-permute-start(bf16[256,256]{1,0:T(8,128)(2,1)S(1)} %hidden_units.1.h0), channel_id=1, source_target_pairs={{0,128},{128,256},{256,384},{384,0},{1,129},{129,257},{257,385},{3... | collective-permute-start | bytes 393224 | tf_op jit(solution)/shard_map/ppermute | solution.py:206
  88.9 3.8 %collective-permute-start.5 = (bf16[256,256]{1,0:T(8,128)(2,1)S(1)}, bf16[256,256]{1,0:T(8,128)(2,1)S(1)}, u32[]{:S(2)}, u32[]{:S(2)}) collective-permute-start(bf16[256,256]{1,0:T(8,128)(2,1)S(1)} %hidden_units.1.h0), channel_id=1, source_target_pairs={{0,256},{128,384},{256,0},{384,128},{1,257},{129,385},{257,1},{385... | collective-permute-start | bytes 393224 | tf_op jit(solution)/shard_map/ppermute | solution.py:206
  92.7 5.5 %collective-permute-start.6 = (bf16[256,256]{1,0:T(8,128)(2,1)S(1)}, bf16[256,256]{1,0:T(8,128)(2,1)S(1)}, u32[]{:S(2)}, u32[]{:S(2)}) collective-permute-start(bf16[256,256]{1,0:T(8,128)(2,1)S(1)} %hidden_units.1.h0), channel_id=1, source_target_pairs={{0,384},{128,0},{256,128},{384,256},{1,385},{129,1},{257,129},{385... | collective-permute-start | bytes 393224 | tf_op jit(solution)/shard_map/ppermute | solution.py:206
  98.2 1.1 collective-permute-done.5.h2
  99.4 9.1 %collective-permute-done.6.h3 = bf16[256,256]{1,0:T(8,128)(2,1)S(1)} collective-permute-done((bf16[256,256]{1,0:T(8,128)(2,1)S(1)}, bf16[256,256]{1,0:T(8,128)(2,1)S(1)}, u32[]{:S(2)}, u32[]{:S(2)}) %collective-permute-start.6) | collective-permute-done | bytes 131104 | tf_op jit(solution)/shard_map/ppermute | solution.py:206
  108.5 3.0 %down.1 = bf16[512,512]{1,0:T(8,128)(2,1)} custom-call(bf16[256,256]{1,0:T(8,128)(2,1)S(1)} %hidden_units.1.h0, bf16[256,256]{1,0:T(8,128)(2,1)S(1)} %collective-permute-done.4.h1, bf16[256,256]{1,0:T(8,128)(2,1)S(1)} %collective-permute-done.5.h2, bf16[256,256]{1,0:T(8,128)(2,1)S(1)} %collective-permute-done.6.h3, ...), custom_call_target="tpu_custom_call" | custom-call | tf_op jit(solution)/shard_map/down/pallas_call | solution.py:169
  111.5 9.7 %all-to-all-start.2 = ((bf16[64,8,512]{2,1,0:T(8,128)(2,1)}), bf16[64,8,512]{2,1,0:T(8,128)(2,1)S(1)}, u32[]{:S(2)}, u32[]{:S(2)}) async-start(bf16[64,8,512]{2,1,0:T(8,128)(2,1)} %bitcast.17), calls=%async_computation.2 | async-start | bytes 1048576 | tf_op jit(solution)/shard_map/all_to_all | solution.py:201
  121.3 0.0 copy-start.4
  121.3 0.0 copy-start.5
  121.3 0.0 copy-start.1
  121.3 0.3 copy.13.query_ref
  121.6 1.7 %copy.14.cache_ref = bf16[1,2,512,576]{3,2,1,0:T(8,128)(2,1)S(1)} copy(bf16[1,2,512,576]{2,3,1,0:T(8,128)(2,1)} %param.11) | data formatting | bytes 2359296 | tf_op args[0]
  123.4 0.2 constant_dynamic-slice_fusion.2
  123.5 2.5 %attend.1 = (bf16[2,128,512]{2,1,0:T(8,128)(2,1)S(1)}, bf16[2,128,512]{2,1,0:T(8,128)(2,1)S(1)}) custom-call(s32[2]{0:T(128)S(1)} %get-tuple-element.19.len_ref, bf16[2,1,2,128,576]{4,3,2,1,0:T(8,128)(2,1)S(1)} %copy.13.query_ref, bf16[1,2,512,576]{3,2,1,0:T(8,128)(2,1)S(1)} %copy.14.cache_ref, bf16[2,1,2,576]{3,2,1,0:T(2,128)(2,1)S(1)} %copy-done.1), custom_call_target="tpu_custom_call" | custom-call | tf_op jit(solution)/shard_map/attend/pallas_call | solution.py:63
  126.0 3.0 %collective-permute-start = (bf16[2,128,512]{2,1,0:T(8,128)(2,1)S(1)}, bf16[2,128,512]{2,1,0:T(8,128)(2,1)S(1)}, u32[]{:S(2)}, u32[]{:S(2)}) collective-permute-start(bf16[2,128,512]{2,1,0:T(8,128)(2,1)S(1)} %get-tuple-element.6), channel_id=1, source_target_pairs={{0,32},{1,33},{2,34},{3,35},{4,36},{5,37},{6,38},{7,39},{8,40},{9,... | collective-permute-start | bytes 786440 | tf_op jit(solution)/shard_map/ppermute | solution.py:206
  129.0 6.4 %collective-permute-start.1 = (bf16[2,128,512]{2,1,0:T(8,128)(2,1)S(1)}, bf16[2,128,512]{2,1,0:T(8,128)(2,1)S(1)}, u32[]{:S(2)}, u32[]{:S(2)}) collective-permute-start(bf16[2,128,512]{2,1,0:T(8,128)(2,1)S(1)} %get-tuple-element.7), channel_id=1, source_target_pairs={{0,63},{1,0},{2,1},{3,2},{4,3},{5,4},{6,5},{7,6},{8,7},{9,8},{10,9... | collective-permute-start | bytes 786440 | tf_op jit(solution)/shard_map/ppermute | solution.py:206
  135.5 1.9 %collective-permute-start.2 = (bf16[2,128,512]{2,1,0:T(8,128)(2,1)S(1)}, bf16[2,128,512]{2,1,0:T(8,128)(2,1)S(1)}, u32[]{:S(2)}, u32[]{:S(2)}) collective-permute-start(bf16[2,128,512]{2,1,0:T(8,128)(2,1)S(1)} %get-tuple-element.7), channel_id=1, source_target_pairs={{0,1},{1,2},{2,3},{3,4},{4,5},{5,6},{6,7},{7,8},{8,9},{9,10},{10,1... | collective-permute-start | bytes 786440 | tf_op jit(solution)/shard_map/ppermute | solution.py:206
  137.4 0.6 fusion.1
  140.1 7.6 %collective-permute-done.2 = bf16[2,128,512]{2,1,0:T(8,128)(2,1)S(1)} collective-permute-done((bf16[2,128,512]{2,1,0:T(8,128)(2,1)S(1)}, bf16[2,128,512]{2,1,0:T(8,128)(2,1)S(1)}, u32[]{:S(2)}, u32[]{:S(2)}) %collective-permute-start.2) | collective-permute-done | bytes 262176 | tf_op jit(solution)/shard_map/ppermute | solution.py:206
  147.7 0.2 combine.1
  147.9 0.7 reshape.47
  148.6 8.5 %all-to-all-start.3 = ((bf16[8,2,896]{2,1,0:T(2,128)(2,1)}), bf16[8,2,896]{2,1,0:T(2,128)(2,1)S(1)}, u32[]{:S(2)}, u32[]{:S(2)}) async-start(bf16[8,2,896]{2,1,0:T(2,128)(2,1)} %reshape.47), calls=%async_computation.3 | async-start | bytes 57344 | tf_op jit(solution)/shard_map/all_to_all | solution.py:201
  157.1 0.1 maximum_bitcast_fusion
  157.1 0.8 copy.16
  157.9 6.3 %all-to-all-done.3 = bf16[8,2,896]{2,1,0:T(2,128)(2,1)S(1)} async-done(((bf16[8,2,896]{2,1,0:T(2,128)(2,1)}), bf16[8,2,896]{2,1,0:T(2,128)(2,1)S(1)}, u32[]{:S(2)}, u32[]{:S(2)}) %all-to-all-start.3) | async-done | bytes 28704 | tf_op jit(solution)/shard_map/all_to_all | solution.py:201
  164.3 0.6 reshape.49
  (16 shorter events, 0.1 us)
Async XLA Ops:
  20.9 1.3 copy-start
  22.1 13.0 %copy-start.2 = (bf16[1,3584,128]{2,1,0:T(8,128)(2,1)S(1)}, bf16[1,3584,128]{2,1,0:T(8,128)(2,1)}, u32[]{:S(2)}) copy-start(bf16[1,3584,128]{2,1,0:T(8,128)(2,1)} %param.20) | copy-start | bytes 2752516
  22.1 58.6 %all-to-all-start.1 = ((bf16[64,8,1792]{2,1,0:T(8,128)(2,1)}), bf16[64,8,1792]{2,1,0:T(8,128)(2,1)S(1)}, u32[]{:S(2)}, u32[]{:S(2)}) async-start(bf16[64,8,1792]{2,1,0:T(8,128)(2,1)} %bitcast.31), calls=%async_computation.1 | async-start | bytes 3670016 | tf_op jit(solution)/shard_map/all_to_all | solution.py:201
  37.7 43.0 %collective-permute-start.3 = (bf16[3584,256]{1,0:T(8,128)(2,1)}, bf16[3584,256]{1,0:T(8,128)(2,1)}, u32[]{:S(2)}, u32[]{:S(2)}) collective-permute-start(bf16[3584,256]{1,0:T(8,128)(2,1)} %pad_maximum_fusion.own_ref), channel_id=1, source_target_pairs={{0,64},{64,0},{1,65},{65,1},{2,66},{66,2},{3,67},{67,3},{4,68},{68... | collective-permute-start | bytes 5505032 | tf_op jit(solution)/shard_map/ppermute | solution.py:206
  43.0 10.1 %collective-permute-start.9 = (bf16[128,896]{1,0:T(8,128)(2,1)S(1)}, bf16[128,896]{1,0:T(8,128)(2,1)S(1)}, u32[]{:S(2)}, u32[]{:S(2)}) collective-permute-start(bf16[128,896]{1,0:T(8,128)(2,1)S(1)} %get-tuple-element.14), channel_id=1, source_target_pairs={{0,384},{128,0},{256,128},{384,256},{1,385},{129,1},{257,129},{385... | collective-permute-start | bytes 688136 | tf_op jit(solution)/shard_map/ppermute | solution.py:206
  44.9 24.6 %collective-permute-start.8 = (bf16[128,896]{1,0:T(8,128)(2,1)S(1)}, bf16[128,896]{1,0:T(8,128)(2,1)S(1)}, u32[]{:S(2)}, u32[]{:S(2)}) collective-permute-start(bf16[128,896]{1,0:T(8,128)(2,1)S(1)} %get-tuple-element.15), channel_id=1, source_target_pairs={{0,256},{128,384},{256,0},{384,128},{1,257},{129,385},{257,1},{385... | collective-permute-start | bytes 688136 | tf_op jit(solution)/shard_map/ppermute | solution.py:206
  50.3 26.6 %collective-permute-start.7 = (bf16[128,896]{1,0:T(8,128)(2,1)S(1)}, bf16[128,896]{1,0:T(8,128)(2,1)S(1)}, u32[]{:S(2)}, u32[]{:S(2)}) collective-permute-start(bf16[128,896]{1,0:T(8,128)(2,1)S(1)} %get-tuple-element.13), channel_id=1, source_target_pairs={{0,128},{128,256},{256,384},{384,0},{1,129},{129,257},{257,385},{3... | collective-permute-start | bytes 688136 | tf_op jit(solution)/shard_map/ppermute | solution.py:206
  77.1 21.2 %collective-permute-start.10 = (bf16[4,128,896]{2,1,0:T(8,128)(2,1)S(1)}, bf16[4,128,896]{2,1,0:T(8,128)(2,1)}, u32[]{:S(2)}, u32[]{:S(2)}) collective-permute-start(bf16[4,128,896]{2,1,0:T(8,128)(2,1)S(1)} %pad_maximum_fusion.1.own_ref), channel_id=1, source_target_pairs={{0,64},{64,0},{1,65},{65,1},{2,66},{66,2},{3,67},{67,3},{4,68},{68... | collective-permute-start | bytes 2752520 | tf_op jit(solution)/shard_map/ppermute | solution.py:206
  85.1 36.1 %copy-start.3 = (bf16[2,1,2,128,576]{3,4,2,1,0:T(8,128)(2,1)S(1)}, bf16[2,1,2,128,576]{3,4,2,1,0:T(8,128)(2,1)}, u32[]{:S(2)}) copy-start(bf16[2,1,2,128,576]{3,4,2,1,0:T(8,128)(2,1)} %param.14) | copy-start | bytes 1769476
  85.2 13.1 %collective-permute-start.4 = (bf16[256,256]{1,0:T(8,128)(2,1)S(1)}, bf16[256,256]{1,0:T(8,128)(2,1)S(1)}, u32[]{:S(2)}, u32[]{:S(2)}) collective-permute-start(bf16[256,256]{1,0:T(8,128)(2,1)S(1)} %hidden_units.1.h0), channel_id=1, source_target_pairs={{0,128},{128,256},{256,384},{384,0},{1,129},{129,257},{257,385},{3... | collective-permute-start | bytes 393224 | tf_op jit(solution)/shard_map/ppermute | solution.py:206
  88.9 10.5 %collective-permute-start.5 = (bf16[256,256]{1,0:T(8,128)(2,1)S(1)}, bf16[256,256]{1,0:T(8,128)(2,1)S(1)}, u32[]{:S(2)}, u32[]{:S(2)}) collective-permute-start(bf16[256,256]{1,0:T(8,128)(2,1)S(1)} %hidden_units.1.h0), channel_id=1, source_target_pairs={{0,256},{128,384},{256,0},{384,128},{1,257},{129,385},{257,1},{385... | collective-permute-start | bytes 393224 | tf_op jit(solution)/shard_map/ppermute | solution.py:206
  92.7 15.8 %collective-permute-start.6 = (bf16[256,256]{1,0:T(8,128)(2,1)S(1)}, bf16[256,256]{1,0:T(8,128)(2,1)S(1)}, u32[]{:S(2)}, u32[]{:S(2)}) collective-permute-start(bf16[256,256]{1,0:T(8,128)(2,1)S(1)} %hidden_units.1.h0), channel_id=1, source_target_pairs={{0,384},{128,0},{256,128},{384,256},{1,385},{129,1},{257,129},{385... | collective-permute-start | bytes 393224 | tf_op jit(solution)/shard_map/ppermute | solution.py:206
  111.5 36.2 %all-to-all-start.2 = ((bf16[64,8,512]{2,1,0:T(8,128)(2,1)}), bf16[64,8,512]{2,1,0:T(8,128)(2,1)S(1)}, u32[]{:S(2)}, u32[]{:S(2)}) async-start(bf16[64,8,512]{2,1,0:T(8,128)(2,1)} %bitcast.17), calls=%async_computation.2 | async-start | bytes 1048576 | tf_op jit(solution)/shard_map/all_to_all | solution.py:201
  121.3 2.0 %copy-start.4 = (s32[64,2]{0,1:T(2,128)S(1)}, s32[64,2]{0,1:T(2,128)}, u32[]{:S(2)}) copy-start(s32[64,2]{0,1:T(2,128)} %param.13) | copy-start | bytes 1540
  121.3 2.0 %copy-start.5 = (s32[64,2]{0,1:T(2,128)S(1)}, s32[64,2]{0,1:T(2,128)}, u32[]{:S(2)}) copy-start(s32[64,2]{0,1:T(2,128)} %param.12) | copy-start | bytes 1540
  121.3 2.2 %copy-start.1 = (bf16[2,1,2,576]{3,2,1,0:T(2,128)(2,1)S(1)}, bf16[2,1,2,576]{3,2,1,0:T(2,128)(2,1)}, u32[]{:S(2)}) copy-start(bf16[2,1,2,576]{3,2,1,0:T(2,128)(2,1)} %fresh_ref.1) | copy-start | bytes 13828
  126.0 14.0 %collective-permute-start = (bf16[2,128,512]{2,1,0:T(8,128)(2,1)S(1)}, bf16[2,128,512]{2,1,0:T(8,128)(2,1)S(1)}, u32[]{:S(2)}, u32[]{:S(2)}) collective-permute-start(bf16[2,128,512]{2,1,0:T(8,128)(2,1)S(1)} %get-tuple-element.6), channel_id=1, source_target_pairs={{0,32},{1,33},{2,34},{3,35},{4,36},{5,37},{6,38},{7,39},{8,40},{9,... | collective-permute-start | bytes 786440 | tf_op jit(solution)/shard_map/ppermute | solution.py:206
  129.0 11.0 %collective-permute-start.1 = (bf16[2,128,512]{2,1,0:T(8,128)(2,1)S(1)}, bf16[2,128,512]{2,1,0:T(8,128)(2,1)S(1)}, u32[]{:S(2)}, u32[]{:S(2)}) collective-permute-start(bf16[2,128,512]{2,1,0:T(8,128)(2,1)S(1)} %get-tuple-element.7), channel_id=1, source_target_pairs={{0,63},{1,0},{2,1},{3,2},{4,3},{5,4},{6,5},{7,6},{8,7},{9,8},{10,9... | collective-permute-start | bytes 786440 | tf_op jit(solution)/shard_map/ppermute | solution.py:206
  135.5 12.2 %collective-permute-start.2 = (bf16[2,128,512]{2,1,0:T(8,128)(2,1)S(1)}, bf16[2,128,512]{2,1,0:T(8,128)(2,1)S(1)}, u32[]{:S(2)}, u32[]{:S(2)}) collective-permute-start(bf16[2,128,512]{2,1,0:T(8,128)(2,1)S(1)} %get-tuple-element.7), channel_id=1, source_target_pairs={{0,1},{1,2},{2,3},{3,4},{4,5},{5,6},{6,7},{7,8},{8,9},{9,10},{10,1... | collective-permute-start | bytes 786440 | tf_op jit(solution)/shard_map/ppermute | solution.py:206
  148.6 15.7 %all-to-all-start.3 = ((bf16[8,2,896]{2,1,0:T(2,128)(2,1)}), bf16[8,2,896]{2,1,0:T(2,128)(2,1)S(1)}, u32[]{:S(2)}, u32[]{:S(2)}) async-start(bf16[8,2,896]{2,1,0:T(2,128)(2,1)} %reshape.47), calls=%async_computation.3 | async-start | bytes 57344 | tf_op jit(solution)/shard_map/all_to_all | solution.py:201

commit v2 on v1

--- a/solution.py
+++ b/solution.py
@@ -146,12 +146,13 @@
     )(rows, own, peer)
 
 
-def down_kernel(h0, h1, h2, h3, own_ref, peer_ref, out_ref):
+def down_kernel(h0, h1, h2_top, h2_bottom, h3, own_ref, peer_ref, out_ref):
     slots, part = out_ref.shape
     total = None
-    for number, ref in enumerate((h0, h1, h2, h3)):
+    hs = (h0[...], h1[...], jnp.concatenate([h2_top[...], h2_bottom[...]], 0), h3[...])
+    for number, h in enumerate(hs):
         weights = jnp.concatenate([own_ref[number], peer_ref[number]], 0)
-        term = dot(ref[...], weights)
+        term = dot(h, weights)
         total = term if total is None else total + term
     value = total.astype(BF)
     rest = value.shape[1] - part
@@ -169,7 +170,7 @@
     return pl.pallas_call(
         down_kernel,
         out_shape=jax.ShapeDtypeStruct((2 * rows, part), BF),
-        in_specs=vmem(6),
+        in_specs=vmem(7),
         out_specs=vmem(1)[0],
         compiler_params=PARAMS,
         name="down",
@@ -232,8 +233,11 @@
     packed = jnp.concatenate([hidden, routes.astype(BF), route_logits], -1)[:, 0]
     packed = jnp.broadcast_to(packed[None], (yh_size, *packed.shape))
     tokens = exchange(packed.reshape(-1, *packed.shape[2:]), DP)
+    served = attend(lengths[own_rank], queries, latent_cache, new_latent)
+    tokens, served0, served1 = lax.optimization_barrier((tokens, *served))
     tokens = tokens.reshape(-1, tokens.shape[-1])
     send, mix = dispatch(tokens, slots, half)
+    send, served0, served1 = lax.optimization_barrier((send, served0, served1))
     arrived = exchange(send.reshape(experts, 2 * CAP, half), EP).reshape(slots, half)
 
     own_w = jnp.concatenate([w_gate[0], w_up[0]], 1)
@@ -245,7 +249,6 @@
     own_down = jnp.stack([shifted(x, "yh", s) if s else x for s, x in enumerate(down_blocks)])
     peer_down = shifted(own_down, "c", 1)
 
-    served0, served1 = attend(lengths[own_rank], queries, latent_cache, new_latent)
     far = shifted(served0, EP, experts // 2)
     lower = shifted(served1, EP, 1)
     upper = shifted(served1, EP, -1)
@@ -258,9 +261,14 @@
     )
     attended = jnp.stack([result0, result1], 1)[:, None]
 
+    arrived, peer_w, own_down, peer_down, attended = lax.optimization_barrier(
+        (arrived, peer_w, own_down, peer_down, attended)
+    )
     h = hidden_units(arrived, own_w, peer_w)
-    hs = [h, *(shifted(h, "yh", s) for s in range(1, yh_size))]
-    out = down(hs, own_down, peer_down, part)
+    before, after = shifted(h, "yh", 1), shifted(h, "yh", -1)
+    middle = h.shape[0] // 2
+    across = (shifted(before[:middle], "yh", 1), shifted(after[middle:], "yh", -1))
+    out = down((h, before, *across, after), own_down, peer_down, part)
     back = exchange(out.reshape(experts, 2 * CAP, part), EP).reshape(slots, part)
     mixed = combine(mix, back, chunk)
     final = exchange(mixed.reshape(-1, requests, chunk), DP)

time: 166 us -> 175 us (1.054)
  blocking collectives: 17.1 us -> 24.7 us
  local copies, waits for them, and re-layouts: 8.54 us -> 10.9 us
  waiting for transfers between devices: 48.8 us -> 46.9 us
  other arithmetic: 3.55 us -> 5.38 us
    all_to_all x1, blocking collectives: 17.1 us -> 24.7 us  [exchange(): return lax.all_to_all(x, axes, split_axis=0, concat_axis=0, tiled=True)]
    ppermute x11 -> x12, waiting for transfers between devices: 42.5 us -> 37.8 us  [shifted(): return lax.ppermute(x, axes, [(i, (i + by) % size) for i in range(size)])]
    ppermute x11 -> x12, starting transfers between devices: 41.1 us -> 44.3 us  [shifted(): return lax.ppermute(x, axes, [(i, (i + by) % size) for i in range(size)])]
    all_to_all x3, starting transfers between devices: 31.2 us -> 28.3 us  [exchange(): return lax.all_to_all(x, axes, split_axis=0, concat_axis=0, tiled=True)]
    all_to_all x3, waiting for transfers between devices: 6.31 us -> 9.15 us  [exchange(): return lax.all_to_all(x, axes, split_axis=0, concat_axis=0, tiled=True)]
    unnamed x15 -> x21, local copies, waits for them, and re-layouts: 4.1 us -> 4.91 us
  transfers between devices with their start and end apart: 14 -> 15, of which waited for: 7 -> 7; matrix products, arithmetic and copies ran while one was open for 5% -> 6% of each run, Pallas kernels for 4% -> 1%
where the time goes in v2:
time: 175 us; the launch traced here: 174 us
  starting transfers between devices  72.6 us (41%)
  waiting for transfers between devices  46.9 us (27%)
  blocking collectives  24.7 us (14%)
  local copies, waits for them, and re-layouts  10.9 us (6%)
  Pallas kernels  10.7 us (6%)
  other arithmetic  5.38 us (3%)
  between operations  2.95 us (2%)
    ppermute x12, starting transfers between devices, shifted(): return lax.ppermute(x, axes, [(i, (i + by) % size) for i in range(size)])  44.3 us
    ppermute x12, waiting for transfers between devices, shifted(): return lax.ppermute(x, axes, [(i, (i + by) % size) for i in range(size)])  37.8 us
    all_to_all x3, starting transfers between devices, exchange(): return lax.all_to_all(x, axes, split_axis=0, concat_axis=0, tiled=True)  28.3 us
    all_to_all x1, blocking collectives, exchange(): return lax.all_to_all(x, axes, split_axis=0, concat_axis=0, tiled=True)  24.7 us
    all_to_all x3, waiting for transfers between devices, exchange(): return lax.all_to_all(x, axes, split_axis=0, concat_axis=0, tiled=True)  9.15 us
    unnamed x21, local copies, waits for them, and re-layouts  4.91 us
    pallas_call x1, Pallas kernels, hidden_units(): pl.pallas_call(hidden_kernel, out_shape=jax.ShapeDtypeStruct((rows.shape[...  4.39 us
  transfers between devices with their start and end apart: 15, of which 7 were waited for; matrix products, arithmetic and copies ran while one was open for 6% of the time, Pallas kernels for 1%

profile of v2, /device:TPU:1, one launch (start us, length us, event | category | flops | bytes accessed | tf_op | source)
XLA Modules:
  0.0 174.1 jit_solution(18203893611841881478)
XLA Ops:
  0.6 0.8 convert_element_type.3
  1.4 0.8 concatenate.6
  2.3 0.7 broadcast_in_dim.11
  3.0 10.7 %all-to-all-start = ((bf16[8,2,3600]{2,1,0:T(2,128)(2,1)}), bf16[8,2,3600]{2,1,0:T(2,128)(2,1)}, u32[]{:S(2)}, u32[]{:S(2)}) async-start(bf16[8,2,3600]{2,1,0:T(2,128)(2,1)} %bitcast.1), calls=%async_computation | async-start | bytes 237568 | tf_op jit(solution)/shard_map/all_to_all | solution.py:202
  13.7 1.4 copy.13.query_ref
  15.1 0.7 copy.14.cache_ref
  15.9 0.2 constant_dynamic-slice_fusion
  16.1 2.4 %attend.1 = (bf16[2,128,512]{2,1,0:T(8,128)(2,1)S(1)}, bf16[2,128,512]{2,1,0:T(8,128)(2,1)S(1)}) custom-call(s32[2]{0:T(128)S(1)} %get-tuple-element.41.len_ref, bf16[2,1,2,128,576]{4,3,2,1,0:T(8,128)(2,1)S(1)} %copy.13.query_ref, bf16[1,2,512,576]{3,2,1,0:T(8,128)(2,1)S(1)} %copy.14.cache_ref, bf16[2,1,2,576]{3,2,1,0:T(2,128)(2,1)S(1)} %copy-done.3), custom_call_target="tpu_custom_call" | custom-call | tf_op jit(solution)/shard_map/attend/pallas_call | solution.py:63
  18.5 0.0 copy-start.1
  18.5 0.7 copy-done.1
  19.2 2.8 %all-to-all-done = bf16[8,2,3600]{2,1,0:T(2,128)(2,1)} async-done(((bf16[8,2,3600]{2,1,0:T(2,128)(2,1)}), bf16[8,2,3600]{2,1,0:T(2,128)(2,1)}, u32[]{:S(2)}, u32[]{:S(2)}) %all-to-all-start) | async-done | bytes 115232 | tf_op jit(solution)/shard_map/all_to_all | solution.py:202
  22.0 1.0 reshape.42.tokens_ref
  23.0 1.4 dispatch.1
  24.4 1.2 copy-done
  25.7 11.4 %all-to-all-start.1 = ((bf16[64,8,1792]{2,1,0:T(8,128)(2,1)}), bf16[64,8,1792]{2,1,0:T(8,128)(2,1)S(1)}, u32[]{:S(2)}, u32[]{:S(2)}) async-start(bf16[64,8,1792]{2,1,0:T(8,128)(2,1)} %bitcast.32), calls=%async_computation.1 | async-start | bytes 3670016 | tf_op jit(solution)/shard_map/all_to_all | solution.py:202
  37.0 2.6 %pad_maximum_fusion.own_ref = bf16[3584,256]{1,0:T(8,128)(2,1)} fusion(bf16[3584,128]{1,0:T(8,128)(2,1)S(1)} %bitcast.33, bf16[3584,128]{1,0:T(8,128)(2,1)} %bitcast.34), kind=kLoop, calls=%fused_computation | loop fusion | flops 3670016 | bytes 3670016 | tf_op jit(solution)/shard_map/concatenate | solution.py:243
  39.6 3.8 %collective-permute-start = (bf16[3584,256]{1,0:T(8,128)(2,1)}, bf16[3584,256]{1,0:T(8,128)(2,1)}, u32[]{:S(2)}, u32[]{:S(2)}) collective-permute-start(bf16[3584,256]{1,0:T(8,128)(2,1)} %pad_maximum_fusion.own_ref), channel_id=1, source_target_pairs={{0,64},{64,0},{1,65},{65,1},{2,66},{66,2},{3,67},{67,3},{4,68},{68... | collective-permute-start | bytes 5505032 | tf_op jit(solution)/shard_map/ppermute | solution.py:207
  43.5 1.4 constant_dynamic-slice_fusion.1
  44.9 2.2 %collective-permute-start.1 = (bf16[128,896]{1,0:T(8,128)(2,1)S(1)}, bf16[128,896]{1,0:T(8,128)(2,1)S(1)}, u32[]{:S(2)}, u32[]{:S(2)}) collective-permute-start(bf16[128,896]{1,0:T(8,128)(2,1)S(1)} %get-tuple-element.35), channel_id=1, source_target_pairs={{0,128},{128,256},{256,384},{384,0},{1,129},{129,257},{257,385},{3... | collective-permute-start | bytes 688136 | tf_op jit(solution)/shard_map/ppermute | solution.py:207
  47.1 5.2 %collective-permute-start.3 = (bf16[128,896]{1,0:T(8,128)(2,1)S(1)}, bf16[128,896]{1,0:T(8,128)(2,1)S(1)}, u32[]{:S(2)}, u32[]{:S(2)}) collective-permute-start(bf16[128,896]{1,0:T(8,128)(2,1)S(1)} %get-tuple-element.36), channel_id=1, source_target_pairs={{0,384},{128,0},{256,128},{384,256},{1,385},{129,1},{257,129},{385... | collective-permute-start | bytes 688136 | tf_op jit(solution)/shard_map/ppermute | solution.py:207
  52.3 3.4 %collective-permute-start.2 = (bf16[128,896]{1,0:T(8,128)(2,1)S(1)}, bf16[128,896]{1,0:T(8,128)(2,1)S(1)}, u32[]{:S(2)}, u32[]{:S(2)}) collective-permute-start(bf16[128,896]{1,0:T(8,128)(2,1)S(1)} %get-tuple-element.37), channel_id=1, source_target_pairs={{0,256},{128,384},{256,0},{384,128},{1,257},{129,385},{257,1},{385... | collective-permute-start | bytes 688136 | tf_op jit(solution)/shard_map/ppermute | solution.py:207
  55.7 14.3 %collective-permute-done.1 = bf16[128,896]{1,0:T(8,128)(2,1)S(1)} collective-permute-done((bf16[128,896]{1,0:T(8,128)(2,1)S(1)}, bf16[128,896]{1,0:T(8,128)(2,1)S(1)}, u32[]{:S(2)}, u32[]{:S(2)}) %collective-permute-start.1) | collective-permute-done | bytes 229408 | tf_op jit(solution)/shard_map/ppermute | solution.py:207
  70.0 11.7 %collective-permute-done.2 = bf16[128,896]{1,0:T(8,128)(2,1)S(1)} collective-permute-done((bf16[128,896]{1,0:T(8,128)(2,1)S(1)}, bf16[128,896]{1,0:T(8,128)(2,1)S(1)}, u32[]{:S(2)}, u32[]{:S(2)}) %collective-permute-start.2) | collective-permute-done | bytes 229408 | tf_op jit(solution)/shard_map/ppermute | solution.py:207
  81.7 0.1 pad_maximum_fusion.1.own_ref
  81.9 3.1 %collective-permute-start.4 = (bf16[4,128,896]{2,1,0:T(8,128)(2,1)S(1)}, bf16[4,128,896]{2,1,0:T(8,128)(2,1)}, u32[]{:S(2)}, u32[]{:S(2)}) collective-permute-start(bf16[4,128,896]{2,1,0:T(8,128)(2,1)S(1)} %pad_maximum_fusion.1.own_ref), channel_id=1, source_target_pairs={{0,64},{64,0},{1,65},{65,1},{2,66},{66,2},{3,67},{67,3},{4,68},{68... | collective-permute-start | bytes 2752520 | tf_op jit(solution)/shard_map/ppermute | solution.py:207
  85.0 3.0 %collective-permute-start.5 = (bf16[2,128,512]{2,1,0:T(8,128)(2,1)S(1)}, bf16[2,128,512]{2,1,0:T(8,128)(2,1)}, u32[]{:S(2)}, u32[]{:S(2)}) collective-permute-start(bf16[2,128,512]{2,1,0:T(8,128)(2,1)S(1)} %copy-done.2), channel_id=1, source_target_pairs={{0,32},{1,33},{2,34},{3,35},{4,36},{5,37},{6,38},{7,39},{8,40},{9,... | collective-permute-start | bytes 786440 | tf_op jit(solution)/shard_map/ppermute | solution.py:207
  88.0 1.9 %collective-permute-start.7 = (bf16[2,128,512]{2,1,0:T(8,128)(2,1)S(1)}, bf16[2,128,512]{2,1,0:T(8,128)(2,1)}, u32[]{:S(2)}, u32[]{:S(2)}) collective-permute-start(bf16[2,128,512]{2,1,0:T(8,128)(2,1)S(1)} %get-tuple-element.25), channel_id=1, source_target_pairs={{0,1},{1,2},{2,3},{3,4},{4,5},{5,6},{6,7},{7,8},{8,9},{9,10},{10,1... | collective-permute-start | bytes 786440 | tf_op jit(solution)/shard_map/ppermute | solution.py:207
  89.9 7.6 %collective-permute-start.6 = (bf16[2,128,512]{2,1,0:T(8,128)(2,1)S(1)}, bf16[2,128,512]{2,1,0:T(8,128)(2,1)}, u32[]{:S(2)}, u32[]{:S(2)}) collective-permute-start(bf16[2,128,512]{2,1,0:T(8,128)(2,1)S(1)} %get-tuple-element.25), channel_id=1, source_target_pairs={{0,63},{1,0},{2,1},{3,2},{4,3},{5,4},{6,5},{7,6},{8,7},{9,8},{10,9... | collective-permute-start | bytes 786440 | tf_op jit(solution)/shard_map/ppermute | solution.py:207
  97.5 0.5 fusion.1
  100.0 2.9 %collective-permute-done.7 = bf16[2,128,512]{2,1,0:T(8,128)(2,1)} collective-permute-done((bf16[2,128,512]{2,1,0:T(8,128)(2,1)S(1)}, bf16[2,128,512]{2,1,0:T(8,128)(2,1)}, u32[]{:S(2)}, u32[]{:S(2)}) %collective-permute-start.7) | collective-permute-done | bytes 262176 | tf_op jit(solution)/shard_map/ppermute | solution.py:207
  103.0 1.0 select_bitcast_fusion
  103.9 0.8 maximum_bitcast_fusion
  104.8 4.4 %hidden_units.1.h0 = bf16[256,256]{1,0:T(8,128)(2,1)S(1)} custom-call(bf16[512,1792]{1,0:T(8,128)(2,1)S(1)} %bitcast.29, bf16[3584,256]{1,0:T(8,128)(2,1)} %pad_maximum_fusion.own_ref, bf16[3584,256]{1,0:T(8,128)(2,1)} %collective-permute-done.peer_ref), custom_call_target="tpu_custom_call" | custom-call | tf_op jit(solution)/shard_map/hidden_units/pallas_call | solution.py:139
  109.2 3.9 %collective-permute-start.10 = (bf16[256,256]{1,0:T(8,128)(2,1)S(1)}, bf16[256,256]{1,0:T(8,128)(2,1)S(1)}, u32[]{:S(2)}, u32[]{:S(2)}) collective-permute-start(bf16[256,256]{1,0:T(8,128)(2,1)S(1)} %hidden_units.1.h0), channel_id=1, source_target_pairs={{0,384},{128,0},{256,128},{384,256},{1,385},{129,1},{257,129},{385... | collective-permute-start | bytes 393224 | tf_op jit(solution)/shard_map/ppermute | solution.py:207
  113.1 2.3 %collective-permute-start.8 = (bf16[256,256]{1,0:T(8,128)(2,1)S(1)}, bf16[256,256]{1,0:T(8,128)(2,1)S(1)}, u32[]{:S(2)}, u32[]{:S(2)}) collective-permute-start(bf16[256,256]{1,0:T(8,128)(2,1)S(1)} %hidden_units.1.h0), channel_id=1, source_target_pairs={{0,128},{128,256},{256,384},{384,0},{1,129},{129,257},{257,385},{3... | collective-permute-start | bytes 393224 | tf_op jit(solution)/shard_map/ppermute | solution.py:207
  115.4 3.8 %collective-permute-done.10.h3 = bf16[256,256]{1,0:T(8,128)(2,1)S(1)} collective-permute-done((bf16[256,256]{1,0:T(8,128)(2,1)S(1)}, bf16[256,256]{1,0:T(8,128)(2,1)S(1)}, u32[]{:S(2)}, u32[]{:S(2)}) %collective-permute-start.10) | collective-permute-done | bytes 131104 | tf_op jit(solution)/shard_map/ppermute | solution.py:207
  119.2 5.1 %collective-permute-start.11 = (bf16[128,256]{1,0:T(8,128)(2,1)S(1)}, bf16[128,256]{1,0:T(8,128)(2,1)S(1)}, u32[]{:S(2)}, u32[]{:S(2)}) collective-permute-start(bf16[128,256]{1,0:T(8,128)(2,1)S(1)} %slice.20), channel_id=1, source_target_pairs={{0,384},{128,0},{256,128},{384,256},{1,385},{129,1},{257,129},{385... | collective-permute-start | bytes 196616 | tf_op jit(solution)/shard_map/ppermute | solution.py:207
  124.3 0.0 copy-start.4
  124.3 2.9 %collective-permute-start.9 = (bf16[128,256]{1,0:T(8,128)(2,1)S(1)}, bf16[128,256]{1,0:T(8,128)(2,1)S(1)}, u32[]{:S(2)}, u32[]{:S(2)}) collective-permute-start(bf16[128,256]{1,0:T(8,128)(2,1)S(1)} %slice.19), channel_id=1, source_target_pairs={{0,128},{128,256},{256,384},{384,0},{1,129},{129,257},{257,385},{3... | collective-permute-start | bytes 196616 | tf_op jit(solution)/shard_map/ppermute | solution.py:207
  127.2 5.1 %collective-permute-done.9.h2_top = bf16[128,256]{1,0:T(8,128)(2,1)S(1)} collective-permute-done((bf16[128,256]{1,0:T(8,128)(2,1)S(1)}, bf16[128,256]{1,0:T(8,128)(2,1)S(1)}, u32[]{:S(2)}, u32[]{:S(2)}) %collective-permute-start.9) | collective-permute-done | bytes 65568 | tf_op jit(solution)/shard_map/ppermute | solution.py:207
  132.3 2.3 %down.1 = bf16[512,512]{1,0:T(8,128)(2,1)S(1)} custom-call(bf16[256,256]{1,0:T(8,128)(2,1)S(1)} %hidden_units.1.h0, bf16[256,256]{1,0:T(8,128)(2,1)S(1)} %collective-permute-done.8.h1, bf16[128,256]{1,0:T(8,128)(2,1)S(1)} %collective-permute-done.9.h2_top, bf16[128,256]{1,0:T(8,128)(2,1)S(1)} %collective-permute-done.11.h2_bottom, ...), custom_call_target="tpu_custom_call" | custom-call | tf_op jit(solution)/shard_map/down/pallas_call | solution.py:170
  134.5 24.7 %all_to_all.20 = bf16[64,8,512]{2,1,0:T(8,128)(2,1)S(1)} all-to-all(bf16[64,8,512]{2,1,0:T(8,128)(2,1)S(1)} %bitcast.31), channel_id=1, replica_groups=mesh['yh'=4,'c'=2,'yl'=2,'x'=4,'z'=8] {'yl','x','z'}, dimensions={0} | all-to-all | bytes 1048576 | tf_op jit(solution)/shard_map/all_to_all | solution.py:202
  159.2 0.2 combine.1
  159.4 0.7 reshape.47
  160.1 6.2 %all-to-all-start.3 = ((bf16[8,2,896]{2,1,0:T(2,128)(2,1)}), bf16[8,2,896]{2,1,0:T(2,128)(2,1)S(1)}, u32[]{:S(2)}, u32[]{:S(2)}) async-start(bf16[8,2,896]{2,1,0:T(2,128)(2,1)} %reshape.47), calls=%async_computation.3 | async-start | bytes 57344 | tf_op jit(solution)/shard_map/all_to_all | solution.py:202
  166.3 0.8 copy.16
  167.1 6.4 %all-to-all-done.3 = bf16[8,2,896]{2,1,0:T(2,128)(2,1)S(1)} async-done(((bf16[8,2,896]{2,1,0:T(2,128)(2,1)}), bf16[8,2,896]{2,1,0:T(2,128)(2,1)S(1)}, u32[]{:S(2)}, u32[]{:S(2)}) %all-to-all-start.3) | async-done | bytes 28704 | tf_op jit(solution)/shard_map/all_to_all | solution.py:202
  173.5 0.6 reshape.49
  (26 shorter events, 0.1 us)
Async XLA Ops:
  0.6 14.5 %copy-start.5 = (bf16[1,2,512,576]{2,3,1,0:T(8,128)(2,1)S(1)}, bf16[1,2,512,576]{2,3,1,0:T(8,128)(2,1)}, u32[]{:S(2)}) copy-start(bf16[1,2,512,576]{2,3,1,0:T(8,128)(2,1)} %param.11) | copy-start | bytes 3538948
  3.0 19.1 %all-to-all-start = ((bf16[8,2,3600]{2,1,0:T(2,128)(2,1)}), bf16[8,2,3600]{2,1,0:T(2,128)(2,1)}, u32[]{:S(2)}, u32[]{:S(2)}) async-start(bf16[8,2,3600]{2,1,0:T(2,128)(2,1)} %bitcast.1), calls=%async_computation | async-start | bytes 237568 | tf_op jit(solution)/shard_map/all_to_all | solution.py:202
  13.7 2.1 %copy-start.7 = (s32[64,2]{0,1:T(2,128)S(1)}, s32[64,2]{0,1:T(2,128)}, u32[]{:S(2)}) copy-start(s32[64,2]{0,1:T(2,128)} %param.13) | copy-start | bytes 1540
  13.7 2.2 %copy-start.8 = (s32[64,2]{0,1:T(2,128)S(1)}, s32[64,2]{0,1:T(2,128)}, u32[]{:S(2)}) copy-start(s32[64,2]{0,1:T(2,128)} %param.12) | copy-start | bytes 1540
  13.7 2.3 %copy-start.3 = (bf16[2,1,2,576]{3,2,1,0:T(2,128)(2,1)S(1)}, bf16[2,1,2,576]{3,2,1,0:T(2,128)(2,1)}, u32[]{:S(2)}) copy-start(bf16[2,1,2,576]{3,2,1,0:T(2,128)(2,1)} %fresh_ref.1) | copy-start | bytes 13828
  18.5 0.7 copy-start.1
  24.4 1.2 copy-start
  25.7 11.4 %copy-start.6 = (bf16[1,3584,128]{2,1,0:T(8,128)(2,1)S(1)}, bf16[1,3584,128]{2,1,0:T(8,128)(2,1)}, u32[]{:S(2)}) copy-start(bf16[1,3584,128]{2,1,0:T(8,128)(2,1)} %param.20) | copy-start | bytes 2752516
  25.7 79.1 %all-to-all-start.1 = ((bf16[64,8,1792]{2,1,0:T(8,128)(2,1)}), bf16[64,8,1792]{2,1,0:T(8,128)(2,1)S(1)}, u32[]{:S(2)}, u32[]{:S(2)}) async-start(bf16[64,8,1792]{2,1,0:T(8,128)(2,1)} %bitcast.32), calls=%async_computation.1 | async-start | bytes 3670016 | tf_op jit(solution)/shard_map/all_to_all | solution.py:202
  39.6 65.2 %collective-permute-start = (bf16[3584,256]{1,0:T(8,128)(2,1)}, bf16[3584,256]{1,0:T(8,128)(2,1)}, u32[]{:S(2)}, u32[]{:S(2)}) collective-permute-start(bf16[3584,256]{1,0:T(8,128)(2,1)} %pad_maximum_fusion.own_ref), channel_id=1, source_target_pairs={{0,64},{64,0},{1,65},{65,1},{2,66},{66,2},{3,67},{67,3},{4,68},{68... | collective-permute-start | bytes 5505032 | tf_op jit(solution)/shard_map/ppermute | solution.py:207
  43.5 41.5 %copy-start.2 = (bf16[2,128,512]{2,1,0:T(8,128)(2,1)S(1)}, bf16[2,128,512]{2,1,0:T(8,128)(2,1)}, u32[]{:S(2)}) copy-start(bf16[2,128,512]{2,1,0:T(8,128)(2,1)} %copy-done.1) | copy-start | bytes 786436
  44.9 25.1 %collective-permute-start.1 = (bf16[128,896]{1,0:T(8,128)(2,1)S(1)}, bf16[128,896]{1,0:T(8,128)(2,1)S(1)}, u32[]{:S(2)}, u32[]{:S(2)}) collective-permute-start(bf16[128,896]{1,0:T(8,128)(2,1)S(1)} %get-tuple-element.35), channel_id=1, source_target_pairs={{0,128},{128,256},{256,384},{384,0},{1,129},{129,257},{257,385},{3... | collective-permute-start | bytes 688136 | tf_op jit(solution)/shard_map/ppermute | solution.py:207
  47.1 22.9 %collective-permute-start.3 = (bf16[128,896]{1,0:T(8,128)(2,1)S(1)}, bf16[128,896]{1,0:T(8,128)(2,1)S(1)}, u32[]{:S(2)}, u32[]{:S(2)}) collective-permute-start(bf16[128,896]{1,0:T(8,128)(2,1)S(1)} %get-tuple-element.36), channel_id=1, source_target_pairs={{0,384},{128,0},{256,128},{384,256},{1,385},{129,1},{257,129},{385... | collective-permute-start | bytes 688136 | tf_op jit(solution)/shard_map/ppermute | solution.py:207
  52.3 29.4 %collective-permute-start.2 = (bf16[128,896]{1,0:T(8,128)(2,1)S(1)}, bf16[128,896]{1,0:T(8,128)(2,1)S(1)}, u32[]{:S(2)}, u32[]{:S(2)}) collective-permute-start(bf16[128,896]{1,0:T(8,128)(2,1)S(1)} %get-tuple-element.37), channel_id=1, source_target_pairs={{0,256},{128,384},{256,0},{384,128},{1,257},{129,385},{257,1},{385... | collective-permute-start | bytes 688136 | tf_op jit(solution)/shard_map/ppermute | solution.py:207
  81.9 22.9 %collective-permute-start.4 = (bf16[4,128,896]{2,1,0:T(8,128)(2,1)S(1)}, bf16[4,128,896]{2,1,0:T(8,128)(2,1)}, u32[]{:S(2)}, u32[]{:S(2)}) collective-permute-start(bf16[4,128,896]{2,1,0:T(8,128)(2,1)S(1)} %pad_maximum_fusion.1.own_ref), channel_id=1, source_target_pairs={{0,64},{64,0},{1,65},{65,1},{2,66},{66,2},{3,67},{67,3},{4,68},{68... | collective-permute-start | bytes 2752520 | tf_op jit(solution)/shard_map/ppermute | solution.py:207
  85.0 15.0 %collective-permute-start.5 = (bf16[2,128,512]{2,1,0:T(8,128)(2,1)S(1)}, bf16[2,128,512]{2,1,0:T(8,128)(2,1)}, u32[]{:S(2)}, u32[]{:S(2)}) collective-permute-start(bf16[2,128,512]{2,1,0:T(8,128)(2,1)S(1)} %copy-done.2), channel_id=1, source_target_pairs={{0,32},{1,33},{2,34},{3,35},{4,36},{5,37},{6,38},{7,39},{8,40},{9,... | collective-permute-start | bytes 786440 | tf_op jit(solution)/shard_map/ppermute | solution.py:207
  88.0 15.0 %collective-permute-start.7 = (bf16[2,128,512]{2,1,0:T(8,128)(2,1)S(1)}, bf16[2,128,512]{2,1,0:T(8,128)(2,1)}, u32[]{:S(2)}, u32[]{:S(2)}) collective-permute-start(bf16[2,128,512]{2,1,0:T(8,128)(2,1)S(1)} %get-tuple-element.25), channel_id=1, source_target_pairs={{0,1},{1,2},{2,3},{3,4},{4,5},{5,6},{6,7},{7,8},{8,9},{9,10},{10,1... | collective-permute-start | bytes 786440 | tf_op jit(solution)/shard_map/ppermute | solution.py:207
  89.9 13.1 %collective-permute-start.6 = (bf16[2,128,512]{2,1,0:T(8,128)(2,1)S(1)}, bf16[2,128,512]{2,1,0:T(8,128)(2,1)}, u32[]{:S(2)}, u32[]{:S(2)}) collective-permute-start(bf16[2,128,512]{2,1,0:T(8,128)(2,1)S(1)} %get-tuple-element.25), channel_id=1, source_target_pairs={{0,63},{1,0},{2,1},{3,2},{4,3},{5,4},{6,5},{7,6},{8,7},{9,8},{10,9... | collective-permute-start | bytes 786440 | tf_op jit(solution)/shard_map/ppermute | solution.py:207
  109.2 10.0 %collective-permute-start.10 = (bf16[256,256]{1,0:T(8,128)(2,1)S(1)}, bf16[256,256]{1,0:T(8,128)(2,1)S(1)}, u32[]{:S(2)}, u32[]{:S(2)}) collective-permute-start(bf16[256,256]{1,0:T(8,128)(2,1)S(1)} %hidden_units.1.h0), channel_id=1, source_target_pairs={{0,384},{128,0},{256,128},{384,256},{1,385},{129,1},{257,129},{385... | collective-permute-start | bytes 393224 | tf_op jit(solution)/shard_map/ppermute | solution.py:207
  113.1 11.2 %collective-permute-start.8 = (bf16[256,256]{1,0:T(8,128)(2,1)S(1)}, bf16[256,256]{1,0:T(8,128)(2,1)S(1)}, u32[]{:S(2)}, u32[]{:S(2)}) collective-permute-start(bf16[256,256]{1,0:T(8,128)(2,1)S(1)} %hidden_units.1.h0), channel_id=1, source_target_pairs={{0,128},{128,256},{256,384},{384,0},{1,129},{129,257},{257,385},{3... | collective-permute-start | bytes 393224 | tf_op jit(solution)/shard_map/ppermute | solution.py:207
  119.2 8.0 %collective-permute-start.11 = (bf16[128,256]{1,0:T(8,128)(2,1)S(1)}, bf16[128,256]{1,0:T(8,128)(2,1)S(1)}, u32[]{:S(2)}, u32[]{:S(2)}) collective-permute-start(bf16[128,256]{1,0:T(8,128)(2,1)S(1)} %slice.20), channel_id=1, source_target_pairs={{0,384},{128,0},{256,128},{384,256},{1,385},{129,1},{257,129},{385... | collective-permute-start | bytes 196616 | tf_op jit(solution)/shard_map/ppermute | solution.py:207
  124.3 42.0 %copy-start.4 = (bf16[2,1,2,128,512]{4,3,0,2,1:T(8,128)(2,1)S(1)}, bf16[2,1,2,128,512]{4,3,0,2,1:T(8,128)(2,1)}, u32[]{:S(2)}) copy-start(bf16[2,1,2,128,512]{4,3,0,2,1:T(8,128)(2,1)} %maximum_bitcast_fusion) | copy-start | bytes 1572868
  124.3 8.0 %collective-permute-start.9 = (bf16[128,256]{1,0:T(8,128)(2,1)S(1)}, bf16[128,256]{1,0:T(8,128)(2,1)S(1)}, u32[]{:S(2)}, u32[]{:S(2)}) collective-permute-start(bf16[128,256]{1,0:T(8,128)(2,1)S(1)} %slice.19), channel_id=1, source_target_pairs={{0,128},{128,256},{256,384},{384,0},{1,129},{129,257},{257,385},{3... | collective-permute-start | bytes 196616 | tf_op jit(solution)/shard_map/ppermute | solution.py:207
  160.1 13.4 %all-to-all-start.3 = ((bf16[8,2,896]{2,1,0:T(2,128)(2,1)}), bf16[8,2,896]{2,1,0:T(2,128)(2,1)S(1)}, u32[]{:S(2)}, u32[]{:S(2)}) async-start(bf16[8,2,896]{2,1,0:T(2,128)(2,1)} %reshape.47), calls=%async_computation.3 | async-start | bytes 57344 | tf_op jit(solution)/shard_map/all_to_all | solution.py:202

commit v3 on v1

v3 whole, which is shorter than its diff:
```python
import functools

import jax
import jax.numpy as jnp
from jax import lax
from jax.experimental import pallas as pl
from jax.experimental.pallas import tpu as pltpu
from jax.sharding import Mesh
from jax.sharding import PartitionSpec as P

KV_RANK = 512
HEAD_QK = 192
CAP = 4
EP = ("yl", "x", "z")
DP = ("yh", "c")
COLUMN = ("yh", "c", "yl")
PLANE = ("x", "z")
BF = jnp.bfloat16
F32 = jnp.float32
PARAMS = pltpu.CompilerParams(vmem_limit_bytes=48 * 1024 * 1024)


def dot(a, b, dims=((1,), (0,))):
    return lax.dot_general(a, b, (dims, ((), ())), preferred_element_type=F32)


def iota(shape, dim):
    return lax.broadcasted_iota(jnp.int32, shape, dim)


def vmem(n):
    return [pl.BlockSpec(memory_space=pltpu.VMEM)] * n


def attend_kernel(len_ref, query_ref, cache_ref, fresh_ref, out0_ref, out1_ref, keys_ref):
    steps, _, requests, heads, width = query_ref.shape
    cached = cache_ref.shape[2]
    total = keys_ref.shape[0]
    rows = steps * heads
    column = iota((rows, total), 1)
    row_step = iota((rows, total), 0) // heads
    for request, out_ref in zip(range(requests), (out0_ref, out1_ref)):
        keys_ref[:cached] = cache_ref[0, request]
        place = iota((total - cached, width), 0)
        tail = jnp.zeros((total - cached, width), F32)
        for step in range(steps):
            row = fresh_ref[step, 0, request : request + 1, :].astype(F32)
            tail = jnp.where(place == step, row, tail)
        keys_ref[cached:] = tail.astype(BF)
        query = query_ref[:, 0, request].reshape(rows, width)
        keys = keys_ref[...]
        scores = dot(query, keys, ((1,), (1,))) * (HEAD_QK**-0.5)
        old = column < len_ref[request]
        new = (column >= cached) & (column - cached <= row_step)
        scores = jnp.where(old | new, scores, -jnp.inf)
        weights = jnp.exp(scores - jnp.max(scores, 1, keepdims=True))
        probs = (weights / jnp.sum(weights, 1, keepdims=True)).astype(BF)
        served = dot(probs, keys[:, :KV_RANK]).astype(BF)
        out_ref[...] = served.reshape(steps, heads, KV_RANK)


def attend(length, queries, cache, fresh):
    steps, _, _, heads, width = queries.shape
    out = jax.ShapeDtypeStruct((steps, heads, KV_RANK), BF)
    return pl.pallas_call(
        attend_kernel,
        out_shape=(out, out),
        in_specs=[pl.BlockSpec(memory_space=pltpu.SMEM), *vmem(3)],
        out_specs=tuple(vmem(2)),
        scratch_shapes=[pltpu.VMEM((cache.shape[2] + 128, width), BF)],
        compiler_params=PARAMS,
        name="attend",
    )(length, queries, cache, fresh)


def dispatch_kernel(yl_ref, tokens_ref, send_ref, mix_ref):
    rows = tokens_ref.shape[0]
    slots, width = send_ref.shape
    tail = tokens_ref[:, width:].astype(F32)
    top = tail.shape[1] // 2
    sigmoid = jax.nn.sigmoid(tail[:, top:])
    gates = 2.5 * sigmoid / jnp.sum(sigmoid, 1, keepdims=True)
    slot = iota((rows, slots), 1)
    expert = (slot // (2 * CAP) + yl_ref[0] * (slots // (2 * CAP))).astype(F32)
    named = jnp.zeros((rows, slots), F32)
    gate = jnp.zeros((rows, slots), F32)
    for k in range(top):
        hit = tail[:, k : k + 1] == expert
        named = jnp.where(hit, 1.0, named)
        gate = jnp.where(hit, gates[:, k : k + 1], gate)
    this, other = iota((rows, rows), 0), iota((rows, rows), 1)
    before = ((other < this) & (other // 2 % 2 == this // 2 % 2)).astype(F32)
    earlier = dot(before.astype(BF), named.astype(BF))
    chosen = (named > 0) & (earlier == (slot % CAP).astype(F32))
    chosen = chosen & (slot % (2 * CAP) // CAP == iota((rows, slots), 0) // 2 % 2)
    pick = chosen.astype(F32).astype(BF)
    send_ref[...] = dot(pick, tokens_ref[:, :width], ((0,), (0,))).astype(BF)
    high = gate.astype(BF).astype(F32)
    mix = [jnp.where(chosen, part, 0.0) for part in (high, gate - high)]
    mix_ref[...] = jnp.concatenate(mix, 0).astype(BF)


def dispatch(yl, tokens, slots, width):
    return pl.pallas_call(
        dispatch_kernel,
        out_shape=(
            jax.ShapeDtypeStruct((slots, width), BF),
            jax.ShapeDtypeStruct((2 * tokens.shape[0], slots), BF),
        ),
        in_specs=[pl.BlockSpec(memory_space=pltpu.SMEM), *vmem(1)],
        out_specs=tuple(vmem(2)),
        compiler_params=PARAMS,
        name="dispatch",
    )(yl.reshape(1), tokens)


def hidden_kernel(rows_ref, own_ref, peer_ref, out_ref):
    units = own_ref.shape[1] // 2
    rows = rows_ref[...]
    for place, ref in enumerate((own_ref, peer_ref)):
        both = dot(rows, ref[...])
        gate, up = both[:, :units], both[:, units:]
        value = gate / (1.0 + jnp.exp(-gate)) * up
        out_ref[:, place * units : (place + 1) * units] = value.astype(BF)


def hidden_units(rows, own, peer):
    return pl.pallas_call(
        hidden_kernel,
        out_shape=jax.ShapeDtypeStruct((rows.shape[0], own.shape[1]), BF),
        in_specs=vmem(3),
        out_specs=vmem(1)[0],
        compiler_params=PARAMS,
        name="hidden_units",
    )(rows, own, peer)


def down_kernel(yh_ref, h_ref, own_ref, peer_ref, out_ref):
    total = None
    count = h_ref.shape[0]
    for number in range(count):
        weights = jnp.concatenate([own_ref[number], peer_ref[number]], 0)
        term = dot(h_ref[(yh_ref[0] + count - number) % count], weights)
        total = term if total is None else total + term
    out_ref[...] = total.astype(BF)


def down(yh, h, own, peer):
    return pl.pallas_call(
        down_kernel,
        out_shape=jax.ShapeDtypeStruct((h.shape[1], own.shape[2]), BF),
        in_specs=[pl.BlockSpec(memory_space=pltpu.SMEM), *vmem(3)],
        out_specs=vmem(1)[0],
        compiler_params=PARAMS,
        name="down",
    )(yh.reshape(1), h, own, peer)


def combine_kernel(mix_ref, back_ref, out_ref):
    rows = out_ref.shape[0]
    value = dot(mix_ref[...], back_ref[...])
    out_ref[...] = value[:rows] + value[rows:]


def combine(mix, back):
    return pl.pallas_call(
        combine_kernel,
        out_shape=jax.ShapeDtypeStruct((mix.shape[0] // 2, back.shape[1]), F32),
        in_specs=vmem(2),
        out_specs=vmem(1)[0],
        compiler_params=PARAMS,
        name="combine",
    )(mix, back)


def exchange(x, axes):
    return lax.all_to_all(x, axes, split_axis=0, concat_axis=0, tiled=True)


def shifted(x, axes, by):
    size = lax.axis_size(axes)
    return lax.ppermute(x, axes, [(i, (i + by) % size) for i in range(size)])


def shards(
    latent_cache,
    lengths,
    new_home,
    queries,
    new_latent,
    hidden,
    routes,
    route_logits,
    w_gate,
    w_up,
    w_down,
):
    experts = lax.axis_size(EP)
    yh_size, yl_size = lax.axis_size("yh"), lax.axis_size("yl")
    peers = experts // yl_size
    own_rank = lax.axis_index(EP)
    steps, _, requests, width = hidden.shape
    chunk = width // yh_size
    block = yl_size * CAP
    slots = peers * block

    packed = jnp.concatenate([hidden, routes.astype(BF), route_logits], -1)[:, 0]
    packed = jnp.broadcast_to(packed[None, :, None], (yh_size, steps, yl_size, *packed.shape[1:]))
    tokens = exchange(packed.reshape(-1, *packed.shape[3:]), COLUMN)
    served = attend(lengths[own_rank], queries, latent_cache, new_latent)
    tokens, served0, served1 = lax.optimization_barrier((tokens, *served))
    tokens = tokens.reshape(-1, tokens.shape[-1])
    send, mix = dispatch(lax.axis_index("yl"), tokens, slots, width)
    arrived = exchange(send.reshape(peers, block, width), PLANE).reshape(slots, width)

    own_w = jnp.concatenate([w_gate[0], w_up[0]], 1)
    peer_w = shifted(own_w, "c", 1)
    yh = lax.axis_index("yh")
    sent = [
        lax.dynamic_slice_in_dim(w_down[0], (yh + s) % yh_size * chunk, chunk, 1)
        for s in range(yh_size)
    ]
    own_down = jnp.stack([shifted(x, "yh", s) if s else x for s, x in enumerate(sent)])
    peer_down = shifted(own_down, "c", 1)

    far = shifted(served0, EP, experts // 2)
    lower = shifted(served1, EP, 1)
    upper = shifted(served1, EP, -1)
    home = new_home[own_rank]
    result0 = jnp.where(home[0] == own_rank, served0, far)
    result1 = jnp.where(
        home[1] == own_rank,
        served1,
        jnp.where(home[1] == (own_rank + 1) % experts, upper, lower),
    )
    attended = jnp.stack([result0, result1], 1)[:, None]

    arrived, peer_w, own_down, attended = lax.optimization_barrier(
        (arrived, peer_w, own_down, attended)
    )
    h = hidden_units(arrived, own_w, peer_w)
    h = exchange(jnp.broadcast_to(h[None], (yh_size, *h.shape)), "yh")
    out = down(yh, h, own_down, peer_down)
    back = exchange(out.reshape(peers, block, chunk), PLANE).reshape(slots, chunk)
    mixed = combine(mix, back)
    final = exchange(mixed.reshape(-1, requests, chunk), COLUMN)
    final = final.reshape(yh_size, steps, yl_size, requests, chunk).sum(2).astype(BF)
    moe_out = final.transpose(1, 2, 0, 3).reshape(steps, 1, requests, width)
    return attended, moe_out


def solution(mesh):
    torus = Mesh(mesh.devices.reshape(4, 2, 2, 4, 8), ("yh", "c", "yl", "x", "z"))
    placed = (
        P(EP, DP, None, None),
        P(None, DP),
        P(None, DP),
        P(None, EP, DP, None, None),
        P(None, EP, DP, None),
        P(None, EP, DP, None),
        P(None, EP, DP, None),
        P(None, EP, DP, None),
        P(EP, None, DP),
        P(EP, None, DP),
        P(EP, DP, None),
    )
    return jax.shard_map(
        shards,
        mesh=torus,
        in_specs=placed,
        out_specs=(P(None, EP, DP, None, None), P(None, EP, DP, None)),
        check_vma=False,
    )
```

time: 166 us -> 150 us (0.904)
  waiting for transfers between devices: 48.8 us -> 37 us
  starting transfers between devices: 72.3 us -> 67 us
  local copies, waits for them, and re-layouts: 8.54 us -> 12.7 us
  Pallas kernels: 11.5 us -> 8.65 us
  blocking collectives: 17.1 us -> 14.4 us
  other arithmetic: 3.55 us -> 5.7 us
    ppermute x11 -> x8, waiting for transfers between devices: 42.5 us -> 10.9 us  [shifted(): return lax.ppermute(x, axes, [(i, (i + by) % size) for i in range(size)])]
    all_to_all x3 -> x4, waiting for transfers between devices: 6.31 us -> 26.1 us  [exchange(): return lax.all_to_all(x, axes, split_axis=0, concat_axis=0, tiled=True)]
    ppermute x11 -> x8, starting transfers between devices: 41.1 us -> 26.9 us  [shifted(): return lax.ppermute(x, axes, [(i, (i + by) % size) for i in range(size)])]
    all_to_all x3 -> x4, starting transfers between devices: 31.2 us -> 40.1 us  [exchange(): return lax.all_to_all(x, axes, split_axis=0, concat_axis=0, tiled=True)]
    all_to_all x1, blocking collectives: 17.1 us -> 14.4 us  [exchange(): return lax.all_to_all(x, axes, split_axis=0, concat_axis=0, tiled=True)]
    unnamed x15 -> x19, local copies, waits for them, and re-layouts: 4.1 us -> 5.83 us
  transfers between devices with their start and end apart: 14 -> 12, of which waited for: 7 -> 6; matrix products, arithmetic and copies ran while one was open for 5% -> 8% of each run, Pallas kernels for 4% -> 4%
where the time goes in v3:
time: 150 us; the launch traced here: 149 us
  starting transfers between devices  67 us (45%)
  waiting for transfers between devices  37 us (25%)
  blocking collectives  14.4 us (10%)
  local copies, waits for them, and re-layouts  12.7 us (8%)
  Pallas kernels  8.65 us (6%)
  other arithmetic  5.7 us (4%)
  between operations  3.03 us (2%)
    all_to_all x4, starting transfers between devices, exchange(): return lax.all_to_all(x, axes, split_axis=0, concat_axis=0, tiled=True)  40.1 us
    ppermute x8, starting transfers between devices, shifted(): return lax.ppermute(x, axes, [(i, (i + by) % size) for i in range(size)])  26.9 us
    all_to_all x4, waiting for transfers between devices, exchange(): return lax.all_to_all(x, axes, split_axis=0, concat_axis=0, tiled=True)  26.1 us
    all_to_all x1, blocking collectives, exchange(): return lax.all_to_all(x, axes, split_axis=0, concat_axis=0, tiled=True)  14.4 us
    ppermute x8, waiting for transfers between devices, shifted(): return lax.ppermute(x, axes, [(i, (i + by) % size) for i in range(size)])  10.9 us
    unnamed x19, local copies, waits for them, and re-layouts  5.83 us
    pallas_call x1, Pallas kernels, hidden_units(): pl.pallas_call(hidden_kernel, out_shape=jax.ShapeDtypeStruct((rows.shape[...  3.18 us
  transfers between devices with their start and end apart: 12, of which 6 were waited for; matrix products, arithmetic and copies ran while one was open for 8% of the time, Pallas kernels for 4%

profile of v3, /device:TPU:1, one launch (start us, length us, event | category | flops | bytes accessed | tf_op | source)
XLA Modules:
  0.0 148.5 jit_solution(3015552663824600000)
XLA Ops:
  0.6 0.7 convert_element_type.10
  1.3 0.8 concatenate.6
  2.2 0.8 broadcast_in_dim.17
  3.0 10.2 %all-to-all-start = ((bf16[16,2,3600]{2,1,0:T(2,128)(2,1)}), bf16[16,2,3600]{2,1,0:T(2,128)(2,1)S(1)}, u32[]{:S(2)}, u32[]{:S(2)}) async-start(bf16[16,2,3600]{2,1,0:T(2,128)(2,1)} %bitcast.2), calls=%async_computation | async-start | bytes 475136 | tf_op jit(solution)/shard_map/all_to_all | solution.py:177
  13.2 0.0 copy-start.7
  13.2 0.0 copy-start.1
  13.2 1.7 %copy.20.cache_ref = bf16[1,2,512,576]{3,2,1,0:T(8,128)(2,1)S(1)} copy(bf16[1,2,512,576]{2,3,1,0:T(8,128)(2,1)} %param.11) | data formatting | bytes 2359296 | tf_op args[0]
  14.9 1.4 copy.19.query_ref
  16.3 0.2 constant_dynamic-slice_fusion
  16.5 2.5 %attend.1 = (bf16[2,128,512]{2,1,0:T(8,128)(2,1)S(1)}, bf16[2,128,512]{2,1,0:T(8,128)(2,1)S(1)}) custom-call(s32[2]{0:T(128)S(1)} %get-tuple-element.37.len_ref, bf16[2,1,2,128,576]{4,3,2,1,0:T(8,128)(2,1)S(1)} %copy.19.query_ref, bf16[1,2,512,576]{3,2,1,0:T(8,128)(2,1)S(1)} %copy.20.cache_ref, bf16[2,1,2,576]{3,2,1,0:T(2,128)(2,1)S(1)} %copy-done.1), custom_call_target="tpu_custom_call" | custom-call | tf_op jit(solution)/shard_map/attend/pallas_call | solution.py:65
  19.0 3.9 %all-to-all-done = bf16[16,2,3600]{2,1,0:T(2,128)(2,1)S(1)} async-done(((bf16[16,2,3600]{2,1,0:T(2,128)(2,1)}), bf16[16,2,3600]{2,1,0:T(2,128)(2,1)S(1)}, u32[]{:S(2)}, u32[]{:S(2)}) %all-to-all-start) | async-done | bytes 230432 | tf_op jit(solution)/shard_map/all_to_all | solution.py:177
  22.9 0.2 reshape.50.tokens_ref
  23.1 0.9 dispatch.1
  24.0 1.3 copy-done
  25.3 11.3 %all-to-all-start.1 = ((bf16[32,8,3584]{2,1,0:T(8,128)(2,1)}), bf16[32,8,3584]{2,1,0:T(8,128)(2,1)S(1)}, u32[]{:S(2)}, u32[]{:S(2)}) async-start(bf16[32,8,3584]{2,1,0:T(8,128)(2,1)} %bitcast.34), calls=%async_computation.1 | async-start | bytes 3670016 | tf_op jit(solution)/shard_map/all_to_all | solution.py:177
  36.6 2.6 %pad_maximum_fusion.own_ref = bf16[3584,256]{1,0:T(8,128)(2,1)} fusion(bf16[3584,128]{1,0:T(8,128)(2,1)S(1)} %bitcast.37, bf16[3584,128]{1,0:T(8,128)(2,1)} %bitcast.38), kind=kLoop, calls=%fused_computation | loop fusion | flops 3670016 | bytes 3670016 | tf_op jit(solution)/shard_map/concatenate | solution.py:216
  39.2 2.6 %collective-permute-start = (bf16[3584,256]{1,0:T(8,128)(2,1)}, bf16[3584,256]{1,0:T(8,128)(2,1)}, u32[]{:S(2)}, u32[]{:S(2)}) collective-permute-start(bf16[3584,256]{1,0:T(8,128)(2,1)} %pad_maximum_fusion.own_ref), channel_id=1, source_target_pairs={{0,64},{64,0},{1,65},{65,1},{2,66},{66,2},{3,67},{67,3},{4,68},{68... | collective-permute-start | bytes 5505032 | tf_op jit(solution)/shard_map/ppermute | solution.py:182
  41.9 2.1 %constant_dynamic-slice_fusion.1 = (bf16[1,128,896]{2,1,0:T(8,128)(2,1)S(1)}, bf16[128,896]{1,0:T(8,128)(2,1)S(1)}, bf16[128,896]{1,0:T(8,128)(2,1)}, bf16[128,896]{1,0:T(8,128)(2,1)S(1)}) fusion(bf16[1,128,3584]{2,1,0:T(8,128)(2,1)} %param.21, s32[]{:T(128)S(6)} %select_n.61, s32[]{:T(128)S(6)} %select_n.63, s32[]{:T(128)S(6)} %select_n.67, s32[]{:T(128)S(6)} %select_n.65), kind=kLoop, calls=%fused_computation.11 | loop fusion | bytes 1835024 | tf_op jit(solution)/shard_map/dynamic_slice | solution.py:220
  43.9 4.4 %collective-permute-start.2 = (bf16[128,896]{1,0:T(8,128)(2,1)S(1)}, bf16[128,896]{1,0:T(8,128)(2,1)S(1)}, u32[]{:S(2)}, u32[]{:S(2)}) collective-permute-start(bf16[128,896]{1,0:T(8,128)(2,1)S(1)} %get-tuple-element.33), channel_id=1, source_target_pairs={{0,256},{128,384},{256,0},{384,128},{1,257},{129,385},{257,1},{385... | collective-permute-start | bytes 688136 | tf_op jit(solution)/shard_map/ppermute | solution.py:182
  48.3 4.5 %collective-permute-start.3 = (bf16[128,896]{1,0:T(8,128)(2,1)}, bf16[128,896]{1,0:T(8,128)(2,1)S(1)}, u32[]{:S(2)}, u32[]{:S(2)}) collective-permute-start(bf16[128,896]{1,0:T(8,128)(2,1)} %get-tuple-element.32), channel_id=1, source_target_pairs={{0,384},{128,0},{256,128},{384,256},{1,385},{129,1},{257,129},{385... | collective-permute-start | bytes 688136 | tf_op jit(solution)/shard_map/ppermute | solution.py:182
  52.8 1.9 %collective-permute-start.1 = (bf16[128,896]{1,0:T(8,128)(2,1)S(1)}, bf16[128,896]{1,0:T(8,128)(2,1)S(1)}, u32[]{:S(2)}, u32[]{:S(2)}) collective-permute-start(bf16[128,896]{1,0:T(8,128)(2,1)S(1)} %get-tuple-element.31), channel_id=1, source_target_pairs={{0,128},{128,256},{256,384},{384,0},{1,129},{129,257},{257,385},{3... | collective-permute-start | bytes 688136 | tf_op jit(solution)/shard_map/ppermute | solution.py:182
  54.8 7.4 %collective-permute-start.5 = (bf16[2,128,512]{2,1,0:T(8,128)(2,1)S(1)}, bf16[2,128,512]{2,1,0:T(8,128)(2,1)}, u32[]{:S(2)}, u32[]{:S(2)}) collective-permute-start(bf16[2,128,512]{2,1,0:T(8,128)(2,1)S(1)} %get-tuple-element.18), channel_id=1, source_target_pairs={{0,63},{1,0},{2,1},{3,2},{4,3},{5,4},{6,5},{7,6},{8,7},{9,8},{10,9... | collective-permute-start | bytes 786440 | tf_op jit(solution)/shard_map/ppermute | solution.py:182
  62.1 0.0 collective-permute-done.2
  62.1 1.9 %collective-permute-start.6 = (bf16[2,128,512]{2,1,0:T(8,128)(2,1)S(1)}, bf16[2,128,512]{2,1,0:T(8,128)(2,1)}, u32[]{:S(2)}, u32[]{:S(2)}) collective-permute-start(bf16[2,128,512]{2,1,0:T(8,128)(2,1)S(1)} %get-tuple-element.18), channel_id=1, source_target_pairs={{0,1},{1,2},{2,3},{3,4},{4,5},{5,6},{6,7},{7,8},{8,9},{9,10},{10,1... | collective-permute-start | bytes 786440 | tf_op jit(solution)/shard_map/ppermute | solution.py:182
  64.1 0.6 fusion.1
  66.7 4.9 %collective-permute-done.3 = bf16[128,896]{1,0:T(8,128)(2,1)S(1)} collective-permute-done((bf16[128,896]{1,0:T(8,128)(2,1)}, bf16[128,896]{1,0:T(8,128)(2,1)S(1)}, u32[]{:S(2)}, u32[]{:S(2)}) %collective-permute-start.3) | collective-permute-done | bytes 229408 | tf_op jit(solution)/shard_map/ppermute | solution.py:182
  71.7 1.9 %collective-permute-start.4 = (bf16[2,128,512]{2,1,0:T(8,128)(2,1)S(1)}, bf16[2,128,512]{2,1,0:T(8,128)(2,1)S(1)}, u32[]{:S(2)}, u32[]{:S(2)}) collective-permute-start(bf16[2,128,512]{2,1,0:T(8,128)(2,1)S(1)} %get-tuple-element.17), channel_id=1, source_target_pairs={{0,32},{1,33},{2,34},{3,35},{4,36},{5,37},{6,38},{7,39},{8,40},{9,... | collective-permute-start | bytes 786440 | tf_op jit(solution)/shard_map/ppermute | solution.py:182
  73.6 0.0 collective-permute-done.1
  73.6 0.7 copy-done.5
  74.3 1.3 pad_maximum_fusion.1.own_ref
  75.6 2.4 %collective-permute-start.7 = (bf16[4,128,896]{2,1,0:T(8,128)(2,1)S(1)}, bf16[4,128,896]{2,1,0:T(8,128)(2,1)}, u32[]{:S(2)}, u32[]{:S(2)}) collective-permute-start(bf16[4,128,896]{2,1,0:T(8,128)(2,1)S(1)} %pad_maximum_fusion.1.own_ref), channel_id=1, source_target_pairs={{0,64},{64,0},{1,65},{65,1},{2,66},{66,2},{3,67},{67,3},{4,68},{68... | collective-permute-start | bytes 2752520 | tf_op jit(solution)/shard_map/ppermute | solution.py:182
  78.0 5.7 %collective-permute-done.5 = bf16[2,128,512]{2,1,0:T(8,128)(2,1)} collective-permute-done((bf16[2,128,512]{2,1,0:T(8,128)(2,1)S(1)}, bf16[2,128,512]{2,1,0:T(8,128)(2,1)}, u32[]{:S(2)}, u32[]{:S(2)}) %collective-permute-start.5) | collective-permute-done | bytes 262176 | tf_op jit(solution)/shard_map/ppermute | solution.py:182
  83.7 0.2 collective-permute-done.6
  83.9 1.0 select_bitcast_fusion
  84.9 0.0 collective-permute-done.4
  84.9 0.1 maximum_bitcast_fusion
  85.0 3.2 %hidden_units.1 = bf16[256,256]{1,0:T(8,128)(2,1)S(1)} custom-call(bf16[256,3584]{1,0:T(8,128)(2,1)S(1)} %bitcast.33, bf16[3584,256]{1,0:T(8,128)(2,1)} %pad_maximum_fusion.own_ref, bf16[3584,256]{1,0:T(8,128)(2,1)} %collective-permute-done.peer_ref), custom_call_target="tpu_custom_call" | custom-call | tf_op jit(solution)/shard_map/hidden_units/pallas_call | solution.py:128
  88.2 0.8 broadcast_in_dim.19
  89.0 5.5 %all-to-all-start.2 = ((bf16[4,256,256]{2,1,0:T(8,128)(2,1)}), bf16[4,256,256]{2,1,0:T(8,128)(2,1)S(1)}, u32[]{:S(2)}, u32[]{:S(2)}) async-start(bf16[4,256,256]{2,1,0:T(8,128)(2,1)} %broadcast_in_dim.19), calls=%async_computation.2 | async-start | bytes 1048576 | tf_op jit(solution)/shard_map/all_to_all | solution.py:177
  94.5 14.9 %all-to-all-done.2.h_ref = bf16[4,256,256]{2,1,0:T(8,128)(2,1)S(1)} async-done(((bf16[4,256,256]{2,1,0:T(8,128)(2,1)}), bf16[4,256,256]{2,1,0:T(8,128)(2,1)S(1)}, u32[]{:S(2)}, u32[]{:S(2)}) %all-to-all-start.2) | async-done | bytes 524320 | tf_op jit(solution)/shard_map/all_to_all | solution.py:177
  109.4 1.9 %down.1 = bf16[256,896]{1,0:T(8,128)(2,1)S(1)} custom-call(s32[1]{0:T(128)} %bitcast.18.yh_ref, bf16[4,256,256]{2,1,0:T(8,128)(2,1)S(1)} %all-to-all-done.2.h_ref, bf16[4,128,896]{2,1,0:T(8,128)(2,1)S(1)} %pad_maximum_fusion.1.own_ref, bf16[4,128,896]{2,1,0:T(8,128)(2,1)} %collective-permute-done.7.peer_ref), custom_call_target="tpu_custom_call" | custom-call | tf_op jit(solution)/shard_map/down/pallas_call | solution.py:149
  111.3 14.4 %all_to_all.25 = bf16[32,8,896]{2,1,0:T(8,128)(2,1)S(1)} all-to-all(bf16[32,8,896]{2,1,0:T(8,128)(2,1)S(1)} %bitcast.36), channel_id=1, replica_groups=mesh['yh'=4,'c'=2,'yl'=2,'x'=4,'z'=8] {'x','z'}, dimensions={0} | all-to-all | bytes 917504 | tf_op jit(solution)/shard_map/all_to_all | solution.py:177
  125.7 0.2 combine.1
  125.9 0.7 reshape.56
  126.7 13.0 %all-to-all-start.4 = ((f32[16,2,896]{2,1,0:T(2,128)}), f32[16,2,896]{2,1,0:T(2,128)S(1)}, u32[]{:S(2)}, u32[]{:S(2)}) async-start(f32[16,2,896]{2,1,0:T(2,128)} %reshape.56), calls=%async_computation.4 | async-start | bytes 229376 | tf_op jit(solution)/shard_map/all_to_all | solution.py:177
  139.7 0.8 copy.22
  140.5 7.3 %all-to-all-done.4 = f32[16,2,896]{2,1,0:T(2,128)S(1)} async-done(((f32[16,2,896]{2,1,0:T(2,128)}), f32[16,2,896]{2,1,0:T(2,128)S(1)}, u32[]{:S(2)}, u32[]{:S(2)}) %all-to-all-start.4) | async-done | bytes 114720 | tf_op jit(solution)/shard_map/all_to_all | solution.py:177
  147.9 0.6 reshape.58
  (18 shorter events, 0.1 us)
Async XLA Ops:
  3.0 19.9 %all-to-all-start = ((bf16[16,2,3600]{2,1,0:T(2,128)(2,1)}), bf16[16,2,3600]{2,1,0:T(2,128)(2,1)S(1)}, u32[]{:S(2)}, u32[]{:S(2)}) async-start(bf16[16,2,3600]{2,1,0:T(2,128)(2,1)} %bitcast.2), calls=%async_computation | async-start | bytes 475136 | tf_op jit(solution)/shard_map/all_to_all | solution.py:177
  13.2 3.1 %copy-start.6 = (s32[64,2]{0,1:T(2,128)S(1)}, s32[64,2]{0,1:T(2,128)}, u32[]{:S(2)}) copy-start(s32[64,2]{0,1:T(2,128)} %param.13) | copy-start | bytes 1540
  13.2 3.1 %copy-start.7 = (s32[64,2]{0,1:T(2,128)S(1)}, s32[64,2]{0,1:T(2,128)}, u32[]{:S(2)}) copy-start(s32[64,2]{0,1:T(2,128)} %param.12) | copy-start | bytes 1540
  13.2 3.3 %copy-start.1 = (bf16[2,1,2,576]{3,2,1,0:T(2,128)(2,1)S(1)}, bf16[2,1,2,576]{3,2,1,0:T(2,128)(2,1)}, u32[]{:S(2)}) copy-start(bf16[2,1,2,576]{3,2,1,0:T(2,128)(2,1)} %fresh_ref.1) | copy-start | bytes 13828
  24.0 1.3 copy-start
  25.3 11.4 %copy-start.2 = (bf16[1,3584,128]{2,1,0:T(8,128)(2,1)S(1)}, bf16[1,3584,128]{2,1,0:T(8,128)(2,1)}, u32[]{:S(2)}) copy-start(bf16[1,3584,128]{2,1,0:T(8,128)(2,1)} %param.20) | copy-start | bytes 2752516
  25.3 59.7 %all-to-all-start.1 = ((bf16[32,8,3584]{2,1,0:T(8,128)(2,1)}), bf16[32,8,3584]{2,1,0:T(8,128)(2,1)S(1)}, u32[]{:S(2)}, u32[]{:S(2)}) async-start(bf16[32,8,3584]{2,1,0:T(8,128)(2,1)} %bitcast.34), calls=%async_computation.1 | async-start | bytes 3670016 | tf_op jit(solution)/shard_map/all_to_all | solution.py:177
  39.2 45.7 %collective-permute-start = (bf16[3584,256]{1,0:T(8,128)(2,1)}, bf16[3584,256]{1,0:T(8,128)(2,1)}, u32[]{:S(2)}, u32[]{:S(2)}) collective-permute-start(bf16[3584,256]{1,0:T(8,128)(2,1)} %pad_maximum_fusion.own_ref), channel_id=1, source_target_pairs={{0,64},{64,0},{1,65},{65,1},{2,66},{66,2},{3,67},{67,3},{4,68},{68... | collective-permute-start | bytes 5505032 | tf_op jit(solution)/shard_map/ppermute | solution.py:182
  43.9 18.2 %collective-permute-start.2 = (bf16[128,896]{1,0:T(8,128)(2,1)S(1)}, bf16[128,896]{1,0:T(8,128)(2,1)S(1)}, u32[]{:S(2)}, u32[]{:S(2)}) collective-permute-start(bf16[128,896]{1,0:T(8,128)(2,1)S(1)} %get-tuple-element.33), channel_id=1, source_target_pairs={{0,256},{128,384},{256,0},{384,128},{1,257},{129,385},{257,1},{385... | collective-permute-start | bytes 688136 | tf_op jit(solution)/shard_map/ppermute | solution.py:182
  48.3 23.4 %collective-permute-start.3 = (bf16[128,896]{1,0:T(8,128)(2,1)}, bf16[128,896]{1,0:T(8,128)(2,1)S(1)}, u32[]{:S(2)}, u32[]{:S(2)}) collective-permute-start(bf16[128,896]{1,0:T(8,128)(2,1)} %get-tuple-element.32), channel_id=1, source_target_pairs={{0,384},{128,0},{256,128},{384,256},{1,385},{129,1},{257,129},{385... | collective-permute-start | bytes 688136 | tf_op jit(solution)/shard_map/ppermute | solution.py:182
  52.8 20.8 %collective-permute-start.1 = (bf16[128,896]{1,0:T(8,128)(2,1)S(1)}, bf16[128,896]{1,0:T(8,128)(2,1)S(1)}, u32[]{:S(2)}, u32[]{:S(2)}) collective-permute-start(bf16[128,896]{1,0:T(8,128)(2,1)S(1)} %get-tuple-element.31), channel_id=1, source_target_pairs={{0,128},{128,256},{256,384},{384,0},{1,129},{129,257},{257,385},{3... | collective-permute-start | bytes 688136 | tf_op jit(solution)/shard_map/ppermute | solution.py:182
  54.8 28.9 %collective-permute-start.5 = (bf16[2,128,512]{2,1,0:T(8,128)(2,1)S(1)}, bf16[2,128,512]{2,1,0:T(8,128)(2,1)}, u32[]{:S(2)}, u32[]{:S(2)}) collective-permute-start(bf16[2,128,512]{2,1,0:T(8,128)(2,1)S(1)} %get-tuple-element.18), channel_id=1, source_target_pairs={{0,63},{1,0},{2,1},{3,2},{4,3},{5,4},{6,5},{7,6},{8,7},{9,8},{10,9... | collective-permute-start | bytes 786440 | tf_op jit(solution)/shard_map/ppermute | solution.py:182
  62.1 11.5 %copy-start.3 = (bf16[128,896]{1,0:T(8,128)(2,1)}, bf16[128,896]{1,0:T(8,128)(2,1)S(1)}, u32[]{:S(2)}) copy-start(bf16[128,896]{1,0:T(8,128)(2,1)S(1)} %collective-permute-done.2) | copy-start | bytes 688132
  62.1 21.7 %collective-permute-start.6 = (bf16[2,128,512]{2,1,0:T(8,128)(2,1)S(1)}, bf16[2,128,512]{2,1,0:T(8,128)(2,1)}, u32[]{:S(2)}, u32[]{:S(2)}) collective-permute-start(bf16[2,128,512]{2,1,0:T(8,128)(2,1)S(1)} %get-tuple-element.18), channel_id=1, source_target_pairs={{0,1},{1,2},{2,3},{3,4},{4,5},{5,6},{6,7},{7,8},{8,9},{9,10},{10,1... | collective-permute-start | bytes 786440 | tf_op jit(solution)/shard_map/ppermute | solution.py:182
  71.7 2.0 %copy-start.4 = (bf16[128,896]{1,0:T(8,128)(2,1)}, bf16[128,896]{1,0:T(8,128)(2,1)S(1)}, u32[]{:S(2)}) copy-start(bf16[128,896]{1,0:T(8,128)(2,1)S(1)} %collective-permute-done.3) | copy-start | bytes 688132
  71.7 13.2 %collective-permute-start.4 = (bf16[2,128,512]{2,1,0:T(8,128)(2,1)S(1)}, bf16[2,128,512]{2,1,0:T(8,128)(2,1)S(1)}, u32[]{:S(2)}, u32[]{:S(2)}) collective-permute-start(bf16[2,128,512]{2,1,0:T(8,128)(2,1)S(1)} %get-tuple-element.17), channel_id=1, source_target_pairs={{0,32},{1,33},{2,34},{3,35},{4,36},{5,37},{6,38},{7,39},{8,40},{9,... | collective-permute-start | bytes 786440 | tf_op jit(solution)/shard_map/ppermute | solution.py:182
  73.6 0.7 copy-start.5
  75.6 19.0 %collective-permute-start.7 = (bf16[4,128,896]{2,1,0:T(8,128)(2,1)S(1)}, bf16[4,128,896]{2,1,0:T(8,128)(2,1)}, u32[]{:S(2)}, u32[]{:S(2)}) collective-permute-start(bf16[4,128,896]{2,1,0:T(8,128)(2,1)S(1)} %pad_maximum_fusion.1.own_ref), channel_id=1, source_target_pairs={{0,64},{64,0},{1,65},{65,1},{2,66},{66,2},{3,67},{67,3},{4,68},{68... | collective-permute-start | bytes 2752520 | tf_op jit(solution)/shard_map/ppermute | solution.py:182
  89.0 20.4 %all-to-all-start.2 = ((bf16[4,256,256]{2,1,0:T(8,128)(2,1)}), bf16[4,256,256]{2,1,0:T(8,128)(2,1)S(1)}, u32[]{:S(2)}, u32[]{:S(2)}) async-start(bf16[4,256,256]{2,1,0:T(8,128)(2,1)} %broadcast_in_dim.19), calls=%async_computation.2 | async-start | bytes 1048576 | tf_op jit(solution)/shard_map/all_to_all | solution.py:177
  126.7 21.1 %all-to-all-start.4 = ((f32[16,2,896]{2,1,0:T(2,128)}), f32[16,2,896]{2,1,0:T(2,128)S(1)}, u32[]{:S(2)}, u32[]{:S(2)}) async-start(f32[16,2,896]{2,1,0:T(2,128)} %reshape.56), calls=%async_computation.4 | async-start | bytes 229376 | tf_op jit(solution)/shard_map/all_to_all | solution.py:177

commit v4 on v3

--- a/solution.py
+++ b/solution.py
@@ -73,7 +73,41 @@
     )(length, queries, cache, fresh)
 
 
-def dispatch_kernel(yl_ref, tokens_ref, send_ref, mix_ref):
+def hbm():
+    return pl.BlockSpec(memory_space=pltpu.HBM)
+
+
+def pack_kernel(hidden_ref, routes_ref, logits_ref, out_ref, rows_ref, done):
+    width = hidden_ref.shape[3]
+    steps = hidden_ref.shape[0]
+    per_core = rows_ref.shape[0] // 4 // steps
+    for step in range(steps):
+        parts = (routes_ref[step, 0].astype(F32), logits_ref[step, 0].astype(F32))
+        tail = jnp.concatenate(parts, -1).astype(BF)
+        for peer in range(rows_ref.shape[0]):
+            if peer // per_core % steps == step:
+                rows_ref[peer, :, :width] = hidden_ref[step, 0]
+                rows_ref[peer, :, width:] = tail
+    copy = pltpu.make_async_copy(rows_ref, out_ref, done)
+    copy.start()
+    copy.wait()
+
+
+def pack(hidden, routes, logits, peers):
+    _, _, requests, width = hidden.shape
+    shape = (peers, requests, width + routes.shape[3] + logits.shape[3])
+    return pl.pallas_call(
+        pack_kernel,
+        out_shape=jax.ShapeDtypeStruct(shape, BF),
+        in_specs=vmem(3),
+        out_specs=hbm(),
+        scratch_shapes=[pltpu.VMEM(shape, BF), pltpu.SemaphoreType.DMA],
+        compiler_params=PARAMS,
+        name="pack",
+    )(hidden, routes, logits)
+
+
+def dispatch_kernel(yl_ref, tokens_ref, send_ref, mix_ref, held_ref, done):
     rows = tokens_ref.shape[0]
     slots, width = send_ref.shape
     tail = tokens_ref[:, width:].astype(F32)
@@ -94,10 +128,19 @@
     chosen = (named > 0) & (earlier == (slot % CAP).astype(F32))
     chosen = chosen & (slot % (2 * CAP) // CAP == iota((rows, slots), 0) // 2 % 2)
     pick = chosen.astype(F32).astype(BF)
-    send_ref[...] = dot(pick, tokens_ref[:, :width], ((0,), (0,))).astype(BF)
+    copies = []
+    for part in range(0, slots, 128):
+        span = slice(part, part + 128)
+        sent = dot(pick[:, span], tokens_ref[:, :width], ((0,), (0,)))
+        held_ref[span] = sent.astype(BF)
+        copy = pltpu.make_async_copy(held_ref.at[span], send_ref.at[span], done.at[part // 128])
+        copy.start()
+        copies.append(copy)
     high = gate.astype(BF).astype(F32)
     mix = [jnp.where(chosen, part, 0.0) for part in (high, gate - high)]
     mix_ref[...] = jnp.concatenate(mix, 0).astype(BF)
+    for copy in copies:
+        copy.wait()
 
 
 def dispatch(yl, tokens, slots, width):
@@ -108,28 +151,42 @@
             jax.ShapeDtypeStruct((2 * tokens.shape[0], slots), BF),
         ),
         in_specs=[pl.BlockSpec(memory_space=pltpu.SMEM), *vmem(1)],
-        out_specs=tuple(vmem(2)),
+        out_specs=(hbm(), *vmem(1)),
+        scratch_shapes=[
+            pltpu.VMEM((slots, width), BF),
+            pltpu.SemaphoreType.DMA((slots // 128,)),
+        ],
         compiler_params=PARAMS,
         name="dispatch",
     )(yl.reshape(1), tokens)
 
 
-def hidden_kernel(rows_ref, own_ref, peer_ref, out_ref):
+def hidden_kernel(rows_ref, own_ref, peer_ref, out_ref, held_ref, done):
     units = own_ref.shape[1] // 2
     rows = rows_ref[...]
     for place, ref in enumerate((own_ref, peer_ref)):
         both = dot(rows, ref[...])
         gate, up = both[:, :units], both[:, units:]
         value = gate / (1.0 + jnp.exp(-gate)) * up
-        out_ref[:, place * units : (place + 1) * units] = value.astype(BF)
-
-
-def hidden_units(rows, own, peer):
+        held_ref[:, place * units : (place + 1) * units] = value.astype(BF)
+    copies = [
+        pltpu.make_async_copy(held_ref, out_ref.at[peer], done.at[peer])
+        for peer in range(out_ref.shape[0])
+    ]
+    for copy in copies:
+        copy.start()
+    for copy in copies:
+        copy.wait()
+
+
+def hidden_units(rows, own, peer, peers):
+    shape = (rows.shape[0], own.shape[1])
     return pl.pallas_call(
         hidden_kernel,
-        out_shape=jax.ShapeDtypeStruct((rows.shape[0], own.shape[1]), BF),
+        out_shape=jax.ShapeDtypeStruct((peers, *shape), BF),
         in_specs=vmem(3),
-        out_specs=vmem(1)[0],
+        out_specs=hbm(),
+        scratch_shapes=[pltpu.VMEM(shape, BF), pltpu.SemaphoreType.DMA((peers,))],
         compiler_params=PARAMS,
         name="hidden_units",
     )(rows, own, peer)
@@ -156,18 +213,26 @@
     )(yh.reshape(1), h, own, peer)
 
 
-def combine_kernel(mix_ref, back_ref, out_ref):
-    rows = out_ref.shape[0]
+def combine_kernel(mix_ref, back_ref, out_ref, held_ref, done):
+    peers, requests, _ = out_ref.shape
+    rows = peers * requests
     value = dot(mix_ref[...], back_ref[...])
-    out_ref[...] = value[:rows] + value[rows:]
-
-
-def combine(mix, back):
+    value = (value[:rows] + value[rows:]).astype(BF)
+    for peer in range(peers):
+        held_ref[peer] = value[peer * requests : (peer + 1) * requests]
+    copy = pltpu.make_async_copy(held_ref, out_ref, done)
+    copy.start()
+    copy.wait()
+
+
+def combine(mix, back, requests):
+    shape = (mix.shape[0] // 2 // requests, requests, back.shape[1])
     return pl.pallas_call(
         combine_kernel,
-        out_shape=jax.ShapeDtypeStruct((mix.shape[0] // 2, back.shape[1]), F32),
+        out_shape=jax.ShapeDtypeStruct(shape, BF),
         in_specs=vmem(2),
-        out_specs=vmem(1)[0],
+        out_specs=hbm(),
+        scratch_shapes=[pltpu.VMEM(shape, BF), pltpu.SemaphoreType.DMA],
         compiler_params=PARAMS,
         name="combine",
     )(mix, back)
@@ -204,9 +269,8 @@
     block = yl_size * CAP
     slots = peers * block
 
-    packed = jnp.concatenate([hidden, routes.astype(BF), route_logits], -1)[:, 0]
-    packed = jnp.broadcast_to(packed[None, :, None], (yh_size, steps, yl_size, *packed.shape[1:]))
-    tokens = exchange(packed.reshape(-1, *packed.shape[3:]), COLUMN)
+    packed = pack(hidden, routes, route_logits, yh_size * steps * yl_size)
+    tokens = exchange(packed, COLUMN)
     served = attend(lengths[own_rank], queries, latent_cache, new_latent)
     tokens, served0, served1 = lax.optimization_barrier((tokens, *served))
     tokens = tokens.reshape(-1, tokens.shape[-1])
@@ -224,8 +288,12 @@
     peer_down = shifted(own_down, "c", 1)
 
     far = shifted(served0, EP, experts // 2)
+    arrived, peer_w, own_down, far = lax.optimization_barrier((arrived, peer_w, own_down, far))
+    h = hidden_units(arrived, own_w, peer_w, yh_size)
+    h, served1 = lax.optimization_barrier((h, served1))
     lower = shifted(served1, EP, 1)
     upper = shifted(served1, EP, -1)
+    h, lower, upper = lax.optimization_barrier((exchange(h, "yh"), lower, upper))
     home = new_home[own_rank]
     result0 = jnp.where(home[0] == own_rank, served0, far)
     result1 = jnp.where(
@@ -235,18 +303,12 @@
     )
     attended = jnp.stack([result0, result1], 1)[:, None]
 
-    arrived, peer_w, own_down, attended = lax.optimization_barrier(
-        (arrived, peer_w, own_down, attended)
-    )
-    h = hidden_units(arrived, own_w, peer_w)
-    h = exchange(jnp.broadcast_to(h[None], (yh_size, *h.shape)), "yh")
     out = down(yh, h, own_down, peer_down)
     back = exchange(out.reshape(peers, block, chunk), PLANE).reshape(slots, chunk)
-    mixed = combine(mix, back)
-    final = exchange(mixed.reshape(-1, requests, chunk), COLUMN)
-    final = final.reshape(yh_size, steps, yl_size, requests, chunk).sum(2).astype(BF)
-    moe_out = final.transpose(1, 2, 0, 3).reshape(steps, 1, requests, width)
-    return attended, moe_out
+    final = exchange(combine(mix, back, requests), COLUMN)
+    final = final.reshape(yh_size, steps, yl_size, requests, chunk).astype(F32)
+    final = final.sum(2).astype(BF).transpose(1, 2, 0, 3)
+    return attended, final.reshape(steps, 1, requests, width)
 
 
 def solution(mesh):

time: 150 us -> 152 us (1.013)
  blocking collectives: 14.4 us -> 0 us
  waiting for transfers between devices: 37 us -> 50.8 us
  starting transfers between devices: 67 us -> 71 us
  Pallas kernels: 8.65 us -> 12.3 us
  other arithmetic: 5.7 us -> 2.92 us
  local copies, waits for them, and re-layouts: 12.7 us -> 10.5 us
    all_to_all x1 -> x0, blocking collectives: 14.4 us -> none  [exchange(): return lax.all_to_all(x, axes, split_axis=0, concat_axis=0, tiled=True)]
    ppermute x8, waiting for transfers between devices: 10.9 us -> 24.9 us  [shifted(): return lax.ppermute(x, axes, [(i, (i + by) % size) for i in range(size)])]
    ppermute x8, starting transfers between devices: 26.9 us -> 32.5 us  [shifted(): return lax.ppermute(x, axes, [(i, (i + by) % size) for i in range(size)])]
    pallas_call x2 -> x3, Pallas kernels: 3.38 us -> 5.62 us  [the longest x1 4 us: hidden_units(): pl.pallas_call(hidden_kernel, out_shape=jax.ShapeDtypeStruct((peers, *sha...]
    unnamed x19 -> x27, local copies, waits for them, and re-layouts: 5.83 us -> 7.59 us
    broadcast_in_dim x2 -> x0, local copies, waits for them, and re-layouts: 1.64 us -> none  [the longest x1 0.83 us: shards(): h = exchange(jnp.broadcast_to(h[None], (yh_size, *h.shape)), 'yh')]
    all_to_all x4 -> x5, starting transfers between devices: 40.1 us -> 38.5 us  [exchange(): return lax.all_to_all(x, axes, split_axis=0, concat_axis=0, tiled=True)]
    all_to_all x4 -> x5, waiting for transfers between devices: 26.1 us -> 25.9 us  [exchange(): return lax.all_to_all(x, axes, split_axis=0, concat_axis=0, tiled=True)]
  transfers between devices with their start and end apart: 12 -> 13, of which waited for: 6 -> 8; matrix products, arithmetic and copies ran while one was open for 8% -> 5% of each run, Pallas kernels for 4% -> 4%
where the time goes in v4:
time: 152 us; the launch traced here: 151 us
  starting transfers between devices  71 us (47%)
  waiting for transfers between devices  50.8 us (33%)
  Pallas kernels  12.3 us (8%)
  local copies, waits for them, and re-layouts  10.5 us (7%)
  between operations  2.99 us (2%)
  other arithmetic  2.92 us (2%)
    all_to_all x5, starting transfers between devices, exchange(): return lax.all_to_all(x, axes, split_axis=0, concat_axis=0, tiled=True)  38.5 us
    ppermute x8, starting transfers between devices, shifted(): return lax.ppermute(x, axes, [(i, (i + by) % size) for i in range(size)])  32.5 us
    all_to_all x5, waiting for transfers between devices, exchange(): return lax.all_to_all(x, axes, split_axis=0, concat_axis=0, tiled=True)  25.9 us
    ppermute x8, waiting for transfers between devices, shifted(): return lax.ppermute(x, axes, [(i, (i + by) % size) for i in range(size)])  24.9 us
    unnamed x27, local copies, waits for them, and re-layouts  7.59 us
    pallas_call x1, Pallas kernels, hidden_units(): pl.pallas_call(hidden_kernel, out_shape=jax.ShapeDtypeStruct((peers, *sha...  4 us
  transfers between devices with their start and end apart: 13, of which 8 were waited for; matrix products, arithmetic and copies ran while one was open for 5% of the time, Pallas kernels for 4%

profile of v4, /device:TPU:1, one launch (start us, length us, event | category | flops | bytes accessed | tf_op | source)
XLA Modules:
  0.0 150.6 jit_solution(9122414558141403504)
XLA Ops:
  0.6 0.7 copy-done.1
  1.4 0.7 copy-done.3
  2.1 0.7 copy-done.4
  2.7 0.8 pack.1
  3.5 10.2 %all-to-all-start = ((bf16[16,2,3600]{2,1,0:T(2,128)(2,1)}), bf16[16,2,3600]{2,1,0:T(2,128)(2,1)S(1)}, u32[]{:S(2)}, u32[]{:S(2)}) async-start(bf16[16,2,3600]{2,1,0:T(2,128)(2,1)} %pack.1), calls=%async_computation | async-start | bytes 475136 | tf_op jit(solution)/shard_map/all_to_all | solution.py:242
  13.8 0.0 copy-start.11
  13.8 0.0 copy-start.2
  13.8 1.7 %copy.20.cache_ref = bf16[1,2,512,576]{3,2,1,0:T(8,128)(2,1)S(1)} copy(bf16[1,2,512,576]{2,3,1,0:T(8,128)(2,1)} %param.11) | data formatting | bytes 2359296 | tf_op args[0]
  15.5 0.3 copy.19.query_ref
  15.8 0.2 constant_dynamic-slice_fusion.2
  16.0 2.5 %attend.1 = (bf16[2,128,512]{2,1,0:T(8,128)(2,1)S(1)}, bf16[2,128,512]{2,1,0:T(8,128)(2,1)S(1)}) custom-call(s32[2]{0:T(128)S(1)} %get-tuple-element.47.len_ref, bf16[2,1,2,128,576]{4,3,2,1,0:T(8,128)(2,1)S(1)} %copy.19.query_ref, bf16[1,2,512,576]{3,2,1,0:T(8,128)(2,1)S(1)} %copy.20.cache_ref, bf16[2,1,2,576]{3,2,1,0:T(2,128)(2,1)S(1)} %copy-done.2), custom_call_target="tpu_custom_call" | custom-call | tf_op jit(solution)/shard_map/attend/pallas_call | solution.py:65
  18.5 5.0 %all-to-all-done = bf16[16,2,3600]{2,1,0:T(2,128)(2,1)S(1)} async-done(((bf16[16,2,3600]{2,1,0:T(2,128)(2,1)}), bf16[16,2,3600]{2,1,0:T(2,128)(2,1)S(1)}, u32[]{:S(2)}, u32[]{:S(2)}) %all-to-all-start) | async-done | bytes 230432 | tf_op jit(solution)/shard_map/all_to_all | solution.py:242
  23.5 0.2 reshape.41.tokens_ref
  23.7 1.6 %dispatch.1 = (bf16[256,3584]{1,0:T(8,128)(2,1)S(1)}, bf16[64,256]{1,0:T(8,128)(2,1)S(1)}) custom-call(s32[1]{0:T(128)} %bitcast.1.yl_ref, bf16[32,3600]{1,0:T(8,128)(2,1)S(1)} %reshape.41.tokens_ref), custom_call_target="tpu_custom_call" | custom-call | tf_op jit(solution)/shard_map/dispatch/pallas_call | solution.py:147
  25.3 1.2 copy-done
  26.5 11.3 %all-to-all-start.1 = ((bf16[32,8,3584]{2,1,0:T(8,128)(2,1)}), bf16[32,8,3584]{2,1,0:T(8,128)(2,1)S(1)}, u32[]{:S(2)}, u32[]{:S(2)}) async-start(bf16[32,8,3584]{2,1,0:T(8,128)(2,1)} %bitcast.30), calls=%async_computation.1 | async-start | bytes 3670016 | tf_op jit(solution)/shard_map/all_to_all | solution.py:242
  37.9 2.6 %pad_maximum_fusion.own_ref = bf16[3584,256]{1,0:T(8,128)(2,1)} fusion(bf16[3584,128]{1,0:T(8,128)(2,1)S(1)} %bitcast.32, bf16[3584,128]{1,0:T(8,128)(2,1)} %bitcast.33), kind=kLoop, calls=%fused_computation | loop fusion | flops 3670016 | bytes 3670016 | tf_op jit(solution)/shard_map/concatenate | solution.py:280
  40.4 2.6 %collective-permute-start = (bf16[3584,256]{1,0:T(8,128)(2,1)}, bf16[3584,256]{1,0:T(8,128)(2,1)}, u32[]{:S(2)}, u32[]{:S(2)}) collective-permute-start(bf16[3584,256]{1,0:T(8,128)(2,1)} %pad_maximum_fusion.own_ref), channel_id=1, source_target_pairs={{0,64},{64,0},{1,65},{65,1},{2,66},{66,2},{3,67},{67,3},{4,68},{68... | collective-permute-start | bytes 5505032 | tf_op jit(solution)/shard_map/ppermute | solution.py:247
  43.1 1.4 constant_dynamic-slice_fusion
  44.5 3.6 %collective-permute-start.3 = (bf16[128,896]{1,0:T(8,128)(2,1)S(1)}, bf16[128,896]{1,0:T(8,128)(2,1)S(1)}, u32[]{:S(2)}, u32[]{:S(2)}) collective-permute-start(bf16[128,896]{1,0:T(8,128)(2,1)S(1)} %get-tuple-element.42), channel_id=1, source_target_pairs={{0,384},{128,0},{256,128},{384,256},{1,385},{129,1},{257,129},{385... | collective-permute-start | bytes 688136 | tf_op jit(solution)/shard_map/ppermute | solution.py:247
  48.1 2.6 %collective-permute-start.1 = (bf16[128,896]{1,0:T(8,128)(2,1)S(1)}, bf16[128,896]{1,0:T(8,128)(2,1)S(1)}, u32[]{:S(2)}, u32[]{:S(2)}) collective-permute-start(bf16[128,896]{1,0:T(8,128)(2,1)S(1)} %get-tuple-element.41), channel_id=1, source_target_pairs={{0,128},{128,256},{256,384},{384,0},{1,129},{129,257},{257,385},{3... | collective-permute-start | bytes 688136 | tf_op jit(solution)/shard_map/ppermute | solution.py:247
  50.7 4.6 %collective-permute-start.2 = (bf16[128,896]{1,0:T(8,128)(2,1)S(1)}, bf16[128,896]{1,0:T(8,128)(2,1)S(1)}, u32[]{:S(2)}, u32[]{:S(2)}) collective-permute-start(bf16[128,896]{1,0:T(8,128)(2,1)S(1)} %get-tuple-element.43), channel_id=1, source_target_pairs={{0,256},{128,384},{256,0},{384,128},{1,257},{129,385},{257,1},{385... | collective-permute-start | bytes 688136 | tf_op jit(solution)/shard_map/ppermute | solution.py:247
  55.3 2.7 %collective-permute-start.4 = (bf16[2,128,512]{2,1,0:T(8,128)(2,1)S(1)}, bf16[2,128,512]{2,1,0:T(8,128)(2,1)S(1)}, u32[]{:S(2)}, u32[]{:S(2)}) collective-permute-start(bf16[2,128,512]{2,1,0:T(8,128)(2,1)S(1)} %get-tuple-element.20), channel_id=1, source_target_pairs={{0,32},{1,33},{2,34},{3,35},{4,36},{5,37},{6,38},{7,39},{8,40},{9,... | collective-permute-start | bytes 786440 | tf_op jit(solution)/shard_map/ppermute | solution.py:247
  58.0 1.4 collective-permute-done.3
  59.5 0.0 collective-permute-done.1
  59.5 5.4 %collective-permute-done.2 = bf16[128,896]{1,0:T(8,128)(2,1)S(1)} collective-permute-done((bf16[128,896]{1,0:T(8,128)(2,1)S(1)}, bf16[128,896]{1,0:T(8,128)(2,1)S(1)}, u32[]{:S(2)}, u32[]{:S(2)}) %collective-permute-start.2) | collective-permute-done | bytes 229408 | tf_op jit(solution)/shard_map/ppermute | solution.py:247
  64.8 0.1 pad_maximum_fusion.1.own_ref
  65.0 6.9 %collective-permute-start.7 = (bf16[4,128,896]{2,1,0:T(8,128)(2,1)S(1)}, bf16[4,128,896]{2,1,0:T(8,128)(2,1)}, u32[]{:S(2)}, u32[]{:S(2)}) collective-permute-start(bf16[4,128,896]{2,1,0:T(8,128)(2,1)S(1)} %pad_maximum_fusion.1.own_ref), channel_id=1, source_target_pairs={{0,64},{64,0},{1,65},{65,1},{2,66},{66,2},{3,67},{67,3},{4,68},{68... | collective-permute-start | bytes 2752520 | tf_op jit(solution)/shard_map/ppermute | solution.py:247
  71.9 4.2 %collective-permute-done.4 = bf16[2,128,512]{2,1,0:T(8,128)(2,1)S(1)} collective-permute-done((bf16[2,128,512]{2,1,0:T(8,128)(2,1)S(1)}, bf16[2,128,512]{2,1,0:T(8,128)(2,1)S(1)}, u32[]{:S(2)}, u32[]{:S(2)}) %collective-permute-start.4) | collective-permute-done | bytes 262176 | tf_op jit(solution)/shard_map/ppermute | solution.py:247
  76.1 0.7 copy-done.9
  76.8 4.1 %all-to-all-done.1 = bf16[32,8,3584]{2,1,0:T(8,128)(2,1)S(1)} async-done(((bf16[32,8,3584]{2,1,0:T(8,128)(2,1)}), bf16[32,8,3584]{2,1,0:T(8,128)(2,1)S(1)}, u32[]{:S(2)}, u32[]{:S(2)}) %all-to-all-start.1) | async-done | bytes 1835040 | tf_op jit(solution)/shard_map/all_to_all | solution.py:242
  80.9 4.0 %hidden_units.1 = bf16[4,256,256]{2,1,0:T(8,128)(2,1)} custom-call(bf16[256,3584]{1,0:T(8,128)(2,1)S(1)} %bitcast.29, bf16[3584,256]{1,0:T(8,128)(2,1)} %pad_maximum_fusion.own_ref, bf16[3584,256]{1,0:T(8,128)(2,1)} %collective-permute-done.peer_ref), custom_call_target="tpu_custom_call" | custom-call | tf_op jit(solution)/shard_map/hidden_units/pallas_call | solution.py:184
  84.9 3.7 %all-to-all-start.2 = ((bf16[4,256,256]{2,1,0:T(8,128)(2,1)}), bf16[4,256,256]{2,1,0:T(8,128)(2,1)S(1)}, u32[]{:S(2)}, u32[]{:S(2)}) async-start(bf16[4,256,256]{2,1,0:T(8,128)(2,1)} %hidden_units.1), calls=%async_computation.2 | async-start | bytes 1048576 | tf_op jit(solution)/shard_map/all_to_all | solution.py:242
  88.6 4.5 %collective-permute-start.5 = (bf16[2,128,512]{2,1,0:T(8,128)(2,1)S(1)}, bf16[2,128,512]{2,1,0:T(8,128)(2,1)S(1)}, u32[]{:S(2)}, u32[]{:S(2)}) collective-permute-start(bf16[2,128,512]{2,1,0:T(8,128)(2,1)S(1)} %get-tuple-element.27), channel_id=1, source_target_pairs={{0,1},{1,2},{2,3},{3,4},{4,5},{5,6},{6,7},{7,8},{8,9},{9,10},{10,1... | collective-permute-start | bytes 786440 | tf_op jit(solution)/shard_map/ppermute | solution.py:247
  93.1 5.1 %collective-permute-start.6 = (bf16[2,128,512]{2,1,0:T(8,128)(2,1)S(1)}, bf16[2,128,512]{2,1,0:T(8,128)(2,1)S(1)}, u32[]{:S(2)}, u32[]{:S(2)}) collective-permute-start(bf16[2,128,512]{2,1,0:T(8,128)(2,1)S(1)} %get-tuple-element.27), channel_id=1, source_target_pairs={{0,63},{1,0},{2,1},{3,2},{4,3},{5,4},{6,5},{7,6},{8,7},{9,8},{10,9... | collective-permute-start | bytes 786440 | tf_op jit(solution)/shard_map/ppermute | solution.py:247
  98.2 13.9 %collective-permute-done.5 = bf16[2,128,512]{2,1,0:T(8,128)(2,1)S(1)} collective-permute-done((bf16[2,128,512]{2,1,0:T(8,128)(2,1)S(1)}, bf16[2,128,512]{2,1,0:T(8,128)(2,1)S(1)}, u32[]{:S(2)}, u32[]{:S(2)}) %collective-permute-start.5) | collective-permute-done | bytes 262176 | tf_op jit(solution)/shard_map/ppermute | solution.py:247
  112.1 0.7 copy-done.7
  112.7 2.7 %down.1 = bf16[256,896]{1,0:T(8,128)(2,1)} custom-call(s32[1]{0:T(128)} %bitcast.16.yh_ref, bf16[4,256,256]{2,1,0:T(8,128)(2,1)S(1)} %all-to-all-done.2.h_ref, bf16[4,128,896]{2,1,0:T(8,128)(2,1)S(1)} %pad_maximum_fusion.1.own_ref, bf16[4,128,896]{2,1,0:T(8,128)(2,1)} %collective-permute-done.7.peer_ref), custom_call_target="tpu_custom_call" | custom-call | tf_op jit(solution)/shard_map/down/pallas_call | solution.py:206
  115.4 4.0 %all-to-all-start.3 = ((bf16[32,8,896]{2,1,0:T(8,128)(2,1)}), bf16[32,8,896]{2,1,0:T(8,128)(2,1)S(1)}, u32[]{:S(2)}, u32[]{:S(2)}) async-start(bf16[32,8,896]{2,1,0:T(8,128)(2,1)} %bitcast.17), calls=%async_computation.3 | async-start | bytes 917504 | tf_op jit(solution)/shard_map/all_to_all | solution.py:242
  119.4 0.6 fusion.1
  122.1 10.1 %all-to-all-done.3 = bf16[32,8,896]{2,1,0:T(8,128)(2,1)S(1)} async-done(((bf16[32,8,896]{2,1,0:T(8,128)(2,1)}), bf16[32,8,896]{2,1,0:T(8,128)(2,1)S(1)}, u32[]{:S(2)}, u32[]{:S(2)}) %all-to-all-start.3) | async-done | bytes 458784 | tf_op jit(solution)/shard_map/all_to_all | solution.py:242
  132.3 0.8 combine.1
  133.1 9.2 %all-to-all-start.4 = ((bf16[16,2,896]{2,1,0:T(2,128)(2,1)}), bf16[16,2,896]{2,1,0:T(2,128)(2,1)S(1)}, u32[]{:S(2)}, u32[]{:S(2)}) async-start(bf16[16,2,896]{2,1,0:T(2,128)(2,1)} %combine.1), calls=%async_computation.4 | async-start | bytes 114688 | tf_op jit(solution)/shard_map/all_to_all | solution.py:242
  142.4 0.1 maximum_bitcast_fusion
  142.4 0.8 copy.22
  143.2 6.7 %all-to-all-done.4 = bf16[16,2,896]{2,1,0:T(2,128)(2,1)S(1)} async-done(((bf16[16,2,896]{2,1,0:T(2,128)(2,1)}), bf16[16,2,896]{2,1,0:T(2,128)(2,1)S(1)}, u32[]{:S(2)}, u32[]{:S(2)}) %all-to-all-start.4) | async-done | bytes 57376 | tf_op jit(solution)/shard_map/all_to_all | solution.py:242
  149.9 0.1 bitcast_reduce_fusion
  150.0 0.6 reshape.48
  (23 shorter events, 0.1 us)
Async XLA Ops:
  0.6 0.7 copy-start.1
  1.4 0.7 copy-start.3
  2.1 0.7 copy-start.4
  2.7 12.7 %copy-start.6 = (bf16[2,1,2,128,576]{3,4,2,1,0:T(8,128)(2,1)S(1)}, bf16[2,1,2,128,576]{3,4,2,1,0:T(8,128)(2,1)}, u32[]{:S(2)}) copy-start(bf16[2,1,2,128,576]{3,4,2,1,0:T(8,128)(2,1)} %param.14) | copy-start | bytes 1769476
  3.5 19.9 %all-to-all-start = ((bf16[16,2,3600]{2,1,0:T(2,128)(2,1)}), bf16[16,2,3600]{2,1,0:T(2,128)(2,1)S(1)}, u32[]{:S(2)}, u32[]{:S(2)}) async-start(bf16[16,2,3600]{2,1,0:T(2,128)(2,1)} %pack.1), calls=%async_computation | async-start | bytes 475136 | tf_op jit(solution)/shard_map/all_to_all | solution.py:242
  13.7 2.1 %copy-start.10 = (s32[64,2]{0,1:T(2,128)S(1)}, s32[64,2]{0,1:T(2,128)}, u32[]{:S(2)}) copy-start(s32[64,2]{0,1:T(2,128)} %param.13) | copy-start | bytes 1540
  13.8 2.1 %copy-start.11 = (s32[64,2]{0,1:T(2,128)S(1)}, s32[64,2]{0,1:T(2,128)}, u32[]{:S(2)}) copy-start(s32[64,2]{0,1:T(2,128)} %param.12) | copy-start | bytes 1540
  13.8 2.2 %copy-start.2 = (bf16[2,1,2,576]{3,2,1,0:T(2,128)(2,1)S(1)}, bf16[2,1,2,576]{3,2,1,0:T(2,128)(2,1)}, u32[]{:S(2)}) copy-start(bf16[2,1,2,576]{3,2,1,0:T(2,128)(2,1)} %fresh_ref.1) | copy-start | bytes 13828
  25.2 1.2 copy-start
  26.5 11.3 %copy-start.5 = (bf16[1,3584,128]{2,1,0:T(8,128)(2,1)S(1)}, bf16[1,3584,128]{2,1,0:T(8,128)(2,1)}, u32[]{:S(2)}) copy-start(bf16[1,3584,128]{2,1,0:T(8,128)(2,1)} %param.20) | copy-start | bytes 2752516
  26.5 54.4 %all-to-all-start.1 = ((bf16[32,8,3584]{2,1,0:T(8,128)(2,1)}), bf16[32,8,3584]{2,1,0:T(8,128)(2,1)S(1)}, u32[]{:S(2)}, u32[]{:S(2)}) async-start(bf16[32,8,3584]{2,1,0:T(8,128)(2,1)} %bitcast.30), calls=%async_computation.1 | async-start | bytes 3670016 | tf_op jit(solution)/shard_map/all_to_all | solution.py:242
  40.4 36.4 %collective-permute-start = (bf16[3584,256]{1,0:T(8,128)(2,1)}, bf16[3584,256]{1,0:T(8,128)(2,1)}, u32[]{:S(2)}, u32[]{:S(2)}) collective-permute-start(bf16[3584,256]{1,0:T(8,128)(2,1)} %pad_maximum_fusion.own_ref), channel_id=1, source_target_pairs={{0,64},{64,0},{1,65},{65,1},{2,66},{66,2},{3,67},{67,3},{4,68},{68... | collective-permute-start | bytes 5505032 | tf_op jit(solution)/shard_map/ppermute | solution.py:247
  44.5 15.0 %collective-permute-start.3 = (bf16[128,896]{1,0:T(8,128)(2,1)S(1)}, bf16[128,896]{1,0:T(8,128)(2,1)S(1)}, u32[]{:S(2)}, u32[]{:S(2)}) collective-permute-start(bf16[128,896]{1,0:T(8,128)(2,1)S(1)} %get-tuple-element.42), channel_id=1, source_target_pairs={{0,384},{128,0},{256,128},{384,256},{1,385},{129,1},{257,129},{385... | collective-permute-start | bytes 688136 | tf_op jit(solution)/shard_map/ppermute | solution.py:247
  48.1 11.4 %collective-permute-start.1 = (bf16[128,896]{1,0:T(8,128)(2,1)S(1)}, bf16[128,896]{1,0:T(8,128)(2,1)S(1)}, u32[]{:S(2)}, u32[]{:S(2)}) collective-permute-start(bf16[128,896]{1,0:T(8,128)(2,1)S(1)} %get-tuple-element.41), channel_id=1, source_target_pairs={{0,128},{128,256},{256,384},{384,0},{1,129},{129,257},{257,385},{3... | collective-permute-start | bytes 688136 | tf_op jit(solution)/shard_map/ppermute | solution.py:247
  50.7 14.2 %collective-permute-start.2 = (bf16[128,896]{1,0:T(8,128)(2,1)S(1)}, bf16[128,896]{1,0:T(8,128)(2,1)S(1)}, u32[]{:S(2)}, u32[]{:S(2)}) collective-permute-start(bf16[128,896]{1,0:T(8,128)(2,1)S(1)} %get-tuple-element.43), channel_id=1, source_target_pairs={{0,256},{128,384},{256,0},{384,128},{1,257},{129,385},{257,1},{385... | collective-permute-start | bytes 688136 | tf_op jit(solution)/shard_map/ppermute | solution.py:247
  55.3 20.8 %collective-permute-start.4 = (bf16[2,128,512]{2,1,0:T(8,128)(2,1)S(1)}, bf16[2,128,512]{2,1,0:T(8,128)(2,1)S(1)}, u32[]{:S(2)}, u32[]{:S(2)}) collective-permute-start(bf16[2,128,512]{2,1,0:T(8,128)(2,1)S(1)} %get-tuple-element.20), channel_id=1, source_target_pairs={{0,32},{1,33},{2,34},{3,35},{4,36},{5,37},{6,38},{7,39},{8,40},{9,... | collective-permute-start | bytes 786440 | tf_op jit(solution)/shard_map/ppermute | solution.py:247
  65.0 47.1 %collective-permute-start.7 = (bf16[4,128,896]{2,1,0:T(8,128)(2,1)S(1)}, bf16[4,128,896]{2,1,0:T(8,128)(2,1)}, u32[]{:S(2)}, u32[]{:S(2)}) collective-permute-start(bf16[4,128,896]{2,1,0:T(8,128)(2,1)S(1)} %pad_maximum_fusion.1.own_ref), channel_id=1, source_target_pairs={{0,64},{64,0},{1,65},{65,1},{2,66},{66,2},{3,67},{67,3},{4,68},{68... | collective-permute-start | bytes 2752520 | tf_op jit(solution)/shard_map/ppermute | solution.py:247
  76.1 0.7 copy-start.9
  84.9 27.1 %all-to-all-start.2 = ((bf16[4,256,256]{2,1,0:T(8,128)(2,1)}), bf16[4,256,256]{2,1,0:T(8,128)(2,1)S(1)}, u32[]{:S(2)}, u32[]{:S(2)}) async-start(bf16[4,256,256]{2,1,0:T(8,128)(2,1)} %hidden_units.1), calls=%async_computation.2 | async-start | bytes 1048576 | tf_op jit(solution)/shard_map/all_to_all | solution.py:242
  88.6 23.4 %collective-permute-start.5 = (bf16[2,128,512]{2,1,0:T(8,128)(2,1)S(1)}, bf16[2,128,512]{2,1,0:T(8,128)(2,1)S(1)}, u32[]{:S(2)}, u32[]{:S(2)}) collective-permute-start(bf16[2,128,512]{2,1,0:T(8,128)(2,1)S(1)} %get-tuple-element.27), channel_id=1, source_target_pairs={{0,1},{1,2},{2,3},{3,4},{4,5},{5,6},{6,7},{7,8},{8,9},{9,10},{10,1... | collective-permute-start | bytes 786440 | tf_op jit(solution)/shard_map/ppermute | solution.py:247
  93.1 19.0 %collective-permute-start.6 = (bf16[2,128,512]{2,1,0:T(8,128)(2,1)S(1)}, bf16[2,128,512]{2,1,0:T(8,128)(2,1)S(1)}, u32[]{:S(2)}, u32[]{:S(2)}) collective-permute-start(bf16[2,128,512]{2,1,0:T(8,128)(2,1)S(1)} %get-tuple-element.27), channel_id=1, source_target_pairs={{0,63},{1,0},{2,1},{3,2},{4,3},{5,4},{6,5},{7,6},{8,7},{9,8},{10,9... | collective-permute-start | bytes 786440 | tf_op jit(solution)/shard_map/ppermute | solution.py:247
  112.0 0.7 copy-start.7
  115.4 6.7 %copy-start.8 = (bf16[2,128,512]{2,1,0:T(8,128)(2,1)S(1)}, bf16[2,128,512]{2,1,0:T(8,128)(2,1)}, u32[]{:S(2)}) copy-start(bf16[2,128,512]{2,1,0:T(8,128)(2,1)} %copy-done.7) | copy-start | bytes 786436
  115.4 16.9 %all-to-all-start.3 = ((bf16[32,8,896]{2,1,0:T(8,128)(2,1)}), bf16[32,8,896]{2,1,0:T(8,128)(2,1)S(1)}, u32[]{:S(2)}, u32[]{:S(2)}) async-start(bf16[32,8,896]{2,1,0:T(8,128)(2,1)} %bitcast.17), calls=%async_computation.3 | async-start | bytes 917504 | tf_op jit(solution)/shard_map/all_to_all | solution.py:242
  133.1 16.8 %all-to-all-start.4 = ((bf16[16,2,896]{2,1,0:T(2,128)(2,1)}), bf16[16,2,896]{2,1,0:T(2,128)(2,1)S(1)}, u32[]{:S(2)}, u32[]{:S(2)}) async-start(bf16[16,2,896]{2,1,0:T(2,128)(2,1)} %combine.1), calls=%async_computation.4 | async-start | bytes 114688 | tf_op jit(solution)/shard_map/all_to_all | solution.py:242

commit v5 on v4

--- a/solution.py
+++ b/solution.py
@@ -13,8 +13,8 @@
 CAP = 4
 EP = ("yl", "x", "z")
 DP = ("yh", "c")
-COLUMN = ("yh", "c", "yl")
-PLANE = ("x", "z")
+LINE = ("yh", "c", "z")
+PLANE = ("yl", "x")
 BF = jnp.bfloat16
 F32 = jnp.float32
 PARAMS = pltpu.CompilerParams(vmem_limit_bytes=48 * 1024 * 1024)
@@ -77,56 +77,73 @@
     return pl.BlockSpec(memory_space=pltpu.HBM)
 
 
-def pack_kernel(hidden_ref, routes_ref, logits_ref, out_ref, rows_ref, done):
-    width = hidden_ref.shape[3]
-    steps = hidden_ref.shape[0]
-    per_core = rows_ref.shape[0] // 4 // steps
+def pack_kernel(inner, hidden_ref, routes_ref, logits_ref, out_ref, *scratch):
+    hidden_now, routes_now, logits_now, rows_ref, done = scratch
+    pairs = ((hidden_ref, hidden_now), (routes_ref, routes_now), (logits_ref, logits_now))
+    loads = [
+        pltpu.make_async_copy(source, target, done.at[number])
+        for number, (source, target) in enumerate(pairs)
+    ]
+    for load in loads:
+        load.start()
+    for load in loads:
+        load.wait()
+    steps, _, _, width = hidden_ref.shape
     for step in range(steps):
-        parts = (routes_ref[step, 0].astype(F32), logits_ref[step, 0].astype(F32))
+        parts = (routes_now[step, 0].astype(F32), logits_now[step, 0].astype(F32))
         tail = jnp.concatenate(parts, -1).astype(BF)
-        for peer in range(rows_ref.shape[0]):
-            if peer // per_core % steps == step:
-                rows_ref[peer, :, :width] = hidden_ref[step, 0]
-                rows_ref[peer, :, width:] = tail
-    copy = pltpu.make_async_copy(rows_ref, out_ref, done)
-    copy.start()
-    copy.wait()
-
-
-def pack(hidden, routes, logits, peers):
-    _, _, requests, width = hidden.shape
-    shape = (peers, requests, width + routes.shape[3] + logits.shape[3])
-    return pl.pallas_call(
-        pack_kernel,
-        out_shape=jax.ShapeDtypeStruct(shape, BF),
-        in_specs=vmem(3),
+        for place in range(inner):
+            rows_ref[step * inner + place, :, :width] = hidden_now[step, 0]
+            rows_ref[step * inner + place, :, width:] = tail
+    size = steps * inner
+    stores = [
+        pltpu.make_async_copy(rows_ref, out_ref.at[pl.ds(first, size)], done.at[first // size])
+        for first in range(0, out_ref.shape[0], size)
+    ]
+    for store in stores:
+        store.start()
+    for store in stores:
+        store.wait()
+
+
+def pack(hidden, routes, logits, outer, inner):
+    steps, _, requests, width = hidden.shape
+    block = (requests, width + routes.shape[3] + logits.shape[3])
+    return pl.pallas_call(
+        functools.partial(pack_kernel, inner),
+        out_shape=jax.ShapeDtypeStruct((outer * steps * inner, *block), BF),
+        in_specs=[hbm()] * 3,
         out_specs=hbm(),
-        scratch_shapes=[pltpu.VMEM(shape, BF), pltpu.SemaphoreType.DMA],
+        scratch_shapes=[
+            pltpu.VMEM(hidden.shape, BF),
+            pltpu.VMEM(routes.shape, routes.dtype),
+            pltpu.VMEM(logits.shape, BF),
+            pltpu.VMEM((steps * inner, *block), BF),
+            pltpu.SemaphoreType.DMA((max(outer, 3),)),
+        ],
         compiler_params=PARAMS,
         name="pack",
     )(hidden, routes, logits)
 
 
-def dispatch_kernel(yl_ref, tokens_ref, send_ref, mix_ref, held_ref, done):
-    rows = tokens_ref.shape[0]
-    slots, width = send_ref.shape
-    tail = tokens_ref[:, width:].astype(F32)
-    top = tail.shape[1] // 2
-    sigmoid = jax.nn.sigmoid(tail[:, top:])
-    gates = 2.5 * sigmoid / jnp.sum(sigmoid, 1, keepdims=True)
+def chosen_slots(z, line, tail, slots):
+    rows, top = tail.shape
     slot = iota((rows, slots), 1)
-    expert = (slot // (2 * CAP) + yl_ref[0] * (slots // (2 * CAP))).astype(F32)
+    expert = (slot // (CAP * line) * line + z).astype(F32)
     named = jnp.zeros((rows, slots), F32)
-    gate = jnp.zeros((rows, slots), F32)
     for k in range(top):
-        hit = tail[:, k : k + 1] == expert
-        named = jnp.where(hit, 1.0, named)
-        gate = jnp.where(hit, gates[:, k : k + 1], gate)
+        named = jnp.where(tail[:, k : k + 1] == expert, 1.0, named)
     this, other = iota((rows, rows), 0), iota((rows, rows), 1)
-    before = ((other < this) & (other // 2 % 2 == this // 2 % 2)).astype(F32)
+    before = ((other < this) & (other // 2 % line == this // 2 % line)).astype(F32)
     earlier = dot(before.astype(BF), named.astype(BF))
     chosen = (named > 0) & (earlier == (slot % CAP).astype(F32))
-    chosen = chosen & (slot % (2 * CAP) // CAP == iota((rows, slots), 0) // 2 % 2)
+    return chosen & (slot // CAP % line == iota((rows, slots), 0) // 2 % line), expert
+
+
+def dispatch_kernel(line, top, z_ref, tokens_ref, send_ref, held_ref, done):
+    slots, width = send_ref.shape
+    tail = tokens_ref[:, width : width + top].astype(F32)
+    chosen, _ = chosen_slots(z_ref[0], line, tail, slots)
     pick = chosen.astype(F32).astype(BF)
     copies = []
     for part in range(0, slots, 128):
@@ -136,45 +153,65 @@
         copy = pltpu.make_async_copy(held_ref.at[span], send_ref.at[span], done.at[part // 128])
         copy.start()
         copies.append(copy)
-    high = gate.astype(BF).astype(F32)
-    mix = [jnp.where(chosen, part, 0.0) for part in (high, gate - high)]
-    mix_ref[...] = jnp.concatenate(mix, 0).astype(BF)
     for copy in copies:
         copy.wait()
 
 
-def dispatch(yl, tokens, slots, width):
-    return pl.pallas_call(
-        dispatch_kernel,
-        out_shape=(
-            jax.ShapeDtypeStruct((slots, width), BF),
-            jax.ShapeDtypeStruct((2 * tokens.shape[0], slots), BF),
-        ),
+def dispatch(z, line, top, tokens, slots, width):
+    return pl.pallas_call(
+        functools.partial(dispatch_kernel, line, top),
+        out_shape=jax.ShapeDtypeStruct((slots, width), BF),
         in_specs=[pl.BlockSpec(memory_space=pltpu.SMEM), *vmem(1)],
-        out_specs=(hbm(), *vmem(1)),
+        out_specs=hbm(),
         scratch_shapes=[
             pltpu.VMEM((slots, width), BF),
             pltpu.SemaphoreType.DMA((slots // 128,)),
         ],
         compiler_params=PARAMS,
         name="dispatch",
-    )(yl.reshape(1), tokens)
+    )(z, tokens)
+
+
+def mix_kernel(line, z_ref, tail_ref, mix_ref):
+    slots = mix_ref.shape[1]
+    tail = tail_ref[...].astype(F32)
+    top = tail.shape[1] // 2
+    sigmoid = jax.nn.sigmoid(tail[:, top:])
+    gates = 2.5 * sigmoid / jnp.sum(sigmoid, 1, keepdims=True)
+    chosen, expert = chosen_slots(z_ref[0], line, tail[:, :top], slots)
+    gate = jnp.zeros(chosen.shape, F32)
+    for k in range(top):
+        gate = jnp.where(tail[:, k : k + 1] == expert, gates[:, k : k + 1], gate)
+    high = gate.astype(BF).astype(F32)
+    mix = [jnp.where(chosen, part, 0.0) for part in (high, gate - high)]
+    mix_ref[...] = jnp.concatenate(mix, 0).astype(BF)
+
+
+def mixing(z, line, tail, slots):
+    return pl.pallas_call(
+        functools.partial(mix_kernel, line),
+        out_shape=jax.ShapeDtypeStruct((2 * tail.shape[0], slots), BF),
+        in_specs=[pl.BlockSpec(memory_space=pltpu.SMEM), *vmem(1)],
+        out_specs=vmem(1)[0],
+        compiler_params=PARAMS,
+        name="mixing",
+    )(z, tail)
 
 
 def hidden_kernel(rows_ref, own_ref, peer_ref, out_ref, held_ref, done):
     units = own_ref.shape[1] // 2
     rows = rows_ref[...]
+    copies = []
     for place, ref in enumerate((own_ref, peer_ref)):
         both = dot(rows, ref[...])
         gate, up = both[:, :units], both[:, units:]
         value = gate / (1.0 + jnp.exp(-gate)) * up
-        held_ref[:, place * units : (place + 1) * units] = value.astype(BF)
-    copies = [
-        pltpu.make_async_copy(held_ref, out_ref.at[peer], done.at[peer])
-        for peer in range(out_ref.shape[0])
-    ]
-    for copy in copies:
-        copy.start()
+        held_ref[place] = value.astype(BF)
+        for peer in range(out_ref.shape[0]):
+            target = out_ref.at[peer, :, pl.ds(place * units, units)]
+            copy = pltpu.make_async_copy(held_ref.at[place], target, done.at[place, peer])
+            copy.start()
+            copies.append(copy)
     for copy in copies:
         copy.wait()
 
@@ -186,7 +223,10 @@
         out_shape=jax.ShapeDtypeStruct((peers, *shape), BF),
         in_specs=vmem(3),
         out_specs=hbm(),
-        scratch_shapes=[pltpu.VMEM(shape, BF), pltpu.SemaphoreType.DMA((peers,))],
+        scratch_shapes=[
+            pltpu.VMEM((2, shape[0], shape[1] // 2), BF),
+            pltpu.SemaphoreType.DMA((2, peers)),
+        ],
         compiler_params=PARAMS,
         name="hidden_units",
     )(rows, own, peer)
@@ -261,39 +301,44 @@
     w_down,
 ):
     experts = lax.axis_size(EP)
-    yh_size, yl_size = lax.axis_size("yh"), lax.axis_size("yl")
-    peers = experts // yl_size
+    yh_size, line = lax.axis_size("yh"), lax.axis_size("z")
+    peers = experts // line
     own_rank = lax.axis_index(EP)
+    yh, z = lax.axis_index("yh"), lax.axis_index("z").reshape(1)
     steps, _, requests, width = hidden.shape
+    top = routes.shape[3]
     chunk = width // yh_size
-    block = yl_size * CAP
-    slots = peers * block
-
-    packed = pack(hidden, routes, route_logits, yh_size * steps * yl_size)
-    tokens = exchange(packed, COLUMN)
+    slots = experts * CAP
+
+    packed = pack(hidden, routes, route_logits, yh_size, line)
+    tokens = exchange(packed, LINE)
     served = attend(lengths[own_rank], queries, latent_cache, new_latent)
-    tokens, served0, served1 = lax.optimization_barrier((tokens, *served))
-    tokens = tokens.reshape(-1, tokens.shape[-1])
-    send, mix = dispatch(lax.axis_index("yl"), tokens, slots, width)
-    arrived = exchange(send.reshape(peers, block, width), PLANE).reshape(slots, width)
-
+    served, w_gate, w_up = lax.optimization_barrier((served, w_gate, w_up))
     own_w = jnp.concatenate([w_gate[0], w_up[0]], 1)
     peer_w = shifted(own_w, "c", 1)
-    yh = lax.axis_index("yh")
     sent = [
         lax.dynamic_slice_in_dim(w_down[0], (yh + s) % yh_size * chunk, chunk, 1)
         for s in range(yh_size)
     ]
-    own_down = jnp.stack([shifted(x, "yh", s) if s else x for s, x in enumerate(sent)])
+    moved = [shifted(x, "yh", s) if s in (1, yh_size - 1) else x for s, x in enumerate(sent)]
+    tokens, peer_w, served0, served1, *moved = lax.optimization_barrier(
+        (tokens, peer_w, *served, *moved)
+    )
+    tokens = tokens.reshape(-1, tokens.shape[-1])
+    send = dispatch(z, line, top, tokens, slots, width)
+    arrived = exchange(send.reshape(peers, -1, width), PLANE).reshape(slots, width)
+    mix = mixing(z, line, tokens[:, width:], slots)
+    moved = [shifted(x, "yh", s) if 1 < s < yh_size - 1 else x for s, x in enumerate(moved)]
+    own_down = jnp.stack(moved)
     peer_down = shifted(own_down, "c", 1)
 
     far = shifted(served0, EP, experts // 2)
-    arrived, peer_w, own_down, far = lax.optimization_barrier((arrived, peer_w, own_down, far))
+    arrived, peer_w, far, mix = lax.optimization_barrier((arrived, peer_w, far, mix))
     h = hidden_units(arrived, own_w, peer_w, yh_size)
-    h, served1 = lax.optimization_barrier((h, served1))
+    h, own_down = lax.optimization_barrier((h, own_down))
+    h, served1 = lax.optimization_barrier((exchange(h, "yh"), served1))
     lower = shifted(served1, EP, 1)
     upper = shifted(served1, EP, -1)
-    h, lower, upper = lax.optimization_barrier((exchange(h, "yh"), lower, upper))
     home = new_home[own_rank]
     result0 = jnp.where(home[0] == own_rank, served0, far)
     result1 = jnp.where(
@@ -304,9 +349,9 @@
     attended = jnp.stack([result0, result1], 1)[:, None]
 
     out = down(yh, h, own_down, peer_down)
-    back = exchange(out.reshape(peers, block, chunk), PLANE).reshape(slots, chunk)
-    final = exchange(combine(mix, back, requests), COLUMN)
-    final = final.reshape(yh_size, steps, yl_size, requests, chunk).astype(F32)
+    back = exchange(out.reshape(peers, -1, chunk), PLANE).reshape(slots, chunk)
+    final = exchange(combine(mix, back, requests), LINE)
+    final = final.reshape(yh_size, steps, line, requests, chunk).astype(F32)
     final = final.sum(2).astype(BF).transpose(1, 2, 0, 3)
     return attended, final.reshape(steps, 1, requests, width)
 

time: 152 us -> 182 us (1.20)
  blocking collectives: 0 us -> 21.2 us
  waiting for transfers between devices: 50.8 us -> 59.1 us
  starting transfers between devices: 71 us -> 68.7 us
  Pallas kernels: 12.3 us -> 14.2 us
    ppermute x8, waiting for transfers between devices: 24.9 us -> 46.3 us  [shifted(): return lax.ppermute(x, axes, [(i, (i + by) % size) for i in range(size)])]
    all_to_all x0 -> x1, blocking collectives: none -> 21.2 us  [exchange(): return lax.all_to_all(x, axes, split_axis=0, concat_axis=0, tiled=True)]
    all_to_all x5 -> x4, waiting for transfers between devices: 25.9 us -> 12.7 us  [exchange(): return lax.all_to_all(x, axes, split_axis=0, concat_axis=0, tiled=True)]
    all_to_all x5 -> x4, starting transfers between devices: 38.5 us -> 30.5 us  [exchange(): return lax.all_to_all(x, axes, split_axis=0, concat_axis=0, tiled=True)]
    ppermute x8, starting transfers between devices: 32.5 us -> 38.2 us  [shifted(): return lax.ppermute(x, axes, [(i, (i + by) % size) for i in range(size)])]
    unnamed x27 -> x19, local copies, waits for them, and re-layouts: 7.59 us -> 5.17 us
    reshape x1, local copies, waits for them, and re-layouts: 0.18 us -> 2.51 us  [shards(): tokens = tokens.reshape(-1, tokens.shape[-1])]
    another operation x1, other arithmetic: 0.14 us -> 2.12 us  [shards(): own_down = jnp.stack(moved)]
  transfers between devices with their start and end apart: 13 -> 12, of which waited for: 8 -> 5; matrix products, arithmetic and copies ran while one was open for 5% -> 2% of each run, Pallas kernels for 4% -> 4%
where the time goes in v5:
time: 182 us; the launch traced here: 180 us
  starting transfers between devices  68.7 us (38%)
  waiting for transfers between devices  59.1 us (32%)
  blocking collectives  21.2 us (12%)
  Pallas kernels  14.2 us (8%)
  local copies, waits for them, and re-layouts  9.83 us (5%)
  other arithmetic  4.12 us (2%)
  between operations  2.96 us (2%)
    ppermute x8, waiting for transfers between devices, shifted(): return lax.ppermute(x, axes, [(i, (i + by) % size) for i in range(size)])  46.3 us
    ppermute x8, starting transfers between devices, shifted(): return lax.ppermute(x, axes, [(i, (i + by) % size) for i in range(size)])  38.2 us
    all_to_all x4, starting transfers between devices, exchange(): return lax.all_to_all(x, axes, split_axis=0, concat_axis=0, tiled=True)  30.5 us
    all_to_all x1, blocking collectives, exchange(): return lax.all_to_all(x, axes, split_axis=0, concat_axis=0, tiled=True)  21.2 us
    all_to_all x4, waiting for transfers between devices, exchange(): return lax.all_to_all(x, axes, split_axis=0, concat_axis=0, tiled=True)  12.7 us
    unnamed x19, local copies, waits for them, and re-layouts  5.17 us
    pallas_call x1, Pallas kernels, hidden_units(): pl.pallas_call(hidden_kernel, out_shape=jax.ShapeDtypeStruct((peers, *sha...  4.48 us
  transfers between devices with their start and end apart: 12, of which 5 were waited for; matrix products, arithmetic and copies ran while one was open for 2% of the time, Pallas kernels for 4%

profile of v5, /device:TPU:1, one launch (start us, length us, event | category | flops | bytes accessed | tf_op | source)
XLA Modules:
  0.0 180.0 jit_solution(13734055594966615724)
XLA Ops:
  0.7 1.4 copy.22.query_ref
  2.0 1.7 copy.23.cache_ref
  3.8 0.2 constant_dynamic-slice_fusion.1
  4.0 2.5 %attend.1 = (bf16[2,128,512]{2,1,0:T(8,128)(2,1)S(1)}, bf16[2,128,512]{2,1,0:T(8,128)(2,1)S(1)}) custom-call(s32[2]{0:T(128)S(1)} %get-tuple-element.61.len_ref, bf16[2,1,2,128,576]{4,3,2,1,0:T(8,128)(2,1)S(1)} %copy.22.query_ref, bf16[1,2,512,576]{3,2,1,0:T(8,128)(2,1)S(1)} %copy.23.cache_ref, bf16[2,1,2,576]{3,2,1,0:T(2,128)(2,1)S(1)} %copy-done.2), custom_call_target="tpu_custom_call" | custom-call | tf_op jit(solution)/shard_map/attend/pallas_call | solution.py:65
  6.4 0.0 copy-start.1
  6.4 0.0 copy-start.3
  6.4 0.0 copy-start.4
  6.4 1.7 pad_maximum_fusion.own_ref
  8.1 0.0 copy-start.5
  8.1 8.9 %collective-permute-start = (bf16[3584,256]{1,0:T(8,128)(2,1)S(1)}, bf16[3584,256]{1,0:T(8,128)(2,1)}, u32[]{:S(2)}, u32[]{:S(2)}) collective-permute-start(bf16[3584,256]{1,0:T(8,128)(2,1)S(1)} %pad_maximum_fusion.own_ref), channel_id=1, source_target_pairs={{0,64},{64,0},{1,65},{65,1},{2,66},{66,2},{3,67},{67,3},{4,68},{68... | collective-permute-start | bytes 5505032 | tf_op jit(solution)/shard_map/ppermute | solution.py:287
  17.1 1.1 pack.1
  18.2 11.1 %all-to-all-start = ((bf16[64,2,3600]{2,1,0:T(2,128)(2,1)}), bf16[64,2,3600]{2,1,0:T(2,128)(2,1)}, u32[]{:S(2)}, u32[]{:S(2)}) async-start(bf16[64,2,3600]{2,1,0:T(2,128)(2,1)} %pack.1), calls=%async_computation | async-start | bytes 1900544 | tf_op jit(solution)/shard_map/all_to_all | solution.py:282
  29.3 0.8 dynamic-slice_bitcast_fusion
  30.1 5.6 %collective-permute-start.2 = (bf16[128,896]{1,0:T(8,128)(2,1)S(1)}, bf16[128,896]{1,0:T(8,128)(2,1)}, u32[]{:S(2)}, u32[]{:S(2)}) collective-permute-start(bf16[128,896]{1,0:T(8,128)(2,1)S(1)} %get-tuple-element.54), channel_id=1, source_target_pairs={{0,384},{128,0},{256,128},{384,256},{1,385},{129,1},{257,129},{385... | collective-permute-start | bytes 688136 | tf_op jit(solution)/shard_map/ppermute | solution.py:287
  35.7 1.9 %collective-permute-start.1 = (bf16[128,896]{1,0:T(8,128)(2,1)S(1)}, bf16[128,896]{1,0:T(8,128)(2,1)}, u32[]{:S(2)}, u32[]{:S(2)}) collective-permute-start(bf16[128,896]{1,0:T(8,128)(2,1)S(1)} %get-tuple-element.55), channel_id=1, source_target_pairs={{0,128},{128,256},{256,384},{384,0},{1,129},{129,257},{257,385},{3... | collective-permute-start | bytes 688136 | tf_op jit(solution)/shard_map/ppermute | solution.py:287
  37.7 24.9 %collective-permute-done.2 = bf16[128,896]{1,0:T(8,128)(2,1)} collective-permute-done((bf16[128,896]{1,0:T(8,128)(2,1)S(1)}, bf16[128,896]{1,0:T(8,128)(2,1)}, u32[]{:S(2)}, u32[]{:S(2)}) %collective-permute-start.2) | collective-permute-done | bytes 229408 | tf_op jit(solution)/shard_map/ppermute | solution.py:287
  62.6 0.0 collective-permute-done.1
  62.6 0.9 all-to-all-done
  63.4 0.0 collective-permute-done.peer_ref
  63.4 2.5 %reshape.40.tokens_ref = bf16[128,3600]{1,0:T(8,128)(2,1)S(1)} reshape(bf16[64,2,3600]{2,1,0:T(2,128)(2,1)} %all-to-all-done) | data formatting | bytes 1843200 | tf_op jit(solution)/shard_map/reshape | solution.py:327
  66.0 1.7 dispatch.1
  67.6 1.2 copy-done
  68.9 4.3 %all-to-all-start.1 = ((bf16[8,32,3584]{2,1,0:T(8,128)(2,1)}), bf16[8,32,3584]{2,1,0:T(8,128)(2,1)}, u32[]{:S(2)}, u32[]{:S(2)}) async-start(bf16[8,32,3584]{2,1,0:T(8,128)(2,1)} %bitcast.32), calls=%async_computation.1 | async-start | bytes 3670016 | tf_op jit(solution)/shard_map/all_to_all | solution.py:282
  73.2 4.7 %collective-permute-start.4 = (bf16[128,896]{1,0:T(8,128)(2,1)}, bf16[128,896]{1,0:T(8,128)(2,1)S(1)}, u32[]{:S(2)}, u32[]{:S(2)}) collective-permute-start(bf16[128,896]{1,0:T(8,128)(2,1)} %get-tuple-element.38), channel_id=1, source_target_pairs={{0,256},{128,384},{256,0},{384,128},{1,257},{129,385},{257,1},{385... | collective-permute-start | bytes 688136 | tf_op jit(solution)/shard_map/ppermute | solution.py:287
  77.9 3.3 %collective-permute-start.3 = (bf16[2,128,512]{2,1,0:T(8,128)(2,1)S(1)}, bf16[2,128,512]{2,1,0:T(8,128)(2,1)}, u32[]{:S(2)}, u32[]{:S(2)}) collective-permute-start(bf16[2,128,512]{2,1,0:T(8,128)(2,1)S(1)} %get-tuple-element.30), channel_id=1, source_target_pairs={{0,32},{1,33},{2,34},{3,35},{4,36},{5,37},{6,38},{7,39},{8,40},{9,... | collective-permute-start | bytes 786440 | tf_op jit(solution)/shard_map/ppermute | solution.py:287
  81.1 20.9 %collective-permute-done.4 = bf16[128,896]{1,0:T(8,128)(2,1)S(1)} collective-permute-done((bf16[128,896]{1,0:T(8,128)(2,1)}, bf16[128,896]{1,0:T(8,128)(2,1)S(1)}, u32[]{:S(2)}, u32[]{:S(2)}) %collective-permute-start.4) | collective-permute-done | bytes 229408 | tf_op jit(solution)/shard_map/ppermute | solution.py:287
  102.0 2.1 %pad_maximum_fusion.1.own_ref = bf16[4,128,896]{2,1,0:T(8,128)(2,1)} fusion(bf16[1,128,896]{2,1,0:T(8,128)(2,1)} %bitcast.15, bf16[1,128,896]{2,1,0:T(8,128)(2,1)S(1)} %bitcast.37, bf16[1,128,896]{2,1,0:T(8,128)(2,1)} %bitcast.13, bf16[1,128,896]{2,1,0:T(8,128)(2,1)S(1)} %bitcast.36), kind=kLoop, calls=%fused_computation.1 | loop fusion | flops 1376256 | bytes 1835008 | tf_op jit(solution)/shard_map/stack | solution.py:332
  104.1 4.3 %collective-permute-start.7 = (bf16[4,128,896]{2,1,0:T(8,128)(2,1)}, bf16[4,128,896]{2,1,0:T(8,128)(2,1)}, u32[]{:S(2)}, u32[]{:S(2)}) collective-permute-start(bf16[4,128,896]{2,1,0:T(8,128)(2,1)} %pad_maximum_fusion.1.own_ref), channel_id=1, source_target_pairs={{0,64},{64,0},{1,65},{65,1},{2,66},{66,2},{3,67},{67,3},{4,68},{68... | collective-permute-start | bytes 2752520 | tf_op jit(solution)/shard_map/ppermute | solution.py:287
  108.4 0.5 mixing.1.mix_ref
  108.9 0.5 collective-permute-done.3
  109.5 0.0 all-to-all-done.1
  109.5 4.5 %hidden_units.1 = bf16[4,256,256]{2,1,0:T(8,128)(2,1)S(1)} custom-call(bf16[256,3584]{1,0:T(8,128)(2,1)} %bitcast.9.rows_ref, bf16[3584,256]{1,0:T(8,128)(2,1)S(1)} %pad_maximum_fusion.own_ref, bf16[3584,256]{1,0:T(8,128)(2,1)} %collective-permute-done.peer_ref), custom_call_target="tpu_custom_call" | custom-call | tf_op jit(solution)/shard_map/hidden_units/pallas_call | solution.py:221
  114.0 21.2 %all_to_all.25.h_ref = bf16[4,256,256]{2,1,0:T(8,128)(2,1)S(1)} all-to-all(bf16[4,256,256]{2,1,0:T(8,128)(2,1)S(1)} %hidden_units.1), channel_id=1, replica_groups=mesh['yh'=4,'c'=2,'yl'=2,'x'=4,'z'=8] {'yh'}, dimensions={0} | all-to-all | bytes 1048576 | tf_op jit(solution)/shard_map/all_to_all | solution.py:282
  135.2 0.0 collective-permute-done.7.peer_ref
  135.2 2.9 %down.1 = bf16[256,896]{1,0:T(8,128)(2,1)} custom-call(s32[1]{0:T(128)} %bitcast.18.yh_ref, bf16[4,256,256]{2,1,0:T(8,128)(2,1)S(1)} %all_to_all.25.h_ref, bf16[4,128,896]{2,1,0:T(8,128)(2,1)} %pad_maximum_fusion.1.own_ref, bf16[4,128,896]{2,1,0:T(8,128)(2,1)} %collective-permute-done.7.peer_ref), custom_call_target="tpu_custom_call" | custom-call | tf_op jit(solution)/shard_map/down/pallas_call | solution.py:246
  138.1 7.8 %all-to-all-start.3 = ((bf16[8,32,896]{2,1,0:T(8,128)(2,1)}), bf16[8,32,896]{2,1,0:T(8,128)(2,1)S(1)}, u32[]{:S(2)}, u32[]{:S(2)}) async-start(bf16[8,32,896]{2,1,0:T(8,128)(2,1)} %bitcast.19), calls=%async_computation.3 | async-start | bytes 917504 | tf_op jit(solution)/shard_map/all_to_all | solution.py:282
  145.9 3.0 %collective-permute-start.6 = (bf16[2,128,512]{2,1,0:T(8,128)(2,1)S(1)}, bf16[2,128,512]{2,1,0:T(8,128)(2,1)S(1)}, u32[]{:S(2)}, u32[]{:S(2)}) collective-permute-start(bf16[2,128,512]{2,1,0:T(8,128)(2,1)S(1)} %get-tuple-element.42), channel_id=1, source_target_pairs={{0,1},{1,2},{2,3},{3,4},{4,5},{5,6},{6,7},{7,8},{8,9},{9,10},{10,1... | collective-permute-start | bytes 786440 | tf_op jit(solution)/shard_map/ppermute | solution.py:287
  148.9 6.5 %collective-permute-start.5 = (bf16[2,128,512]{2,1,0:T(8,128)(2,1)S(1)}, bf16[2,128,512]{2,1,0:T(8,128)(2,1)S(1)}, u32[]{:S(2)}, u32[]{:S(2)}) collective-permute-start(bf16[2,128,512]{2,1,0:T(8,128)(2,1)S(1)} %get-tuple-element.42), channel_id=1, source_target_pairs={{0,63},{1,0},{2,1},{3,2},{4,3},{5,4},{6,5},{7,6},{8,7},{9,8},{10,9... | collective-permute-start | bytes 786440 | tf_op jit(solution)/shard_map/ppermute | solution.py:287
  155.4 0.6 fusion.1
  157.9 0.0 all-to-all-done.3
  157.9 1.0 combine.1
  158.9 7.4 %all-to-all-start.4 = ((bf16[64,2,896]{2,1,0:T(2,128)(2,1)}), bf16[64,2,896]{2,1,0:T(2,128)(2,1)S(1)}, u32[]{:S(2)}, u32[]{:S(2)}) async-start(bf16[64,2,896]{2,1,0:T(2,128)(2,1)} %combine.1), calls=%async_computation.4 | async-start | bytes 458752 | tf_op jit(solution)/shard_map/all_to_all | solution.py:282
  166.4 0.0 collective-permute-done.5
  166.4 0.1 maximum_bitcast_fusion
  166.5 0.8 copy.25
  167.3 11.9 %all-to-all-done.4 = bf16[64,2,896]{2,1,0:T(2,128)(2,1)S(1)} async-done(((bf16[64,2,896]{2,1,0:T(2,128)(2,1)}), bf16[64,2,896]{2,1,0:T(2,128)(2,1)S(1)}, u32[]{:S(2)}, u32[]{:S(2)}) %all-to-all-start.4) | async-done | bytes 229408 | tf_op jit(solution)/shard_map/all_to_all | solution.py:282
  179.2 0.2 bitcast_reduce_fusion
  179.4 0.6 reshape.47
  (16 shorter events, 0.1 us)
Async XLA Ops:
  0.6 3.1 %copy-start.6 = (s32[64,2]{0,1:T(2,128)S(1)}, s32[64,2]{0,1:T(2,128)}, u32[]{:S(2)}) copy-start(s32[64,2]{0,1:T(2,128)} %param.13) | copy-start | bytes 1540
  0.7 3.1 %copy-start.7 = (s32[64,2]{0,1:T(2,128)S(1)}, s32[64,2]{0,1:T(2,128)}, u32[]{:S(2)}) copy-start(s32[64,2]{0,1:T(2,128)} %param.12) | copy-start | bytes 1540
  0.7 3.3 %copy-start.2 = (bf16[2,1,2,576]{3,2,1,0:T(2,128)(2,1)S(1)}, bf16[2,1,2,576]{3,2,1,0:T(2,128)(2,1)}, u32[]{:S(2)}) copy-start(bf16[2,1,2,576]{3,2,1,0:T(2,128)(2,1)} %fresh_ref.1) | copy-start | bytes 13828
  6.4 10.6 %copy-start.1 = (bf16[2,1,2,3584]{3,2,1,0:T(2,128)(2,1)S(1)}, bf16[2,1,2,3584]{3,2,1,0:T(2,128)(2,1)}, u32[]{:S(2)}) copy-start(bf16[2,1,2,3584]{3,2,1,0:T(2,128)(2,1)} %hidden_ref.1) | copy-start | bytes 86020
  6.4 10.6 %copy-start.3 = (s32[2,1,2,8]{3,2,1,0:T(2,128)S(1)}, s32[2,1,2,8]{3,2,1,0:T(2,128)}, u32[]{:S(2)}) copy-start(s32[2,1,2,8]{3,2,1,0:T(2,128)} %routes_ref.1) | copy-start | bytes 388
  6.4 10.6 %copy-start.4 = (bf16[2,1,2,8]{3,2,1,0:T(2,128)(2,1)S(1)}, bf16[2,1,2,8]{3,2,1,0:T(2,128)(2,1)}, u32[]{:S(2)}) copy-start(bf16[2,1,2,8]{3,2,1,0:T(2,128)(2,1)} %logits_ref.1) | copy-start | bytes 196
  8.1 21.2 %copy-start.5 = (bf16[1,128,3584]{2,1,0:T(8,128)(2,1)S(1)}, bf16[1,128,3584]{2,1,0:T(8,128)(2,1)}, u32[]{:S(2)}) copy-start(bf16[1,128,3584]{2,1,0:T(8,128)(2,1)} %param.21) | copy-start | bytes 2752516
  8.1 55.3 %collective-permute-start = (bf16[3584,256]{1,0:T(8,128)(2,1)S(1)}, bf16[3584,256]{1,0:T(8,128)(2,1)}, u32[]{:S(2)}, u32[]{:S(2)}) collective-permute-start(bf16[3584,256]{1,0:T(8,128)(2,1)S(1)} %pad_maximum_fusion.own_ref), channel_id=1, source_target_pairs={{0,64},{64,0},{1,65},{65,1},{2,66},{66,2},{3,67},{67,3},{4,68},{68... | collective-permute-start | bytes 5505032 | tf_op jit(solution)/shard_map/ppermute | solution.py:287
  18.2 45.2 %all-to-all-start = ((bf16[64,2,3600]{2,1,0:T(2,128)(2,1)}), bf16[64,2,3600]{2,1,0:T(2,128)(2,1)}, u32[]{:S(2)}, u32[]{:S(2)}) async-start(bf16[64,2,3600]{2,1,0:T(2,128)(2,1)} %pack.1), calls=%async_computation | async-start | bytes 1900544 | tf_op jit(solution)/shard_map/all_to_all | solution.py:282
  30.1 32.5 %collective-permute-start.2 = (bf16[128,896]{1,0:T(8,128)(2,1)S(1)}, bf16[128,896]{1,0:T(8,128)(2,1)}, u32[]{:S(2)}, u32[]{:S(2)}) collective-permute-start(bf16[128,896]{1,0:T(8,128)(2,1)S(1)} %get-tuple-element.54), channel_id=1, source_target_pairs={{0,384},{128,0},{256,128},{384,256},{1,385},{129,1},{257,129},{385... | collective-permute-start | bytes 688136 | tf_op jit(solution)/shard_map/ppermute | solution.py:287
  35.7 26.9 %collective-permute-start.1 = (bf16[128,896]{1,0:T(8,128)(2,1)S(1)}, bf16[128,896]{1,0:T(8,128)(2,1)}, u32[]{:S(2)}, u32[]{:S(2)}) collective-permute-start(bf16[128,896]{1,0:T(8,128)(2,1)S(1)} %get-tuple-element.55), channel_id=1, source_target_pairs={{0,128},{128,256},{256,384},{384,0},{1,129},{129,257},{257,385},{3... | collective-permute-start | bytes 688136 | tf_op jit(solution)/shard_map/ppermute | solution.py:287
  67.6 1.3 copy-start
  68.9 40.6 %all-to-all-start.1 = ((bf16[8,32,3584]{2,1,0:T(8,128)(2,1)}), bf16[8,32,3584]{2,1,0:T(8,128)(2,1)}, u32[]{:S(2)}, u32[]{:S(2)}) async-start(bf16[8,32,3584]{2,1,0:T(8,128)(2,1)} %bitcast.32), calls=%async_computation.1 | async-start | bytes 3670016 | tf_op jit(solution)/shard_map/all_to_all | solution.py:282
  73.2 28.8 %collective-permute-start.4 = (bf16[128,896]{1,0:T(8,128)(2,1)}, bf16[128,896]{1,0:T(8,128)(2,1)S(1)}, u32[]{:S(2)}, u32[]{:S(2)}) collective-permute-start(bf16[128,896]{1,0:T(8,128)(2,1)} %get-tuple-element.38), channel_id=1, source_target_pairs={{0,256},{128,384},{256,0},{384,128},{1,257},{129,385},{257,1},{385... | collective-permute-start | bytes 688136 | tf_op jit(solution)/shard_map/ppermute | solution.py:287
  77.9 31.6 %collective-permute-start.3 = (bf16[2,128,512]{2,1,0:T(8,128)(2,1)S(1)}, bf16[2,128,512]{2,1,0:T(8,128)(2,1)}, u32[]{:S(2)}, u32[]{:S(2)}) collective-permute-start(bf16[2,128,512]{2,1,0:T(8,128)(2,1)S(1)} %get-tuple-element.30), channel_id=1, source_target_pairs={{0,32},{1,33},{2,34},{3,35},{4,36},{5,37},{6,38},{7,39},{8,40},{9,... | collective-permute-start | bytes 786440 | tf_op jit(solution)/shard_map/ppermute | solution.py:287
  104.1 31.0 %collective-permute-start.7 = (bf16[4,128,896]{2,1,0:T(8,128)(2,1)}, bf16[4,128,896]{2,1,0:T(8,128)(2,1)}, u32[]{:S(2)}, u32[]{:S(2)}) collective-permute-start(bf16[4,128,896]{2,1,0:T(8,128)(2,1)} %pad_maximum_fusion.1.own_ref), channel_id=1, source_target_pairs={{0,64},{64,0},{1,65},{65,1},{2,66},{66,2},{3,67},{67,3},{4,68},{68... | collective-permute-start | bytes 2752520 | tf_op jit(solution)/shard_map/ppermute | solution.py:287
  138.1 19.8 %all-to-all-start.3 = ((bf16[8,32,896]{2,1,0:T(8,128)(2,1)}), bf16[8,32,896]{2,1,0:T(8,128)(2,1)S(1)}, u32[]{:S(2)}, u32[]{:S(2)}) async-start(bf16[8,32,896]{2,1,0:T(8,128)(2,1)} %bitcast.19), calls=%async_computation.3 | async-start | bytes 917504 | tf_op jit(solution)/shard_map/all_to_all | solution.py:282
  145.9 20.5 %collective-permute-start.6 = (bf16[2,128,512]{2,1,0:T(8,128)(2,1)S(1)}, bf16[2,128,512]{2,1,0:T(8,128)(2,1)S(1)}, u32[]{:S(2)}, u32[]{:S(2)}) collective-permute-start(bf16[2,128,512]{2,1,0:T(8,128)(2,1)S(1)} %get-tuple-element.42), channel_id=1, source_target_pairs={{0,1},{1,2},{2,3},{3,4},{4,5},{5,6},{6,7},{7,8},{8,9},{9,10},{10,1... | collective-permute-start | bytes 786440 | tf_op jit(solution)/shard_map/ppermute | solution.py:287
  148.9 17.4 %collective-permute-start.5 = (bf16[2,128,512]{2,1,0:T(8,128)(2,1)S(1)}, bf16[2,128,512]{2,1,0:T(8,128)(2,1)S(1)}, u32[]{:S(2)}, u32[]{:S(2)}) collective-permute-start(bf16[2,128,512]{2,1,0:T(8,128)(2,1)S(1)} %get-tuple-element.42), channel_id=1, source_target_pairs={{0,63},{1,0},{2,1},{3,2},{4,3},{5,4},{6,5},{7,6},{8,7},{9,8},{10,9... | collective-permute-start | bytes 786440 | tf_op jit(solution)/shard_map/ppermute | solution.py:287
  158.9 20.3 %all-to-all-start.4 = ((bf16[64,2,896]{2,1,0:T(2,128)(2,1)}), bf16[64,2,896]{2,1,0:T(2,128)(2,1)S(1)}, u32[]{:S(2)}, u32[]{:S(2)}) async-start(bf16[64,2,896]{2,1,0:T(2,128)(2,1)} %combine.1), calls=%async_computation.4 | async-start | bytes 458752 | tf_op jit(solution)/shard_map/all_to_all | solution.py:282

commit v6 on v5

--- a/solution.py
+++ b/solution.py
@@ -13,10 +13,11 @@
 CAP = 4
 EP = ("yl", "x", "z")
 DP = ("yh", "c")
-LINE = ("yh", "c", "z")
-PLANE = ("yl", "x")
+COLUMN = ("yh", "c", "yl")
+PLANE = ("x", "z")
 BF = jnp.bfloat16
 F32 = jnp.float32
+ALL_VMEM = pltpu.CompilerParams(vmem_limit_bytes=60 * 1024 * 1024)
 PARAMS = pltpu.CompilerParams(vmem_limit_bytes=48 * 1024 * 1024)
 
 
@@ -121,64 +122,66 @@
             pltpu.VMEM((steps * inner, *block), BF),
             pltpu.SemaphoreType.DMA((max(outer, 3),)),
         ],
-        compiler_params=PARAMS,
+        compiler_params=ALL_VMEM,
         name="pack",
     )(hidden, routes, logits)
 
 
-def chosen_slots(z, line, tail, slots):
+def chosen_slots(yl, tail, slots):
     rows, top = tail.shape
     slot = iota((rows, slots), 1)
-    expert = (slot // (CAP * line) * line + z).astype(F32)
+    expert = (slot // (2 * CAP) + yl * (slots // (2 * CAP))).astype(F32)
     named = jnp.zeros((rows, slots), F32)
     for k in range(top):
         named = jnp.where(tail[:, k : k + 1] == expert, 1.0, named)
     this, other = iota((rows, rows), 0), iota((rows, rows), 1)
-    before = ((other < this) & (other // 2 % line == this // 2 % line)).astype(F32)
+    before = ((other < this) & (other // 2 % 2 == this // 2 % 2)).astype(F32)
     earlier = dot(before.astype(BF), named.astype(BF))
     chosen = (named > 0) & (earlier == (slot % CAP).astype(F32))
-    return chosen & (slot // CAP % line == iota((rows, slots), 0) // 2 % line), expert
-
-
-def dispatch_kernel(line, top, z_ref, tokens_ref, send_ref, held_ref, done):
-    slots, width = send_ref.shape
+    return chosen & (slot % (2 * CAP) // CAP == iota((rows, slots), 0) // 2 % 2), expert
+
+
+def dispatch_kernel(top, yl_ref, tokens_ref, send_ref, held_ref, done):
+    peers, block, width = send_ref.shape
     tail = tokens_ref[:, width : width + top].astype(F32)
-    chosen, _ = chosen_slots(z_ref[0], line, tail, slots)
+    chosen, _ = chosen_slots(yl_ref[0], tail, peers * block)
     pick = chosen.astype(F32).astype(BF)
     copies = []
-    for part in range(0, slots, 128):
-        span = slice(part, part + 128)
-        sent = dot(pick[:, span], tokens_ref[:, :width], ((0,), (0,)))
-        held_ref[span] = sent.astype(BF)
-        copy = pltpu.make_async_copy(held_ref.at[span], send_ref.at[span], done.at[part // 128])
+    group = 128 // block
+    for part in range(peers // group):
+        span = pl.ds(part * group, group)
+        lanes = slice(part * 128, (part + 1) * 128)
+        sent = dot(pick[:, lanes], tokens_ref[:, :width], ((0,), (0,)))
+        held_ref[span] = sent.reshape(group, block, width).astype(BF)
+        copy = pltpu.make_async_copy(held_ref.at[span], send_ref.at[span], done.at[part])
         copy.start()
         copies.append(copy)
     for copy in copies:
         copy.wait()
 
 
-def dispatch(z, line, top, tokens, slots, width):
-    return pl.pallas_call(
-        functools.partial(dispatch_kernel, line, top),
-        out_shape=jax.ShapeDtypeStruct((slots, width), BF),
+def dispatch(yl, top, tokens, peers, block, width):
+    return pl.pallas_call(
+        functools.partial(dispatch_kernel, top),
+        out_shape=jax.ShapeDtypeStruct((peers, block, width), BF),
         in_specs=[pl.BlockSpec(memory_space=pltpu.SMEM), *vmem(1)],
         out_specs=hbm(),
         scratch_shapes=[
-            pltpu.VMEM((slots, width), BF),
-            pltpu.SemaphoreType.DMA((slots // 128,)),
+            pltpu.VMEM((peers, block, width), BF),
+            pltpu.SemaphoreType.DMA((peers * block // 128,)),
         ],
         compiler_params=PARAMS,
         name="dispatch",
-    )(z, tokens)
-
-
-def mix_kernel(line, z_ref, tail_ref, mix_ref):
+    )(yl, tokens)
+
+
+def mix_kernel(yl_ref, tail_ref, mix_ref):
     slots = mix_ref.shape[1]
     tail = tail_ref[...].astype(F32)
     top = tail.shape[1] // 2
     sigmoid = jax.nn.sigmoid(tail[:, top:])
     gates = 2.5 * sigmoid / jnp.sum(sigmoid, 1, keepdims=True)
-    chosen, expert = chosen_slots(z_ref[0], line, tail[:, :top], slots)
+    chosen, expert = chosen_slots(yl_ref[0], tail[:, :top], slots)
     gate = jnp.zeros(chosen.shape, F32)
     for k in range(top):
         gate = jnp.where(tail[:, k : k + 1] == expert, gates[:, k : k + 1], gate)
@@ -187,31 +190,31 @@
     mix_ref[...] = jnp.concatenate(mix, 0).astype(BF)
 
 
-def mixing(z, line, tail, slots):
-    return pl.pallas_call(
-        functools.partial(mix_kernel, line),
+def mixing(yl, tail, slots):
+    return pl.pallas_call(
+        mix_kernel,
         out_shape=jax.ShapeDtypeStruct((2 * tail.shape[0], slots), BF),
         in_specs=[pl.BlockSpec(memory_space=pltpu.SMEM), *vmem(1)],
         out_specs=vmem(1)[0],
         compiler_params=PARAMS,
         name="mixing",
-    )(z, tail)
+    )(yl, tail)
 
 
 def hidden_kernel(rows_ref, own_ref, peer_ref, out_ref, held_ref, done):
     units = own_ref.shape[1] // 2
     rows = rows_ref[...]
-    copies = []
     for place, ref in enumerate((own_ref, peer_ref)):
         both = dot(rows, ref[...])
         gate, up = both[:, :units], both[:, units:]
         value = gate / (1.0 + jnp.exp(-gate)) * up
-        held_ref[place] = value.astype(BF)
-        for peer in range(out_ref.shape[0]):
-            target = out_ref.at[peer, :, pl.ds(place * units, units)]
-            copy = pltpu.make_async_copy(held_ref.at[place], target, done.at[place, peer])
-            copy.start()
-            copies.append(copy)
+        held_ref[:, place * units : (place + 1) * units] = value.astype(BF)
+    copies = [
+        pltpu.make_async_copy(held_ref, out_ref.at[peer], done.at[peer])
+        for peer in range(out_ref.shape[0])
+    ]
+    for copy in copies:
+        copy.start()
     for copy in copies:
         copy.wait()
 
@@ -223,10 +226,7 @@
         out_shape=jax.ShapeDtypeStruct((peers, *shape), BF),
         in_specs=vmem(3),
         out_specs=hbm(),
-        scratch_shapes=[
-            pltpu.VMEM((2, shape[0], shape[1] // 2), BF),
-            pltpu.SemaphoreType.DMA((2, peers)),
-        ],
+        scratch_shapes=[pltpu.VMEM(shape, BF), pltpu.SemaphoreType.DMA((peers,))],
         compiler_params=PARAMS,
         name="hidden_units",
     )(rows, own, peer)
@@ -301,44 +301,42 @@
     w_down,
 ):
     experts = lax.axis_size(EP)
-    yh_size, line = lax.axis_size("yh"), lax.axis_size("z")
-    peers = experts // line
+    yh_size, yl_size = lax.axis_size("yh"), lax.axis_size("yl")
+    peers = experts // yl_size
     own_rank = lax.axis_index(EP)
-    yh, z = lax.axis_index("yh"), lax.axis_index("z").reshape(1)
     steps, _, requests, width = hidden.shape
+    chunk = width // yh_size
+    block = yl_size * CAP
+    slots = peers * block
+
     top = routes.shape[3]
-    chunk = width // yh_size
-    slots = experts * CAP
-
-    packed = pack(hidden, routes, route_logits, yh_size, line)
-    tokens = exchange(packed, LINE)
+    yl = lax.axis_index("yl").reshape(1)
+
+    packed = pack(hidden, routes, route_logits, yh_size, yl_size)
+    tokens = exchange(packed, COLUMN)
+    own_w = jnp.concatenate([w_gate[0], w_up[0]], 1)
     served = attend(lengths[own_rank], queries, latent_cache, new_latent)
-    served, w_gate, w_up = lax.optimization_barrier((served, w_gate, w_up))
-    own_w = jnp.concatenate([w_gate[0], w_up[0]], 1)
+    tokens, own_w, served0, served1 = lax.optimization_barrier((tokens, own_w, *served))
+    tokens = tokens.reshape(-1, tokens.shape[-1])
+    send = dispatch(yl, top, tokens, peers, block, width)
+    arrived = exchange(send, PLANE).reshape(slots, width)
+
+    far = shifted(served0, EP, experts // 2)
+    lower = shifted(served1, EP, 1)
+    upper = shifted(served1, EP, -1)
+    mix = mixing(yl, tokens[:, width:], slots)
     peer_w = shifted(own_w, "c", 1)
+    yh = lax.axis_index("yh")
     sent = [
         lax.dynamic_slice_in_dim(w_down[0], (yh + s) % yh_size * chunk, chunk, 1)
         for s in range(yh_size)
     ]
-    moved = [shifted(x, "yh", s) if s in (1, yh_size - 1) else x for s, x in enumerate(sent)]
-    tokens, peer_w, served0, served1, *moved = lax.optimization_barrier(
-        (tokens, peer_w, *served, *moved)
+    own_down = jnp.stack([shifted(x, "yh", s) if s else x for s, x in enumerate(sent)])
+    peer_down = shifted(own_down, "c", 1)
+    arrived, peer_w, own_down, mix, far, lower, upper = lax.optimization_barrier(
+        (arrived, peer_w, own_down, mix, far, lower, upper)
     )
-    tokens = tokens.reshape(-1, tokens.shape[-1])
-    send = dispatch(z, line, top, tokens, slots, width)
-    arrived = exchange(send.reshape(peers, -1, width), PLANE).reshape(slots, width)
-    mix = mixing(z, line, tokens[:, width:], slots)
-    moved = [shifted(x, "yh", s) if 1 < s < yh_size - 1 else x for s, x in enumerate(moved)]
-    own_down = jnp.stack(moved)
-    peer_down = shifted(own_down, "c", 1)
-
-    far = shifted(served0, EP, experts // 2)
-    arrived, peer_w, far, mix = lax.optimization_barrier((arrived, peer_w, far, mix))
-    h = hidden_units(arrived, own_w, peer_w, yh_size)
-    h, own_down = lax.optimization_barrier((h, own_down))
-    h, served1 = lax.optimization_barrier((exchange(h, "yh"), served1))
-    lower = shifted(served1, EP, 1)
-    upper = shifted(served1, EP, -1)
+    h = exchange(hidden_units(arrived, own_w, peer_w, yh_size), "yh")
     home = new_home[own_rank]
     result0 = jnp.where(home[0] == own_rank, served0, far)
     result1 = jnp.where(
@@ -349,9 +347,9 @@
     attended = jnp.stack([result0, result1], 1)[:, None]
 
     out = down(yh, h, own_down, peer_down)
-    back = exchange(out.reshape(peers, -1, chunk), PLANE).reshape(slots, chunk)
-    final = exchange(combine(mix, back, requests), LINE)
-    final = final.reshape(yh_size, steps, line, requests, chunk).astype(F32)
+    back = exchange(out.reshape(peers, block, chunk), PLANE).reshape(slots, chunk)
+    final = exchange(combine(mix, back, requests), COLUMN)
+    final = final.reshape(yh_size, steps, yl_size, requests, chunk).astype(F32)
     final = final.sum(2).astype(BF).transpose(1, 2, 0, 3)
     return attended, final.reshape(steps, 1, requests, width)
 

time: 182 us -> 150 us (0.82)
  blocking collectives: 21.2 us -> 0 us
  waiting for transfers between devices: 59.1 us -> 44.7 us
  starting transfers between devices: 68.7 us -> 80.8 us
  local copies, waits for them, and re-layouts: 9.83 us -> 6.25 us
  other arithmetic: 4.12 us -> 0.55 us
    ppermute x8, waiting for transfers between devices: 46.3 us -> 14.1 us  [shifted(): return lax.ppermute(x, axes, [(i, (i + by) % size) for i in range(size)])]
    all_to_all x1 -> x0, blocking collectives: 21.2 us -> none  [exchange(): return lax.all_to_all(x, axes, split_axis=0, concat_axis=0, tiled=True)]
    all_to_all x4 -> x5, waiting for transfers between devices: 12.7 us -> 30.7 us  [exchange(): return lax.all_to_all(x, axes, split_axis=0, concat_axis=0, tiled=True)]
    all_to_all x4 -> x5, starting transfers between devices: 30.5 us -> 48.4 us  [exchange(): return lax.all_to_all(x, axes, split_axis=0, concat_axis=0, tiled=True)]
    ppermute x8, starting transfers between devices: 38.2 us -> 32.4 us  [shifted(): return lax.ppermute(x, axes, [(i, (i + by) % size) for i in range(size)])]
    another operation x1, other arithmetic: 2.12 us -> 0.14 us  [shards(): jnp.stack([shifted(x, 'yh', s) if s else x for s, x in enumerate(sent)])]
    unnamed x19 -> x29, local copies, waits for them, and re-layouts: 5.17 us -> 3.68 us
  transfers between devices with their start and end apart: 12 -> 13, of which waited for: 5 -> 8; matrix products, arithmetic and copies ran while one was open for 2% -> 3% of each run, Pallas kernels for 4% -> 5%
where the time goes in v6:
time: 150 us; the launch traced here: 149 us
  starting transfers between devices  80.8 us (54%)
  waiting for transfers between devices  44.7 us (30%)
  Pallas kernels  13.9 us (9%)
  local copies, waits for them, and re-layouts  6.25 us (4%)
  between operations  2.98 us (2%)
    all_to_all x5, starting transfers between devices, exchange(): return lax.all_to_all(x, axes, split_axis=0, concat_axis=0, tiled=True)  48.4 us
    ppermute x8, starting transfers between devices, shifted(): return lax.ppermute(x, axes, [(i, (i + by) % size) for i in range(size)])  32.4 us
    all_to_all x5, waiting for transfers between devices, exchange(): return lax.all_to_all(x, axes, split_axis=0, concat_axis=0, tiled=True)  30.7 us
    ppermute x8, waiting for transfers between devices, shifted(): return lax.ppermute(x, axes, [(i, (i + by) % size) for i in range(size)])  14.1 us
    pallas_call x1, Pallas kernels, hidden_units(): pl.pallas_call(hidden_kernel, out_shape=jax.ShapeDtypeStruct((peers, *sha...  4 us
    unnamed x29, local copies, waits for them, and re-layouts  3.68 us
  transfers between devices with their start and end apart: 13, of which 8 were waited for; matrix products, arithmetic and copies ran while one was open for 3% of the time, Pallas kernels for 5%

profile of v6, /device:TPU:1, one launch (start us, length us, event | category | flops | bytes accessed | tf_op | source)
XLA Modules:
  0.0 149.2 jit_solution(13566040668314343659)
XLA Ops:
  0.6 1.6 %pack.1 = bf16[16,2,3600]{2,1,0:T(2,128)(2,1)} custom-call(bf16[2,1,2,3584]{3,2,1,0:T(2,128)(2,1)} %hidden_ref.1, s32[2,1,2,8]{3,2,1,0:T(2,128)} %routes_ref.1, bf16[2,1,2,8]{3,2,1,0:T(2,128)(2,1)} %logits_ref.1), custom_call_target="tpu_custom_call" | custom-call | tf_op jit(solution)/shard_map/pack/pallas_call | solution.py:113
  2.3 10.8 %all-to-all-start = ((bf16[16,2,3600]{2,1,0:T(2,128)(2,1)}), bf16[16,2,3600]{2,1,0:T(2,128)(2,1)}, u32[]{:S(2)}, u32[]{:S(2)}) async-start(bf16[16,2,3600]{2,1,0:T(2,128)(2,1)} %pack.1), calls=%async_computation | async-start | bytes 475136 | tf_op jit(solution)/shard_map/all_to_all | solution.py:282
  13.1 0.0 copy-start.12
  13.1 0.0 copy-start
  13.1 1.4 copy.19.query_ref
  14.5 0.7 copy.20.cache_ref
  15.2 0.0 copy-start.2
  15.3 0.0 copy-start.3
  15.3 0.2 constant_dynamic-slice_fusion.2
  15.5 2.4 %attend.1 = (bf16[2,128,512]{2,1,0:T(8,128)(2,1)S(1)}, bf16[2,128,512]{2,1,0:T(8,128)(2,1)S(1)}) custom-call(s32[2]{0:T(128)S(1)} %get-tuple-element.41.len_ref, bf16[2,1,2,128,576]{4,3,2,1,0:T(8,128)(2,1)S(1)} %copy.19.query_ref, bf16[1,2,512,576]{3,2,1,0:T(8,128)(2,1)S(1)} %copy.20.cache_ref, bf16[2,1,2,576]{3,2,1,0:T(2,128)(2,1)S(1)} %copy-done), custom_call_target="tpu_custom_call" | custom-call | tf_op jit(solution)/shard_map/attend/pallas_call | solution.py:66
  17.9 0.2 pad_maximum_fusion.own_ref
  18.2 4.8 %all-to-all-done = bf16[16,2,3600]{2,1,0:T(2,128)(2,1)} async-done(((bf16[16,2,3600]{2,1,0:T(2,128)(2,1)}), bf16[16,2,3600]{2,1,0:T(2,128)(2,1)}, u32[]{:S(2)}, u32[]{:S(2)}) %all-to-all-start) | async-done | bytes 230432 | tf_op jit(solution)/shard_map/all_to_all | solution.py:282
  22.9 1.1 reshape.38.tokens_ref
  24.1 1.9 %dispatch.1 = bf16[32,8,3584]{2,1,0:T(8,128)(2,1)} custom-call(s32[1]{0:T(128)} %bitcast.3.yl_ref, bf16[32,3600]{1,0:T(8,128)(2,1)S(1)} %reshape.38.tokens_ref), custom_call_target="tpu_custom_call" | custom-call | tf_op jit(solution)/shard_map/dispatch/pallas_call | solution.py:164
  25.9 0.0 copy-start.4
  25.9 10.9 %all-to-all-start.1 = ((bf16[32,8,3584]{2,1,0:T(8,128)(2,1)}), bf16[32,8,3584]{2,1,0:T(8,128)(2,1)}, u32[]{:S(2)}, u32[]{:S(2)}) async-start(bf16[32,8,3584]{2,1,0:T(8,128)(2,1)} %dispatch.1), calls=%async_computation.1 | async-start | bytes 3670016 | tf_op jit(solution)/shard_map/all_to_all | solution.py:282
  36.8 2.6 %collective-permute-start = (bf16[3584,256]{1,0:T(8,128)(2,1)S(1)}, bf16[3584,256]{1,0:T(8,128)(2,1)}, u32[]{:S(2)}, u32[]{:S(2)}) collective-permute-start(bf16[3584,256]{1,0:T(8,128)(2,1)S(1)} %pad_maximum_fusion.own_ref), channel_id=1, source_target_pairs={{0,64},{64,0},{1,65},{65,1},{2,66},{66,2},{3,67},{67,3},{4,68},{68... | collective-permute-start | bytes 5505032 | tf_op jit(solution)/shard_map/ppermute | solution.py:287
  39.5 0.1 constant_dynamic-slice_fusion
  39.6 3.6 %collective-permute-start.3 = (bf16[128,896]{1,0:T(8,128)(2,1)S(1)}, bf16[128,896]{1,0:T(8,128)(2,1)S(1)}, u32[]{:S(2)}, u32[]{:S(2)}) collective-permute-start(bf16[128,896]{1,0:T(8,128)(2,1)S(1)} %get-tuple-element.36), channel_id=1, source_target_pairs={{0,384},{128,0},{256,128},{384,256},{1,385},{129,1},{257,129},{385... | collective-permute-start | bytes 688136 | tf_op jit(solution)/shard_map/ppermute | solution.py:287
  43.2 5.3 %collective-permute-start.2 = (bf16[128,896]{1,0:T(8,128)(2,1)S(1)}, bf16[128,896]{1,0:T(8,128)(2,1)S(1)}, u32[]{:S(2)}, u32[]{:S(2)}) collective-permute-start(bf16[128,896]{1,0:T(8,128)(2,1)S(1)} %get-tuple-element.37), channel_id=1, source_target_pairs={{0,256},{128,384},{256,0},{384,128},{1,257},{129,385},{257,1},{385... | collective-permute-start | bytes 688136 | tf_op jit(solution)/shard_map/ppermute | solution.py:287
  48.5 1.9 %collective-permute-start.1 = (bf16[128,896]{1,0:T(8,128)(2,1)S(1)}, bf16[128,896]{1,0:T(8,128)(2,1)S(1)}, u32[]{:S(2)}, u32[]{:S(2)}) collective-permute-start(bf16[128,896]{1,0:T(8,128)(2,1)S(1)} %get-tuple-element.35), channel_id=1, source_target_pairs={{0,128},{128,256},{256,384},{384,0},{1,129},{129,257},{257,385},{3... | collective-permute-start | bytes 688136 | tf_op jit(solution)/shard_map/ppermute | solution.py:287
  50.4 3.4 %collective-permute-start.5 = (bf16[2,128,512]{2,1,0:T(8,128)(2,1)S(1)}, bf16[2,128,512]{2,1,0:T(8,128)(2,1)S(1)}, u32[]{:S(2)}, u32[]{:S(2)}) collective-permute-start(bf16[2,128,512]{2,1,0:T(8,128)(2,1)S(1)} %get-tuple-element.20), channel_id=1, source_target_pairs={{0,1},{1,2},{2,3},{3,4},{4,5},{5,6},{6,7},{7,8},{8,9},{9,10},{10,1... | collective-permute-start | bytes 786440 | tf_op jit(solution)/shard_map/ppermute | solution.py:287
  53.8 1.9 %collective-permute-done.3 = bf16[128,896]{1,0:T(8,128)(2,1)S(1)} collective-permute-done((bf16[128,896]{1,0:T(8,128)(2,1)S(1)}, bf16[128,896]{1,0:T(8,128)(2,1)S(1)}, u32[]{:S(2)}, u32[]{:S(2)}) %collective-permute-start.3) | collective-permute-done | bytes 229408 | tf_op jit(solution)/shard_map/ppermute | solution.py:287
  55.7 4.2 %collective-permute-start.6 = (bf16[2,128,512]{2,1,0:T(8,128)(2,1)S(1)}, bf16[2,128,512]{2,1,0:T(8,128)(2,1)S(1)}, u32[]{:S(2)}, u32[]{:S(2)}) collective-permute-start(bf16[2,128,512]{2,1,0:T(8,128)(2,1)S(1)} %get-tuple-element.20), channel_id=1, source_target_pairs={{0,63},{1,0},{2,1},{3,2},{4,3},{5,4},{6,5},{7,6},{8,7},{9,8},{10,9... | collective-permute-start | bytes 786440 | tf_op jit(solution)/shard_map/ppermute | solution.py:287
  60.0 1.0 collective-permute-done.2
  61.0 8.2 %collective-permute-start.4 = (bf16[2,128,512]{2,1,0:T(8,128)(2,1)S(1)}, bf16[2,128,512]{2,1,0:T(8,128)(2,1)S(1)}, u32[]{:S(2)}, u32[]{:S(2)}) collective-permute-start(bf16[2,128,512]{2,1,0:T(8,128)(2,1)S(1)} %get-tuple-element.17), channel_id=1, source_target_pairs={{0,32},{1,33},{2,34},{3,35},{4,36},{5,37},{6,38},{7,39},{8,40},{9,... | collective-permute-start | bytes 786440 | tf_op jit(solution)/shard_map/ppermute | solution.py:287
  69.2 0.0 collective-permute-done.1
  69.2 0.1 pad_maximum_fusion.1.own_ref
  69.3 3.3 %collective-permute-start.7 = (bf16[4,128,896]{2,1,0:T(8,128)(2,1)S(1)}, bf16[4,128,896]{2,1,0:T(8,128)(2,1)}, u32[]{:S(2)}, u32[]{:S(2)}) collective-permute-start(bf16[4,128,896]{2,1,0:T(8,128)(2,1)S(1)} %pad_maximum_fusion.1.own_ref), channel_id=1, source_target_pairs={{0,64},{64,0},{1,65},{65,1},{2,66},{66,2},{3,67},{67,3},{4,68},{68... | collective-permute-start | bytes 2752520 | tf_op jit(solution)/shard_map/ppermute | solution.py:287
  72.6 0.3 mixing.1.mix_ref
  73.0 9.7 %collective-permute-done.4 = bf16[2,128,512]{2,1,0:T(8,128)(2,1)S(1)} collective-permute-done((bf16[2,128,512]{2,1,0:T(8,128)(2,1)S(1)}, bf16[2,128,512]{2,1,0:T(8,128)(2,1)S(1)}, u32[]{:S(2)}, u32[]{:S(2)}) %collective-permute-start.4) | collective-permute-done | bytes 262176 | tf_op jit(solution)/shard_map/ppermute | solution.py:287
  82.7 1.3 collective-permute-done.6
  84.1 0.7 copy-done.7
  84.8 4.0 %hidden_units.1 = bf16[4,256,256]{2,1,0:T(8,128)(2,1)} custom-call(bf16[256,3584]{1,0:T(8,128)(2,1)} %bitcast.4.rows_ref, bf16[3584,256]{1,0:T(8,128)(2,1)S(1)} %pad_maximum_fusion.own_ref, bf16[3584,256]{1,0:T(8,128)(2,1)} %collective-permute-done.peer_ref), custom_call_target="tpu_custom_call" | custom-call | tf_op jit(solution)/shard_map/hidden_units/pallas_call | solution.py:224
  88.8 3.5 %all-to-all-start.2 = ((bf16[4,256,256]{2,1,0:T(8,128)(2,1)}), bf16[4,256,256]{2,1,0:T(8,128)(2,1)S(1)}, u32[]{:S(2)}, u32[]{:S(2)}) async-start(bf16[4,256,256]{2,1,0:T(8,128)(2,1)} %hidden_units.1), calls=%async_computation.2 | async-start | bytes 1048576 | tf_op jit(solution)/shard_map/all_to_all | solution.py:282
  92.3 11.0 %all-to-all-done.2.h_ref = bf16[4,256,256]{2,1,0:T(8,128)(2,1)S(1)} async-done(((bf16[4,256,256]{2,1,0:T(8,128)(2,1)}), bf16[4,256,256]{2,1,0:T(8,128)(2,1)S(1)}, u32[]{:S(2)}, u32[]{:S(2)}) %all-to-all-start.2) | async-done | bytes 524320 | tf_op jit(solution)/shard_map/all_to_all | solution.py:282
  103.3 2.7 %down.1 = bf16[256,896]{1,0:T(8,128)(2,1)} custom-call(s32[1]{0:T(128)} %bitcast.15.yh_ref, bf16[4,256,256]{2,1,0:T(8,128)(2,1)S(1)} %all-to-all-done.2.h_ref, bf16[4,128,896]{2,1,0:T(8,128)(2,1)S(1)} %pad_maximum_fusion.1.own_ref, bf16[4,128,896]{2,1,0:T(8,128)(2,1)} %collective-permute-done.7.peer_ref), custom_call_target="tpu_custom_call" | custom-call | tf_op jit(solution)/shard_map/down/pallas_call | solution.py:246
  106.1 10.1 %all-to-all-start.3 = ((bf16[32,8,896]{2,1,0:T(8,128)(2,1)}), bf16[32,8,896]{2,1,0:T(8,128)(2,1)S(1)}, u32[]{:S(2)}, u32[]{:S(2)}) async-start(bf16[32,8,896]{2,1,0:T(8,128)(2,1)} %bitcast.16), calls=%async_computation.3 | async-start | bytes 917504 | tf_op jit(solution)/shard_map/all_to_all | solution.py:282
  116.2 0.5 fusion.1
  118.7 0.1 select_bitcast_fusion
  118.8 8.2 %all-to-all-done.3 = bf16[32,8,896]{2,1,0:T(8,128)(2,1)S(1)} async-done(((bf16[32,8,896]{2,1,0:T(8,128)(2,1)}), bf16[32,8,896]{2,1,0:T(8,128)(2,1)S(1)}, u32[]{:S(2)}, u32[]{:S(2)}) %all-to-all-start.3) | async-done | bytes 458784 | tf_op jit(solution)/shard_map/all_to_all | solution.py:282
  127.0 0.8 combine.1
  127.8 13.1 %all-to-all-start.4 = ((bf16[16,2,896]{2,1,0:T(2,128)(2,1)}), bf16[16,2,896]{2,1,0:T(2,128)(2,1)S(1)}, u32[]{:S(2)}, u32[]{:S(2)}) async-start(bf16[16,2,896]{2,1,0:T(2,128)(2,1)} %combine.1), calls=%async_computation.4 | async-start | bytes 114688 | tf_op jit(solution)/shard_map/all_to_all | solution.py:282
  141.0 0.1 maximum_bitcast_fusion
  141.0 0.8 copy.22
  141.8 6.7 %all-to-all-done.4 = bf16[16,2,896]{2,1,0:T(2,128)(2,1)S(1)} async-done(((bf16[16,2,896]{2,1,0:T(2,128)(2,1)}), bf16[16,2,896]{2,1,0:T(2,128)(2,1)S(1)}, u32[]{:S(2)}, u32[]{:S(2)}) %all-to-all-start.4) | async-done | bytes 57376 | tf_op jit(solution)/shard_map/all_to_all | solution.py:282
  148.5 0.1 bitcast_reduce_fusion
  148.6 0.6 reshape.44
  (27 shorter events, 0.1 us)
Async XLA Ops:
  0.6 13.9 %copy-start.1 = (bf16[1,2,512,576]{2,3,1,0:T(8,128)(2,1)S(1)}, bf16[1,2,512,576]{2,3,1,0:T(8,128)(2,1)}, u32[]{:S(2)}) copy-start(bf16[1,2,512,576]{2,3,1,0:T(8,128)(2,1)} %param.11) | copy-start | bytes 3538948
  2.3 20.6 %all-to-all-start = ((bf16[16,2,3600]{2,1,0:T(2,128)(2,1)}), bf16[16,2,3600]{2,1,0:T(2,128)(2,1)}, u32[]{:S(2)}, u32[]{:S(2)}) async-start(bf16[16,2,3600]{2,1,0:T(2,128)(2,1)} %pack.1), calls=%async_computation | async-start | bytes 475136 | tf_op jit(solution)/shard_map/all_to_all | solution.py:282
  13.1 2.2 %copy-start.11 = (s32[64,2]{0,1:T(2,128)S(1)}, s32[64,2]{0,1:T(2,128)}, u32[]{:S(2)}) copy-start(s32[64,2]{0,1:T(2,128)} %param.13) | copy-start | bytes 1540
  13.1 2.2 %copy-start.12 = (s32[64,2]{0,1:T(2,128)S(1)}, s32[64,2]{0,1:T(2,128)}, u32[]{:S(2)}) copy-start(s32[64,2]{0,1:T(2,128)} %param.12) | copy-start | bytes 1540
  13.1 2.4 %copy-start = (bf16[2,1,2,576]{3,2,1,0:T(2,128)(2,1)S(1)}, bf16[2,1,2,576]{3,2,1,0:T(2,128)(2,1)}, u32[]{:S(2)}) copy-start(bf16[2,1,2,576]{3,2,1,0:T(2,128)(2,1)} %fresh_ref.1) | copy-start | bytes 13828
  15.2 2.7 %copy-start.2 = (bf16[1,3584,128]{2,1,0:T(8,128)(2,1)S(1)}, bf16[1,3584,128]{2,1,0:T(8,128)(2,1)}, u32[]{:S(2)}) copy-start(bf16[1,3584,128]{2,1,0:T(8,128)(2,1)} %param.20) | copy-start | bytes 2752516
  15.3 2.7 %copy-start.3 = (bf16[1,3584,128]{2,1,0:T(8,128)(2,1)S(1)}, bf16[1,3584,128]{2,1,0:T(8,128)(2,1)}, u32[]{:S(2)}) copy-start(bf16[1,3584,128]{2,1,0:T(8,128)(2,1)} %param.19) | copy-start | bytes 2752516
  25.9 13.6 %copy-start.4 = (bf16[1,128,3584]{2,1,0:T(8,128)(2,1)S(1)}, bf16[1,128,3584]{2,1,0:T(8,128)(2,1)}, u32[]{:S(2)}) copy-start(bf16[1,128,3584]{2,1,0:T(8,128)(2,1)} %param.21) | copy-start | bytes 2752516
  25.9 58.8 %all-to-all-start.1 = ((bf16[32,8,3584]{2,1,0:T(8,128)(2,1)}), bf16[32,8,3584]{2,1,0:T(8,128)(2,1)}, u32[]{:S(2)}, u32[]{:S(2)}) async-start(bf16[32,8,3584]{2,1,0:T(8,128)(2,1)} %dispatch.1), calls=%async_computation.1 | async-start | bytes 3670016 | tf_op jit(solution)/shard_map/all_to_all | solution.py:282
  36.8 47.9 %collective-permute-start = (bf16[3584,256]{1,0:T(8,128)(2,1)S(1)}, bf16[3584,256]{1,0:T(8,128)(2,1)}, u32[]{:S(2)}, u32[]{:S(2)}) collective-permute-start(bf16[3584,256]{1,0:T(8,128)(2,1)S(1)} %pad_maximum_fusion.own_ref), channel_id=1, source_target_pairs={{0,64},{64,0},{1,65},{65,1},{2,66},{66,2},{3,67},{67,3},{4,68},{68... | collective-permute-start | bytes 5505032 | tf_op jit(solution)/shard_map/ppermute | solution.py:287
  39.6 16.2 %collective-permute-start.3 = (bf16[128,896]{1,0:T(8,128)(2,1)S(1)}, bf16[128,896]{1,0:T(8,128)(2,1)S(1)}, u32[]{:S(2)}, u32[]{:S(2)}) collective-permute-start(bf16[128,896]{1,0:T(8,128)(2,1)S(1)} %get-tuple-element.36), channel_id=1, source_target_pairs={{0,384},{128,0},{256,128},{384,256},{1,385},{129,1},{257,129},{385... | collective-permute-start | bytes 688136 | tf_op jit(solution)/shard_map/ppermute | solution.py:287
  43.2 17.8 %collective-permute-start.2 = (bf16[128,896]{1,0:T(8,128)(2,1)S(1)}, bf16[128,896]{1,0:T(8,128)(2,1)S(1)}, u32[]{:S(2)}, u32[]{:S(2)}) collective-permute-start(bf16[128,896]{1,0:T(8,128)(2,1)S(1)} %get-tuple-element.37), channel_id=1, source_target_pairs={{0,256},{128,384},{256,0},{384,128},{1,257},{129,385},{257,1},{385... | collective-permute-start | bytes 688136 | tf_op jit(solution)/shard_map/ppermute | solution.py:287
  48.5 20.7 %collective-permute-start.1 = (bf16[128,896]{1,0:T(8,128)(2,1)S(1)}, bf16[128,896]{1,0:T(8,128)(2,1)S(1)}, u32[]{:S(2)}, u32[]{:S(2)}) collective-permute-start(bf16[128,896]{1,0:T(8,128)(2,1)S(1)} %get-tuple-element.35), channel_id=1, source_target_pairs={{0,128},{128,256},{256,384},{384,0},{1,129},{129,257},{257,385},{3... | collective-permute-start | bytes 688136 | tf_op jit(solution)/shard_map/ppermute | solution.py:287
  50.4 32.3 %collective-permute-start.5 = (bf16[2,128,512]{2,1,0:T(8,128)(2,1)S(1)}, bf16[2,128,512]{2,1,0:T(8,128)(2,1)S(1)}, u32[]{:S(2)}, u32[]{:S(2)}) collective-permute-start(bf16[2,128,512]{2,1,0:T(8,128)(2,1)S(1)} %get-tuple-element.20), channel_id=1, source_target_pairs={{0,1},{1,2},{2,3},{3,4},{4,5},{5,6},{6,7},{7,8},{8,9},{9,10},{10,1... | collective-permute-start | bytes 786440 | tf_op jit(solution)/shard_map/ppermute | solution.py:287
  55.7 28.3 %collective-permute-start.6 = (bf16[2,128,512]{2,1,0:T(8,128)(2,1)S(1)}, bf16[2,128,512]{2,1,0:T(8,128)(2,1)S(1)}, u32[]{:S(2)}, u32[]{:S(2)}) collective-permute-start(bf16[2,128,512]{2,1,0:T(8,128)(2,1)S(1)} %get-tuple-element.20), channel_id=1, source_target_pairs={{0,63},{1,0},{2,1},{3,2},{4,3},{5,4},{6,5},{7,6},{8,7},{9,8},{10,9... | collective-permute-start | bytes 786440 | tf_op jit(solution)/shard_map/ppermute | solution.py:287
  61.0 21.7 %collective-permute-start.4 = (bf16[2,128,512]{2,1,0:T(8,128)(2,1)S(1)}, bf16[2,128,512]{2,1,0:T(8,128)(2,1)S(1)}, u32[]{:S(2)}, u32[]{:S(2)}) collective-permute-start(bf16[2,128,512]{2,1,0:T(8,128)(2,1)S(1)} %get-tuple-element.17), channel_id=1, source_target_pairs={{0,32},{1,33},{2,34},{3,35},{4,36},{5,37},{6,38},{7,39},{8,40},{9,... | collective-permute-start | bytes 786440 | tf_op jit(solution)/shard_map/ppermute | solution.py:287
  69.3 22.9 %collective-permute-start.7 = (bf16[4,128,896]{2,1,0:T(8,128)(2,1)S(1)}, bf16[4,128,896]{2,1,0:T(8,128)(2,1)}, u32[]{:S(2)}, u32[]{:S(2)}) collective-permute-start(bf16[4,128,896]{2,1,0:T(8,128)(2,1)S(1)} %pad_maximum_fusion.1.own_ref), channel_id=1, source_target_pairs={{0,64},{64,0},{1,65},{65,1},{2,66},{66,2},{3,67},{67,3},{4,68},{68... | collective-permute-start | bytes 2752520 | tf_op jit(solution)/shard_map/ppermute | solution.py:287
  82.7 1.3 copy-start.9
  82.7 1.3 copy-start.5
  84.1 0.7 copy-start.7
  88.8 14.5 %all-to-all-start.2 = ((bf16[4,256,256]{2,1,0:T(8,128)(2,1)}), bf16[4,256,256]{2,1,0:T(8,128)(2,1)S(1)}, u32[]{:S(2)}, u32[]{:S(2)}) async-start(bf16[4,256,256]{2,1,0:T(8,128)(2,1)} %hidden_units.1), calls=%async_computation.2 | async-start | bytes 1048576 | tf_op jit(solution)/shard_map/all_to_all | solution.py:282
  103.3 15.3 %copy-start.10 = (bf16[2,128,512]{2,1,0:T(8,128)(2,1)S(1)}, bf16[2,128,512]{2,1,0:T(8,128)(2,1)}, u32[]{:S(2)}) copy-start(bf16[2,128,512]{2,1,0:T(8,128)(2,1)} %copy-done.9) | copy-start | bytes 786436
  103.3 15.4 %copy-start.6 = (bf16[2,128,512]{2,1,0:T(8,128)(2,1)S(1)}, bf16[2,128,512]{2,1,0:T(8,128)(2,1)}, u32[]{:S(2)}) copy-start(bf16[2,128,512]{2,1,0:T(8,128)(2,1)} %copy-done.5) | copy-start | bytes 786436
  103.3 15.4 %copy-start.8 = (bf16[2,128,512]{2,1,0:T(8,128)(2,1)S(1)}, bf16[2,128,512]{2,1,0:T(8,128)(2,1)}, u32[]{:S(2)}) copy-start(bf16[2,128,512]{2,1,0:T(8,128)(2,1)} %copy-done.7) | copy-start | bytes 786436
  106.1 20.9 %all-to-all-start.3 = ((bf16[32,8,896]{2,1,0:T(8,128)(2,1)}), bf16[32,8,896]{2,1,0:T(8,128)(2,1)S(1)}, u32[]{:S(2)}, u32[]{:S(2)}) async-start(bf16[32,8,896]{2,1,0:T(8,128)(2,1)} %bitcast.16), calls=%async_computation.3 | async-start | bytes 917504 | tf_op jit(solution)/shard_map/all_to_all | solution.py:282
  127.8 20.7 %all-to-all-start.4 = ((bf16[16,2,896]{2,1,0:T(2,128)(2,1)}), bf16[16,2,896]{2,1,0:T(2,128)(2,1)S(1)}, u32[]{:S(2)}, u32[]{:S(2)}) async-start(bf16[16,2,896]{2,1,0:T(2,128)(2,1)} %combine.1), calls=%async_computation.4 | async-start | bytes 114688 | tf_op jit(solution)/shard_map/all_to_all | solution.py:282

commit v7 on v6

--- a/solution.py
+++ b/solution.py
@@ -13,8 +13,8 @@
 CAP = 4
 EP = ("yl", "x", "z")
 DP = ("yh", "c")
-COLUMN = ("yh", "c", "yl")
-PLANE = ("x", "z")
+LINE = ("z", "yh", "c")
+PLANE = ("yl", "x")
 BF = jnp.bfloat16
 F32 = jnp.float32
 ALL_VMEM = pltpu.CompilerParams(vmem_limit_bytes=60 * 1024 * 1024)
@@ -127,24 +127,52 @@
     )(hidden, routes, logits)
 
 
-def chosen_slots(yl, tail, slots):
+def chosen_slots(z, line, tail, slots):
     rows, top = tail.shape
     slot = iota((rows, slots), 1)
-    expert = (slot // (2 * CAP) + yl * (slots // (2 * CAP))).astype(F32)
+    expert = (slot // (CAP * line) * line + z).astype(F32)
     named = jnp.zeros((rows, slots), F32)
     for k in range(top):
         named = jnp.where(tail[:, k : k + 1] == expert, 1.0, named)
     this, other = iota((rows, rows), 0), iota((rows, rows), 1)
-    before = ((other < this) & (other // 2 % 2 == this // 2 % 2)).astype(F32)
+    group = rows // line
+    before = ((other < this) & (other // group == this // group)).astype(F32)
     earlier = dot(before.astype(BF), named.astype(BF))
     chosen = (named > 0) & (earlier == (slot % CAP).astype(F32))
-    return chosen & (slot % (2 * CAP) // CAP == iota((rows, slots), 0) // 2 % 2), expert
-
-
-def dispatch_kernel(top, yl_ref, tokens_ref, send_ref, held_ref, done):
+    return chosen & (slot // CAP % line == iota((rows, slots), 0) // group), expert
+
+
+def spread_kernel(tokens_ref, out_ref, held_ref, done):
+    blocks, requests, _ = tokens_ref.shape
+    for block in range(blocks):
+        held_ref[block * requests : (block + 1) * requests] = tokens_ref[block]
+    copies = [
+        pltpu.make_async_copy(held_ref, out_ref.at[peer], done.at[peer])
+        for peer in range(out_ref.shape[0])
+    ]
+    for copy in copies:
+        copy.start()
+    for copy in copies:
+        copy.wait()
+
+
+def spread(tokens, peers):
+    shape = (tokens.shape[0] * tokens.shape[1], tokens.shape[2])
+    return pl.pallas_call(
+        spread_kernel,
+        out_shape=jax.ShapeDtypeStruct((peers, *shape), BF),
+        in_specs=vmem(1),
+        out_specs=hbm(),
+        scratch_shapes=[pltpu.VMEM(shape, BF), pltpu.SemaphoreType.DMA((peers,))],
+        compiler_params=PARAMS,
+        name="spread",
+    )(tokens)
+
+
+def dispatch_kernel(line, top, z_ref, tokens_ref, send_ref, held_ref, done):
     peers, block, width = send_ref.shape
     tail = tokens_ref[:, width : width + top].astype(F32)
-    chosen, _ = chosen_slots(yl_ref[0], tail, peers * block)
+    chosen, _ = chosen_slots(z_ref[0], line, tail, peers * block)
     pick = chosen.astype(F32).astype(BF)
     copies = []
     group = 128 // block
@@ -160,9 +188,9 @@
         copy.wait()
 
 
-def dispatch(yl, top, tokens, peers, block, width):
-    return pl.pallas_call(
-        functools.partial(dispatch_kernel, top),
+def dispatch(z, line, top, tokens, peers, block, width):
+    return pl.pallas_call(
+        functools.partial(dispatch_kernel, line, top),
         out_shape=jax.ShapeDtypeStruct((peers, block, width), BF),
         in_specs=[pl.BlockSpec(memory_space=pltpu.SMEM), *vmem(1)],
         out_specs=hbm(),
@@ -172,16 +200,16 @@
         ],
         compiler_params=PARAMS,
         name="dispatch",
-    )(yl, tokens)
-
-
-def mix_kernel(yl_ref, tail_ref, mix_ref):
+    )(z, tokens)
+
+
+def mix_kernel(line, z_ref, tail_ref, mix_ref):
     slots = mix_ref.shape[1]
     tail = tail_ref[...].astype(F32)
     top = tail.shape[1] // 2
     sigmoid = jax.nn.sigmoid(tail[:, top:])
     gates = 2.5 * sigmoid / jnp.sum(sigmoid, 1, keepdims=True)
-    chosen, expert = chosen_slots(yl_ref[0], tail[:, :top], slots)
+    chosen, expert = chosen_slots(z_ref[0], line, tail[:, :top], slots)
     gate = jnp.zeros(chosen.shape, F32)
     for k in range(top):
         gate = jnp.where(tail[:, k : k + 1] == expert, gates[:, k : k + 1], gate)
@@ -190,15 +218,15 @@
     mix_ref[...] = jnp.concatenate(mix, 0).astype(BF)
 
 
-def mixing(yl, tail, slots):
-    return pl.pallas_call(
-        mix_kernel,
+def mixing(z, line, tail, slots):
+    return pl.pallas_call(
+        functools.partial(mix_kernel, line),
         out_shape=jax.ShapeDtypeStruct((2 * tail.shape[0], slots), BF),
         in_specs=[pl.BlockSpec(memory_space=pltpu.SMEM), *vmem(1)],
         out_specs=vmem(1)[0],
         compiler_params=PARAMS,
         name="mixing",
-    )(yl, tail)
+    )(z, tail)
 
 
 def hidden_kernel(rows_ref, own_ref, peer_ref, out_ref, held_ref, done):
@@ -301,42 +329,52 @@
     w_down,
 ):
     experts = lax.axis_size(EP)
-    yh_size, yl_size = lax.axis_size("yh"), lax.axis_size("yl")
-    peers = experts // yl_size
+    yh_size, line = lax.axis_size("yh"), lax.axis_size("z")
+    peers = experts // line
     own_rank = lax.axis_index(EP)
+    yh, z = lax.axis_index("yh"), lax.axis_index("z").reshape(1)
     steps, _, requests, width = hidden.shape
+    top = routes.shape[3]
     chunk = width // yh_size
-    block = yl_size * CAP
-    slots = peers * block
-
-    top = routes.shape[3]
-    yl = lax.axis_index("yl").reshape(1)
-
-    packed = pack(hidden, routes, route_logits, yh_size, yl_size)
-    tokens = exchange(packed, COLUMN)
+    slots = experts * CAP
+
+    block = slots // peers
+
+    tokens = exchange(pack(hidden, routes, route_logits, yh_size, 1), DP)
     own_w = jnp.concatenate([w_gate[0], w_up[0]], 1)
     served = attend(lengths[own_rank], queries, latent_cache, new_latent)
-    tokens, own_w, served0, served1 = lax.optimization_barrier((tokens, own_w, *served))
-    tokens = tokens.reshape(-1, tokens.shape[-1])
-    send = dispatch(yl, top, tokens, peers, block, width)
+    tokens, own_w, w_down, served0, served1 = lax.optimization_barrier(
+        (tokens, own_w, w_down, *served)
+    )
+    tokens, own_w, w_down = lax.optimization_barrier((spread(tokens, line), own_w, w_down))
+    tokens = exchange(tokens, "z").reshape(-1, width + 2 * top)
+
+    def columns(by):
+        return lax.dynamic_slice_in_dim(w_down[0], (yh + by) % yh_size * chunk, chunk, 1)
+
+    peer_w = shifted(own_w, "c", 1)
+    middle = yh_size // 2
+    across = shifted(columns(middle), "yh", middle)
+    far = shifted(served0, EP, experts // 2)
+    tokens, peer_w, across, far, w_down, served1 = lax.optimization_barrier(
+        (tokens, peer_w, across, far, w_down, served1)
+    )
+    send = dispatch(z, line, top, tokens, peers, block, width)
     arrived = exchange(send, PLANE).reshape(slots, width)
 
-    far = shifted(served0, EP, experts // 2)
     lower = shifted(served1, EP, 1)
     upper = shifted(served1, EP, -1)
-    mix = mixing(yl, tokens[:, width:], slots)
-    peer_w = shifted(own_w, "c", 1)
-    yh = lax.axis_index("yh")
-    sent = [
-        lax.dynamic_slice_in_dim(w_down[0], (yh + s) % yh_size * chunk, chunk, 1)
-        for s in range(yh_size)
-    ]
-    own_down = jnp.stack([shifted(x, "yh", s) if s else x for s, x in enumerate(sent)])
+    moved = [columns(0), *(shifted(columns(s), "yh", s) for s in range(1, yh_size) if s != middle)]
+    moved.insert(middle, across)
+    own_down = jnp.stack(moved)
+    mix = mixing(z, line, tokens[:, width:], slots)
+    arrived, own_down, mix, lower, upper = lax.optimization_barrier(
+        (arrived, own_down, mix, lower, upper)
+    )
+    h = hidden_units(arrived, own_w, peer_w, yh_size)
+    h, own_down = lax.optimization_barrier((h, own_down))
     peer_down = shifted(own_down, "c", 1)
-    arrived, peer_w, own_down, mix, far, lower, upper = lax.optimization_barrier(
-        (arrived, peer_w, own_down, mix, far, lower, upper)
-    )
-    h = exchange(hidden_units(arrived, own_w, peer_w, yh_size), "yh")
+    h = exchange(h, "yh")
     home = new_home[own_rank]
     result0 = jnp.where(home[0] == own_rank, served0, far)
     result1 = jnp.where(
@@ -347,10 +385,10 @@
     attended = jnp.stack([result0, result1], 1)[:, None]
 
     out = down(yh, h, own_down, peer_down)
-    back = exchange(out.reshape(peers, block, chunk), PLANE).reshape(slots, chunk)
-    final = exchange(combine(mix, back, requests), COLUMN)
-    final = final.reshape(yh_size, steps, yl_size, requests, chunk).astype(F32)
-    final = final.sum(2).astype(BF).transpose(1, 2, 0, 3)
+    back = exchange(out.reshape(peers, -1, chunk), PLANE).reshape(slots, chunk)
+    final = exchange(combine(mix, back, requests), LINE)
+    final = final.reshape(line, yh_size, steps, requests, chunk).astype(F32)
+    final = final.sum(0).astype(BF).transpose(1, 2, 0, 3)
     return attended, final.reshape(steps, 1, requests, width)
 
 

time: 150 us -> 180 us (1.20)
  blocking collectives: 0 us -> 18.2 us
  waiting for transfers between devices: 44.7 us -> 54.3 us
  starting transfers between devices: 80.8 us -> 74 us
  local copies, waits for them, and re-layouts: 6.25 us -> 12.6 us
  other arithmetic: 0.55 us -> 3.17 us
    ppermute x8, waiting for transfers between devices: 14.1 us -> 33.2 us  [shifted(): return lax.ppermute(x, axes, [(i, (i + by) % size) for i in range(size)])]
    all_to_all x0 -> x1, blocking collectives: none -> 18.2 us  [exchange(): return lax.all_to_all(x, axes, split_axis=0, concat_axis=0, tiled=True)]
    all_to_all x5, waiting for transfers between devices: 30.7 us -> 21.1 us  [exchange(): return lax.all_to_all(x, axes, split_axis=0, concat_axis=0, tiled=True)]
    all_to_all x5, starting transfers between devices: 48.4 us -> 41.4 us  [exchange(): return lax.all_to_all(x, axes, split_axis=0, concat_axis=0, tiled=True)]
    unnamed x29 -> x27, local copies, waits for them, and re-layouts: 3.68 us -> 8.98 us
    dynamic_slice x1 -> x2, local copies, waits for them, and re-layouts: 0.09 us -> 2.18 us  [columns(): lax.dynamic_slice_in_dim(w_down[0], (yh + by) % yh_size * chunk, chunk, 1)]
  transfers between devices with their start and end apart: 13 -> 13, of which waited for: 8 -> 5; matrix products, arithmetic and copies ran while one was open for 3% -> 5% of each run, Pallas kernels for 5% -> 2%
where the time goes in v7:
time: 180 us; the launch traced here: 179 us
  starting transfers between devices  74 us (41%)
  waiting for transfers between devices  54.3 us (30%)
  blocking collectives  18.2 us (10%)
  Pallas kernels  13.9 us (8%)
  local copies, waits for them, and re-layouts  12.6 us (7%)
  other arithmetic  3.17 us (2%)
  between operations  2.99 us (2%)
    all_to_all x5, starting transfers between devices, exchange(): return lax.all_to_all(x, axes, split_axis=0, concat_axis=0, tiled=True)  41.4 us
    ppermute x8, waiting for transfers between devices, shifted(): return lax.ppermute(x, axes, [(i, (i + by) % size) for i in range(size)])  33.2 us
    ppermute x8, starting transfers between devices, shifted(): return lax.ppermute(x, axes, [(i, (i + by) % size) for i in range(size)])  32.6 us
    all_to_all x5, waiting for transfers between devices, exchange(): return lax.all_to_all(x, axes, split_axis=0, concat_axis=0, tiled=True)  21.1 us
    all_to_all x1, blocking collectives, exchange(): return lax.all_to_all(x, axes, split_axis=0, concat_axis=0, tiled=True)  18.2 us
    unnamed x27, local copies, waits for them, and re-layouts  8.98 us
    pallas_call x1, Pallas kernels, hidden_units(): pl.pallas_call(hidden_kernel, out_shape=jax.ShapeDtypeStruct((peers, *sha...  3.9 us
  transfers between devices with their start and end apart: 13, of which 5 were waited for; matrix products, arithmetic and copies ran while one was open for 5% of the time, Pallas kernels for 2%

profile of v7, /device:TPU:1, one launch (start us, length us, event | category | flops | bytes accessed | tf_op | source)
XLA Modules:
  0.0 179.1 jit_solution(15585288389063324836)
XLA Ops:
  0.6 1.5 pack.1
  2.1 10.2 %all-to-all-start = ((bf16[8,2,3600]{2,1,0:T(2,128)(2,1)}), bf16[8,2,3600]{2,1,0:T(2,128)(2,1)S(1)}, u32[]{:S(2)}, u32[]{:S(2)}) async-start(bf16[8,2,3600]{2,1,0:T(2,128)(2,1)} %pack.1), calls=%async_computation | async-start | bytes 237568 | tf_op jit(solution)/shard_map/all_to_all | solution.py:310
  12.3 1.7 pad_maximum_fusion.own_ref
  14.0 0.0 copy-start.10
  14.1 0.0 copy-start.11
  14.1 1.1 copy.19.query_ref
  15.2 1.7 copy.20.cache_ref
  16.9 0.2 constant_dynamic-slice_fusion.2
  17.1 1.1 copy-done.2
  18.2 2.4 %attend.1 = (bf16[2,128,512]{2,1,0:T(8,128)(2,1)S(1)}, bf16[2,128,512]{2,1,0:T(8,128)(2,1)S(1)}) custom-call(s32[2]{0:T(128)S(1)} %get-tuple-element.60.len_ref, bf16[2,1,2,128,576]{4,3,2,1,0:T(8,128)(2,1)S(1)} %copy-done.2, bf16[1,2,512,576]{3,2,1,0:T(8,128)(2,1)S(1)} %copy.20.cache_ref, bf16[2,1,2,576]{3,2,1,0:T(2,128)(2,1)S(1)} %copy-done.5), custom_call_target="tpu_custom_call" | custom-call | tf_op jit(solution)/shard_map/attend/pallas_call | solution.py:66
  20.6 0.7 copy-done.3
  21.3 1.4 spread.1
  22.7 0.9 copy-done.1
  23.7 2.0 %collective-permute-start = (bf16[3584,256]{1,0:T(8,128)(2,1)S(1)}, bf16[3584,256]{1,0:T(8,128)(2,1)}, u32[]{:S(2)}, u32[]{:S(2)}) collective-permute-start(bf16[3584,256]{1,0:T(8,128)(2,1)S(1)} %pad_maximum_fusion.own_ref), channel_id=1, source_target_pairs={{0,64},{64,0},{1,65},{65,1},{2,66},{66,2},{3,67},{67,3},{4,68},{68... | collective-permute-start | bytes 5505032 | tf_op jit(solution)/shard_map/ppermute | solution.py:315
  25.7 8.4 %all-to-all-start.1 = ((bf16[8,16,3600]{2,1,0:T(8,128)(2,1)}), bf16[8,16,3600]{2,1,0:T(8,128)(2,1)S(1)}, u32[]{:S(2)}, u32[]{:S(2)}) async-start(bf16[8,16,3600]{2,1,0:T(8,128)(2,1)} %copy-done.1), calls=%async_computation.1 | async-start | bytes 1900544 | tf_op jit(solution)/shard_map/all_to_all | solution.py:310
  34.1 2.8 %collective-permute-start.2 = (bf16[2,128,512]{2,1,0:T(8,128)(2,1)S(1)}, bf16[2,128,512]{2,1,0:T(8,128)(2,1)}, u32[]{:S(2)}, u32[]{:S(2)}) collective-permute-start(bf16[2,128,512]{2,1,0:T(8,128)(2,1)S(1)} %copy-done.4), channel_id=1, source_target_pairs={{0,32},{1,33},{2,34},{3,35},{4,36},{5,37},{6,38},{7,39},{8,40},{9,... | collective-permute-start | bytes 786440 | tf_op jit(solution)/shard_map/ppermute | solution.py:315
  36.9 1.0 dynamic-slice_bitcast_fusion.2
  37.9 7.0 %collective-permute-start.1 = (bf16[128,896]{1,0:T(8,128)(2,1)S(1)}, bf16[128,896]{1,0:T(8,128)(2,1)S(1)}, u32[]{:S(2)}, u32[]{:S(2)}) collective-permute-start(bf16[128,896]{1,0:T(8,128)(2,1)S(1)} %dynamic-slice_bitcast_fusion.2), channel_id=1, source_target_pairs={{0,256},{128,384},{256,0},{384,128},{1,257},{129,385},{257,1},{385... | collective-permute-start | bytes 688136 | tf_op jit(solution)/shard_map/ppermute | solution.py:315
  44.9 12.9 %collective-permute-done.1 = bf16[128,896]{1,0:T(8,128)(2,1)S(1)} collective-permute-done((bf16[128,896]{1,0:T(8,128)(2,1)S(1)}, bf16[128,896]{1,0:T(8,128)(2,1)S(1)}, u32[]{:S(2)}, u32[]{:S(2)}) %collective-permute-start.1) | collective-permute-done | bytes 229408 | tf_op jit(solution)/shard_map/ppermute | solution.py:315
  57.8 0.7 copy-done.9
  58.5 2.7 %all-to-all-done.1 = bf16[8,16,3600]{2,1,0:T(8,128)(2,1)S(1)} async-done(((bf16[8,16,3600]{2,1,0:T(8,128)(2,1)}), bf16[8,16,3600]{2,1,0:T(8,128)(2,1)S(1)}, u32[]{:S(2)}, u32[]{:S(2)}) %all-to-all-start.1) | async-done | bytes 921632 | tf_op jit(solution)/shard_map/all_to_all | solution.py:310
  61.2 1.6 dispatch.1
  62.8 1.2 copy-done
  64.1 4.7 %all-to-all-start.2 = ((bf16[8,32,3584]{2,1,0:T(8,128)(2,1)}), bf16[8,32,3584]{2,1,0:T(8,128)(2,1)}, u32[]{:S(2)}, u32[]{:S(2)}) async-start(bf16[8,32,3584]{2,1,0:T(8,128)(2,1)} %copy-done), calls=%async_computation.2 | async-start | bytes 3670016 | tf_op jit(solution)/shard_map/all_to_all | solution.py:310
  68.8 1.2 constant_dynamic-slice_fusion
  70.0 5.4 %collective-permute-start.4 = (bf16[128,896]{1,0:T(8,128)(2,1)S(1)}, bf16[128,896]{1,0:T(8,128)(2,1)S(1)}, u32[]{:S(2)}, u32[]{:S(2)}) collective-permute-start(bf16[128,896]{1,0:T(8,128)(2,1)S(1)} %get-tuple-element.55), channel_id=1, source_target_pairs={{0,384},{128,0},{256,128},{384,256},{1,385},{129,1},{257,129},{385... | collective-permute-start | bytes 688136 | tf_op jit(solution)/shard_map/ppermute | solution.py:315
  75.5 1.9 %collective-permute-start.3 = (bf16[128,896]{1,0:T(8,128)(2,1)S(1)}, bf16[128,896]{1,0:T(8,128)(2,1)S(1)}, u32[]{:S(2)}, u32[]{:S(2)}) collective-permute-start(bf16[128,896]{1,0:T(8,128)(2,1)S(1)} %get-tuple-element.56), channel_id=1, source_target_pairs={{0,128},{128,256},{256,384},{384,0},{1,129},{129,257},{257,385},{3... | collective-permute-start | bytes 688136 | tf_op jit(solution)/shard_map/ppermute | solution.py:315
  77.4 1.9 %collective-permute-start.5 = (bf16[2,128,512]{2,1,0:T(8,128)(2,1)S(1)}, bf16[2,128,512]{2,1,0:T(8,128)(2,1)S(1)}, u32[]{:S(2)}, u32[]{:S(2)}) collective-permute-start(bf16[2,128,512]{2,1,0:T(8,128)(2,1)S(1)} %get-tuple-element.36), channel_id=1, source_target_pairs={{0,1},{1,2},{2,3},{3,4},{4,5},{5,6},{6,7},{7,8},{8,9},{9,10},{10,1... | collective-permute-start | bytes 786440 | tf_op jit(solution)/shard_map/ppermute | solution.py:315
  79.3 7.6 %collective-permute-start.6 = (bf16[2,128,512]{2,1,0:T(8,128)(2,1)S(1)}, bf16[2,128,512]{2,1,0:T(8,128)(2,1)}, u32[]{:S(2)}, u32[]{:S(2)}) collective-permute-start(bf16[2,128,512]{2,1,0:T(8,128)(2,1)S(1)} %get-tuple-element.36), channel_id=1, source_target_pairs={{0,63},{1,0},{2,1},{3,2},{4,3},{5,4},{6,5},{7,6},{8,7},{9,8},{10,9... | collective-permute-start | bytes 786440 | tf_op jit(solution)/shard_map/ppermute | solution.py:315
  86.9 0.5 mixing.1.mix_ref
  87.4 20.3 %collective-permute-done.3 = bf16[128,896]{1,0:T(8,128)(2,1)S(1)} collective-permute-done((bf16[128,896]{1,0:T(8,128)(2,1)S(1)}, bf16[128,896]{1,0:T(8,128)(2,1)S(1)}, u32[]{:S(2)}, u32[]{:S(2)}) %collective-permute-start.3) | collective-permute-done | bytes 229408 | tf_op jit(solution)/shard_map/ppermute | solution.py:315
  107.7 1.1 pad_maximum_fusion.1.own_ref
  108.8 0.7 copy-done.7
  109.5 3.9 %hidden_units.1 = bf16[4,256,256]{2,1,0:T(8,128)(2,1)S(1)} custom-call(bf16[256,3584]{1,0:T(8,128)(2,1)} %bitcast.8.rows_ref, bf16[3584,256]{1,0:T(8,128)(2,1)S(1)} %pad_maximum_fusion.own_ref, bf16[3584,256]{1,0:T(8,128)(2,1)} %collective-permute-done.peer_ref), custom_call_target="tpu_custom_call" | custom-call | tf_op jit(solution)/shard_map/hidden_units/pallas_call | solution.py:252
  113.4 3.9 %collective-permute-start.7 = (bf16[4,128,896]{2,1,0:T(8,128)(2,1)S(1)}, bf16[4,128,896]{2,1,0:T(8,128)(2,1)S(1)}, u32[]{:S(2)}, u32[]{:S(2)}) collective-permute-start(bf16[4,128,896]{2,1,0:T(8,128)(2,1)S(1)} %pad_maximum_fusion.1.own_ref), channel_id=1, source_target_pairs={{0,64},{64,0},{1,65},{65,1},{2,66},{66,2},{3,67},{67,3},{4,68},{68... | collective-permute-start | bytes 2752520 | tf_op jit(solution)/shard_map/ppermute | solution.py:315
  117.3 18.2 %all_to_all.30.h_ref = bf16[4,256,256]{2,1,0:T(8,128)(2,1)S(1)} all-to-all(bf16[4,256,256]{2,1,0:T(8,128)(2,1)S(1)} %hidden_units.1), channel_id=1, replica_groups=mesh['yh'=4,'c'=2,'yl'=2,'x'=4,'z'=8] {'yh'}, dimensions={0} | all-to-all | bytes 1048576 | tf_op jit(solution)/shard_map/all_to_all | solution.py:310
  135.5 1.5 down.1
  137.0 6.0 %all-to-all-start.4 = ((bf16[8,32,896]{2,1,0:T(8,128)(2,1)}), bf16[8,32,896]{2,1,0:T(8,128)(2,1)S(1)}, u32[]{:S(2)}, u32[]{:S(2)}) async-start(bf16[8,32,896]{2,1,0:T(8,128)(2,1)} %bitcast.17), calls=%async_computation.4 | async-start | bytes 917504 | tf_op jit(solution)/shard_map/all_to_all | solution.py:310
  143.0 0.6 fusion.1
  145.6 4.5 %all-to-all-done.4 = bf16[8,32,896]{2,1,0:T(8,128)(2,1)S(1)} async-done(((bf16[8,32,896]{2,1,0:T(8,128)(2,1)}), bf16[8,32,896]{2,1,0:T(8,128)(2,1)S(1)}, u32[]{:S(2)}, u32[]{:S(2)}) %all-to-all-start.4) | async-done | bytes 458784 | tf_op jit(solution)/shard_map/all_to_all | solution.py:310
  150.1 1.0 combine.1
  151.1 12.1 %all-to-all-start.5 = ((bf16[64,2,896]{2,1,0:T(2,128)(2,1)}), bf16[64,2,896]{2,1,0:T(2,128)(2,1)S(1)}, u32[]{:S(2)}, u32[]{:S(2)}) async-start(bf16[64,2,896]{2,1,0:T(2,128)(2,1)} %combine.1), calls=%async_computation.5 | async-start | bytes 458752 | tf_op jit(solution)/shard_map/all_to_all | solution.py:310
  163.3 0.1 select_bitcast_fusion
  163.4 0.1 maximum_bitcast_fusion
  163.5 0.8 copy.22
  164.3 14.0 %all-to-all-done.5 = bf16[64,2,896]{2,1,0:T(2,128)(2,1)S(1)} async-done(((bf16[64,2,896]{2,1,0:T(2,128)(2,1)}), bf16[64,2,896]{2,1,0:T(2,128)(2,1)S(1)}, u32[]{:S(2)}, u32[]{:S(2)}) %all-to-all-start.5) | async-done | bytes 229408 | tf_op jit(solution)/shard_map/all_to_all | solution.py:310
  178.3 0.2 reduce_sum.12
  178.5 0.6 reshape.44
  (27 shorter events, 0.1 us)
Async XLA Ops:
  2.1 19.2 %all-to-all-start = ((bf16[8,2,3600]{2,1,0:T(2,128)(2,1)}), bf16[8,2,3600]{2,1,0:T(2,128)(2,1)S(1)}, u32[]{:S(2)}, u32[]{:S(2)}) async-start(bf16[8,2,3600]{2,1,0:T(2,128)(2,1)} %pack.1), calls=%async_computation | async-start | bytes 237568 | tf_op jit(solution)/shard_map/all_to_all | solution.py:310
  12.3 1.7 copy-start.6
  14.0 2.8 %copy-start.10 = (s32[64,2]{0,1:T(2,128)S(1)}, s32[64,2]{0,1:T(2,128)}, u32[]{:S(2)}) copy-start(s32[64,2]{0,1:T(2,128)} %param.13) | copy-start | bytes 1540
  14.1 2.8 %copy-start.11 = (s32[64,2]{0,1:T(2,128)S(1)}, s32[64,2]{0,1:T(2,128)}, u32[]{:S(2)}) copy-start(s32[64,2]{0,1:T(2,128)} %param.12) | copy-start | bytes 1540
  14.1 3.0 %copy-start.5 = (bf16[2,1,2,576]{3,2,1,0:T(2,128)(2,1)S(1)}, bf16[2,1,2,576]{3,2,1,0:T(2,128)(2,1)}, u32[]{:S(2)}) copy-start(bf16[2,1,2,576]{3,2,1,0:T(2,128)(2,1)} %fresh_ref.1) | copy-start | bytes 13828
  17.1 1.1 copy-start.2
  20.6 0.7 copy-start.3
  21.3 12.8 %copy-start.4 = (bf16[2,128,512]{2,1,0:T(8,128)(2,1)S(1)}, bf16[2,128,512]{2,1,0:T(8,128)(2,1)}, u32[]{:S(2)}) copy-start(bf16[2,128,512]{2,1,0:T(8,128)(2,1)} %copy-done.3) | copy-start | bytes 786436
  22.7 1.0 copy-start.1
  23.7 37.5 %collective-permute-start = (bf16[3584,256]{1,0:T(8,128)(2,1)S(1)}, bf16[3584,256]{1,0:T(8,128)(2,1)}, u32[]{:S(2)}, u32[]{:S(2)}) collective-permute-start(bf16[3584,256]{1,0:T(8,128)(2,1)S(1)} %pad_maximum_fusion.own_ref), channel_id=1, source_target_pairs={{0,64},{64,0},{1,65},{65,1},{2,66},{66,2},{3,67},{67,3},{4,68},{68... | collective-permute-start | bytes 5505032 | tf_op jit(solution)/shard_map/ppermute | solution.py:315
  25.7 35.5 %all-to-all-start.1 = ((bf16[8,16,3600]{2,1,0:T(8,128)(2,1)}), bf16[8,16,3600]{2,1,0:T(8,128)(2,1)S(1)}, u32[]{:S(2)}, u32[]{:S(2)}) async-start(bf16[8,16,3600]{2,1,0:T(8,128)(2,1)} %copy-done.1), calls=%async_computation.1 | async-start | bytes 1900544 | tf_op jit(solution)/shard_map/all_to_all | solution.py:310
  34.1 24.4 %collective-permute-start.2 = (bf16[2,128,512]{2,1,0:T(8,128)(2,1)S(1)}, bf16[2,128,512]{2,1,0:T(8,128)(2,1)}, u32[]{:S(2)}, u32[]{:S(2)}) collective-permute-start(bf16[2,128,512]{2,1,0:T(8,128)(2,1)S(1)} %copy-done.4), channel_id=1, source_target_pairs={{0,32},{1,33},{2,34},{3,35},{4,36},{5,37},{6,38},{7,39},{8,40},{9,... | collective-permute-start | bytes 786440 | tf_op jit(solution)/shard_map/ppermute | solution.py:315
  37.9 19.9 %collective-permute-start.1 = (bf16[128,896]{1,0:T(8,128)(2,1)S(1)}, bf16[128,896]{1,0:T(8,128)(2,1)S(1)}, u32[]{:S(2)}, u32[]{:S(2)}) collective-permute-start(bf16[128,896]{1,0:T(8,128)(2,1)S(1)} %dynamic-slice_bitcast_fusion.2), channel_id=1, source_target_pairs={{0,256},{128,384},{256,0},{384,128},{1,257},{129,385},{257,1},{385... | collective-permute-start | bytes 688136 | tf_op jit(solution)/shard_map/ppermute | solution.py:315
  57.8 0.7 copy-start.9
  62.8 1.2 copy-start
  64.1 45.4 %all-to-all-start.2 = ((bf16[8,32,3584]{2,1,0:T(8,128)(2,1)}), bf16[8,32,3584]{2,1,0:T(8,128)(2,1)}, u32[]{:S(2)}, u32[]{:S(2)}) async-start(bf16[8,32,3584]{2,1,0:T(8,128)(2,1)} %copy-done), calls=%async_computation.2 | async-start | bytes 3670016 | tf_op jit(solution)/shard_map/all_to_all | solution.py:310
  70.0 17.4 %collective-permute-start.4 = (bf16[128,896]{1,0:T(8,128)(2,1)S(1)}, bf16[128,896]{1,0:T(8,128)(2,1)S(1)}, u32[]{:S(2)}, u32[]{:S(2)}) collective-permute-start(bf16[128,896]{1,0:T(8,128)(2,1)S(1)} %get-tuple-element.55), channel_id=1, source_target_pairs={{0,384},{128,0},{256,128},{384,256},{1,385},{129,1},{257,129},{385... | collective-permute-start | bytes 688136 | tf_op jit(solution)/shard_map/ppermute | solution.py:315
  75.5 32.3 %collective-permute-start.3 = (bf16[128,896]{1,0:T(8,128)(2,1)S(1)}, bf16[128,896]{1,0:T(8,128)(2,1)S(1)}, u32[]{:S(2)}, u32[]{:S(2)}) collective-permute-start(bf16[128,896]{1,0:T(8,128)(2,1)S(1)} %get-tuple-element.56), channel_id=1, source_target_pairs={{0,128},{128,256},{256,384},{384,0},{1,129},{129,257},{257,385},{3... | collective-permute-start | bytes 688136 | tf_op jit(solution)/shard_map/ppermute | solution.py:315
  77.4 31.4 %collective-permute-start.5 = (bf16[2,128,512]{2,1,0:T(8,128)(2,1)S(1)}, bf16[2,128,512]{2,1,0:T(8,128)(2,1)S(1)}, u32[]{:S(2)}, u32[]{:S(2)}) collective-permute-start(bf16[2,128,512]{2,1,0:T(8,128)(2,1)S(1)} %get-tuple-element.36), channel_id=1, source_target_pairs={{0,1},{1,2},{2,3},{3,4},{4,5},{5,6},{6,7},{7,8},{8,9},{9,10},{10,1... | collective-permute-start | bytes 786440 | tf_op jit(solution)/shard_map/ppermute | solution.py:315
  79.3 30.2 %collective-permute-start.6 = (bf16[2,128,512]{2,1,0:T(8,128)(2,1)S(1)}, bf16[2,128,512]{2,1,0:T(8,128)(2,1)}, u32[]{:S(2)}, u32[]{:S(2)}) collective-permute-start(bf16[2,128,512]{2,1,0:T(8,128)(2,1)S(1)} %get-tuple-element.36), channel_id=1, source_target_pairs={{0,63},{1,0},{2,1},{3,2},{4,3},{5,4},{6,5},{7,6},{8,7},{9,8},{10,9... | collective-permute-start | bytes 786440 | tf_op jit(solution)/shard_map/ppermute | solution.py:315
  108.8 0.7 copy-start.7
  113.4 22.1 %collective-permute-start.7 = (bf16[4,128,896]{2,1,0:T(8,128)(2,1)S(1)}, bf16[4,128,896]{2,1,0:T(8,128)(2,1)S(1)}, u32[]{:S(2)}, u32[]{:S(2)}) collective-permute-start(bf16[4,128,896]{2,1,0:T(8,128)(2,1)S(1)} %pad_maximum_fusion.1.own_ref), channel_id=1, source_target_pairs={{0,64},{64,0},{1,65},{65,1},{2,66},{66,2},{3,67},{67,3},{4,68},{68... | collective-permute-start | bytes 2752520 | tf_op jit(solution)/shard_map/ppermute | solution.py:315
  137.0 26.3 %copy-start.8 = (bf16[2,128,512]{2,1,0:T(8,128)(2,1)S(1)}, bf16[2,128,512]{2,1,0:T(8,128)(2,1)}, u32[]{:S(2)}) copy-start(bf16[2,128,512]{2,1,0:T(8,128)(2,1)} %copy-done.7) | copy-start | bytes 786436
  137.0 13.1 %all-to-all-start.4 = ((bf16[8,32,896]{2,1,0:T(8,128)(2,1)}), bf16[8,32,896]{2,1,0:T(8,128)(2,1)S(1)}, u32[]{:S(2)}, u32[]{:S(2)}) async-start(bf16[8,32,896]{2,1,0:T(8,128)(2,1)} %bitcast.17), calls=%async_computation.4 | async-start | bytes 917504 | tf_op jit(solution)/shard_map/all_to_all | solution.py:310
  151.1 27.1 %all-to-all-start.5 = ((bf16[64,2,896]{2,1,0:T(2,128)(2,1)}), bf16[64,2,896]{2,1,0:T(2,128)(2,1)S(1)}, u32[]{:S(2)}, u32[]{:S(2)}) async-start(bf16[64,2,896]{2,1,0:T(2,128)(2,1)} %combine.1), calls=%async_computation.5 | async-start | bytes 458752 | tf_op jit(solution)/shard_map/all_to_all | solution.py:310

commit v8 on v6

--- a/solution.py
+++ b/solution.py
@@ -322,8 +322,6 @@
     arrived = exchange(send, PLANE).reshape(slots, width)
 
     far = shifted(served0, EP, experts // 2)
-    lower = shifted(served1, EP, 1)
-    upper = shifted(served1, EP, -1)
     mix = mixing(yl, tokens[:, width:], slots)
     peer_w = shifted(own_w, "c", 1)
     yh = lax.axis_index("yh")
@@ -333,10 +331,20 @@
     ]
     own_down = jnp.stack([shifted(x, "yh", s) if s else x for s, x in enumerate(sent)])
     peer_down = shifted(own_down, "c", 1)
-    arrived, peer_w, own_down, mix, far, lower, upper = lax.optimization_barrier(
-        (arrived, peer_w, own_down, mix, far, lower, upper)
+    arrived, peer_w, own_down, mix, far = lax.optimization_barrier(
+        (arrived, peer_w, own_down, mix, far)
     )
     h = exchange(hidden_units(arrived, own_w, peer_w, yh_size), "yh")
+    h, served1 = lax.optimization_barrier((h, served1))
+    lower = shifted(served1, EP, 1)
+    upper = shifted(served1, EP, -1)
+    out = down(yh, h, own_down, peer_down)
+    back = exchange(out.reshape(peers, block, chunk), PLANE).reshape(slots, chunk)
+    mixed, served1 = lax.optimization_barrier((combine(mix, back, requests), served1))
+    final = exchange(mixed, COLUMN)
+    final = final.reshape(yh_size, steps, yl_size, requests, chunk).astype(F32)
+    final = final.sum(2).astype(BF).transpose(1, 2, 0, 3)
+
     home = new_home[own_rank]
     result0 = jnp.where(home[0] == own_rank, served0, far)
     result1 = jnp.where(
@@ -345,12 +353,6 @@
         jnp.where(home[1] == (own_rank + 1) % experts, upper, lower),
     )
     attended = jnp.stack([result0, result1], 1)[:, None]
-
-    out = down(yh, h, own_down, peer_down)
-    back = exchange(out.reshape(peers, block, chunk), PLANE).reshape(slots, chunk)
-    final = exchange(combine(mix, back, requests), COLUMN)
-    final = final.reshape(yh_size, steps, yl_size, requests, chunk).astype(F32)
-    final = final.sum(2).astype(BF).transpose(1, 2, 0, 3)
     return attended, final.reshape(steps, 1, requests, width)
 
 

time: 150 us -> 145 us (0.967)
  blocking collectives: 0 us -> 17.4 us
  waiting for transfers between devices: 44.7 us -> 27.8 us
  starting transfers between devices: 80.8 us -> 74.1 us
    all_to_all x0 -> x1, blocking collectives: none -> 17.4 us  [exchange(): return lax.all_to_all(x, axes, split_axis=0, concat_axis=0, tiled=True)]
    all_to_all x5 -> x4, waiting for transfers between devices: 30.7 us -> 17.4 us  [exchange(): return lax.all_to_all(x, axes, split_axis=0, concat_axis=0, tiled=True)]
    all_to_all x5 -> x4, starting transfers between devices: 48.4 us -> 42.8 us  [exchange(): return lax.all_to_all(x, axes, split_axis=0, concat_axis=0, tiled=True)]
    ppermute x8, waiting for transfers between devices: 14.1 us -> 10.3 us  [shifted(): return lax.ppermute(x, axes, [(i, (i + by) % size) for i in range(size)])]
    unnamed x29 -> x15, local copies, waits for them, and re-layouts: 3.68 us -> 4.6 us
  transfers between devices with their start and end apart: 13 -> 12, of which waited for: 8 -> 8; matrix products, arithmetic and copies ran while one was open for 3% -> 5% of each run, Pallas kernels for 5% -> 5%
where the time goes in v8:
time: 145 us; the launch traced here: 144 us
  starting transfers between devices  74.1 us (51%)
  waiting for transfers between devices  27.8 us (19%)
  blocking collectives  17.4 us (12%)
  Pallas kernels  13.7 us (9%)
  local copies, waits for them, and re-layouts  6.21 us (4%)
  between operations  2.75 us (2%)
  other arithmetic  1.98 us (1%)
    all_to_all x4, starting transfers between devices, exchange(): return lax.all_to_all(x, axes, split_axis=0, concat_axis=0, tiled=True)  42.8 us
    ppermute x8, starting transfers between devices, shifted(): return lax.ppermute(x, axes, [(i, (i + by) % size) for i in range(size)])  31.3 us
    all_to_all x4, waiting for transfers between devices, exchange(): return lax.all_to_all(x, axes, split_axis=0, concat_axis=0, tiled=True)  17.4 us
    all_to_all x1, blocking collectives, exchange(): return lax.all_to_all(x, axes, split_axis=0, concat_axis=0, tiled=True)  17.4 us
    ppermute x8, waiting for transfers between devices, shifted(): return lax.ppermute(x, axes, [(i, (i + by) % size) for i in range(size)])  10.3 us
    unnamed x15, local copies, waits for them, and re-layouts  4.6 us
    pallas_call x1, Pallas kernels, hidden_units(): pl.pallas_call(hidden_kernel, out_shape=jax.ShapeDtypeStruct((peers, *sha...  3.9 us
  transfers between devices with their start and end apart: 12, of which 8 were waited for; matrix products, arithmetic and copies ran while one was open for 5% of the time, Pallas kernels for 5%

profile of v8, /device:TPU:1, one launch (start us, length us, event | category | flops | bytes accessed | tf_op | source)
XLA Modules:
  0.0 143.9 jit_solution(4248684341187151486)
XLA Ops:
  0.6 1.5 %pack.1 = bf16[16,2,3600]{2,1,0:T(2,128)(2,1)} custom-call(bf16[2,1,2,3584]{3,2,1,0:T(2,128)(2,1)} %hidden_ref.1, s32[2,1,2,8]{3,2,1,0:T(2,128)} %routes_ref.1, bf16[2,1,2,8]{3,2,1,0:T(2,128)(2,1)} %logits_ref.1), custom_call_target="tpu_custom_call" | custom-call | tf_op jit(solution)/shard_map/pack/pallas_call | solution.py:113
  2.2 10.2 %all-to-all-start = ((bf16[16,2,3600]{2,1,0:T(2,128)(2,1)}), bf16[16,2,3600]{2,1,0:T(2,128)(2,1)S(1)}, u32[]{:S(2)}, u32[]{:S(2)}) async-start(bf16[16,2,3600]{2,1,0:T(2,128)(2,1)} %pack.1), calls=%async_computation | async-start | bytes 475136 | tf_op jit(solution)/shard_map/all_to_all | solution.py:282
  12.4 0.0 copy-start.5
  12.4 0.0 copy-start
  12.4 1.7 %copy.20.cache_ref = bf16[1,2,512,576]{3,2,1,0:T(8,128)(2,1)S(1)} copy(bf16[1,2,512,576]{2,3,1,0:T(8,128)(2,1)} %param.11) | data formatting | bytes 2359296 | tf_op args[0]
  14.1 1.4 copy.19.query_ref
  15.5 0.2 constant_dynamic-slice_fusion.2
  15.7 2.5 %attend.1 = (bf16[2,128,512]{2,1,0:T(8,128)(2,1)S(1)}, bf16[2,128,512]{2,1,0:T(8,128)(2,1)S(1)}) custom-call(s32[2]{0:T(128)S(1)} %get-tuple-element.45.len_ref, bf16[2,1,2,128,576]{4,3,2,1,0:T(8,128)(2,1)S(1)} %copy.19.query_ref, bf16[1,2,512,576]{3,2,1,0:T(8,128)(2,1)S(1)} %copy.20.cache_ref, bf16[2,1,2,576]{3,2,1,0:T(2,128)(2,1)S(1)} %copy-done), custom_call_target="tpu_custom_call" | custom-call | tf_op jit(solution)/shard_map/attend/pallas_call | solution.py:66
  18.2 1.7 %pad_maximum_fusion.own_ref = bf16[3584,256]{1,0:T(8,128)(2,1)S(1)} fusion(bf16[3584,128]{1,0:T(8,128)(2,1)} %bitcast.29, bf16[3584,128]{1,0:T(8,128)(2,1)} %bitcast.30), kind=kLoop, calls=%fused_computation | loop fusion | flops 3670016 | bytes 3670016 | tf_op jit(solution)/shard_map/concatenate | solution.py:317
  19.8 2.3 %all-to-all-done = bf16[16,2,3600]{2,1,0:T(2,128)(2,1)S(1)} async-done(((bf16[16,2,3600]{2,1,0:T(2,128)(2,1)}), bf16[16,2,3600]{2,1,0:T(2,128)(2,1)S(1)}, u32[]{:S(2)}, u32[]{:S(2)}) %all-to-all-start) | async-done | bytes 230432 | tf_op jit(solution)/shard_map/all_to_all | solution.py:282
  22.1 0.2 reshape.38.tokens_ref
  22.3 1.9 %dispatch.1 = bf16[32,8,3584]{2,1,0:T(8,128)(2,1)} custom-call(s32[1]{0:T(128)} %bitcast.3.yl_ref, bf16[32,3600]{1,0:T(8,128)(2,1)S(1)} %reshape.38.tokens_ref), custom_call_target="tpu_custom_call" | custom-call | tf_op jit(solution)/shard_map/dispatch/pallas_call | solution.py:164
  24.2 0.0 copy-start.1
  24.2 11.5 %all-to-all-start.1 = ((bf16[32,8,3584]{2,1,0:T(8,128)(2,1)}), bf16[32,8,3584]{2,1,0:T(8,128)(2,1)}, u32[]{:S(2)}, u32[]{:S(2)}) async-start(bf16[32,8,3584]{2,1,0:T(8,128)(2,1)} %dispatch.1), calls=%async_computation.1 | async-start | bytes 3670016 | tf_op jit(solution)/shard_map/all_to_all | solution.py:282
  35.7 2.6 %collective-permute-start = (bf16[3584,256]{1,0:T(8,128)(2,1)S(1)}, bf16[3584,256]{1,0:T(8,128)(2,1)}, u32[]{:S(2)}, u32[]{:S(2)}) collective-permute-start(bf16[3584,256]{1,0:T(8,128)(2,1)S(1)} %pad_maximum_fusion.own_ref), channel_id=1, source_target_pairs={{0,64},{64,0},{1,65},{65,1},{2,66},{66,2},{3,67},{67,3},{4,68},{68... | collective-permute-start | bytes 5505032 | tf_op jit(solution)/shard_map/ppermute | solution.py:287
  38.3 0.1 constant_dynamic-slice_fusion
  38.4 3.6 %collective-permute-start.3 = (bf16[128,896]{1,0:T(8,128)(2,1)S(1)}, bf16[128,896]{1,0:T(8,128)(2,1)S(1)}, u32[]{:S(2)}, u32[]{:S(2)}) collective-permute-start(bf16[128,896]{1,0:T(8,128)(2,1)S(1)} %get-tuple-element.40), channel_id=1, source_target_pairs={{0,384},{128,0},{256,128},{384,256},{1,385},{129,1},{257,129},{385... | collective-permute-start | bytes 688136 | tf_op jit(solution)/shard_map/ppermute | solution.py:287
  42.0 2.6 %collective-permute-start.1 = (bf16[128,896]{1,0:T(8,128)(2,1)S(1)}, bf16[128,896]{1,0:T(8,128)(2,1)S(1)}, u32[]{:S(2)}, u32[]{:S(2)}) collective-permute-start(bf16[128,896]{1,0:T(8,128)(2,1)S(1)} %get-tuple-element.39), channel_id=1, source_target_pairs={{0,128},{128,256},{256,384},{384,0},{1,129},{129,257},{257,385},{3... | collective-permute-start | bytes 688136 | tf_op jit(solution)/shard_map/ppermute | solution.py:287
  44.6 5.0 %collective-permute-start.2 = (bf16[128,896]{1,0:T(8,128)(2,1)S(1)}, bf16[128,896]{1,0:T(8,128)(2,1)S(1)}, u32[]{:S(2)}, u32[]{:S(2)}) collective-permute-start(bf16[128,896]{1,0:T(8,128)(2,1)S(1)} %get-tuple-element.41), channel_id=1, source_target_pairs={{0,256},{128,384},{256,0},{384,128},{1,257},{129,385},{257,1},{385... | collective-permute-start | bytes 688136 | tf_op jit(solution)/shard_map/ppermute | solution.py:287
  49.6 2.4 %collective-permute-start.4 = (bf16[2,128,512]{2,1,0:T(8,128)(2,1)S(1)}, bf16[2,128,512]{2,1,0:T(8,128)(2,1)S(1)}, u32[]{:S(2)}, u32[]{:S(2)}) collective-permute-start(bf16[2,128,512]{2,1,0:T(8,128)(2,1)S(1)} %get-tuple-element.19), channel_id=1, source_target_pairs={{0,32},{1,33},{2,34},{3,35},{4,36},{5,37},{6,38},{7,39},{8,40},{9,... | collective-permute-start | bytes 786440 | tf_op jit(solution)/shard_map/ppermute | solution.py:287
  52.0 1.5 %collective-permute-done.3 = bf16[128,896]{1,0:T(8,128)(2,1)S(1)} collective-permute-done((bf16[128,896]{1,0:T(8,128)(2,1)S(1)}, bf16[128,896]{1,0:T(8,128)(2,1)S(1)}, u32[]{:S(2)}, u32[]{:S(2)}) %collective-permute-start.3) | collective-permute-done | bytes 229408 | tf_op jit(solution)/shard_map/ppermute | solution.py:287
  53.6 0.6 collective-permute-done.1
  54.2 4.8 %collective-permute-done.2 = bf16[128,896]{1,0:T(8,128)(2,1)S(1)} collective-permute-done((bf16[128,896]{1,0:T(8,128)(2,1)S(1)}, bf16[128,896]{1,0:T(8,128)(2,1)S(1)}, u32[]{:S(2)}, u32[]{:S(2)}) %collective-permute-start.2) | collective-permute-done | bytes 229408 | tf_op jit(solution)/shard_map/ppermute | solution.py:287
  59.0 0.1 pad_maximum_fusion.1.own_ref
  59.1 6.9 %collective-permute-start.5 = (bf16[4,128,896]{2,1,0:T(8,128)(2,1)S(1)}, bf16[4,128,896]{2,1,0:T(8,128)(2,1)}, u32[]{:S(2)}, u32[]{:S(2)}) collective-permute-start(bf16[4,128,896]{2,1,0:T(8,128)(2,1)S(1)} %pad_maximum_fusion.1.own_ref), channel_id=1, source_target_pairs={{0,64},{64,0},{1,65},{65,1},{2,66},{66,2},{3,67},{67,3},{4,68},{68... | collective-permute-start | bytes 2752520 | tf_op jit(solution)/shard_map/ppermute | solution.py:287
  66.0 0.3 mixing.1.mix_ref
  66.4 3.4 %collective-permute-done.4 = bf16[2,128,512]{2,1,0:T(8,128)(2,1)S(1)} collective-permute-done((bf16[2,128,512]{2,1,0:T(8,128)(2,1)S(1)}, bf16[2,128,512]{2,1,0:T(8,128)(2,1)S(1)}, u32[]{:S(2)}, u32[]{:S(2)}) %collective-permute-start.4) | collective-permute-done | bytes 262176 | tf_op jit(solution)/shard_map/ppermute | solution.py:287
  69.7 0.7 copy-done.2
  70.4 0.0 collective-permute-done.peer_ref
  70.4 8.3 %all-to-all-done.1 = bf16[32,8,3584]{2,1,0:T(8,128)(2,1)} async-done(((bf16[32,8,3584]{2,1,0:T(8,128)(2,1)}), bf16[32,8,3584]{2,1,0:T(8,128)(2,1)}, u32[]{:S(2)}, u32[]{:S(2)}) %all-to-all-start.1) | async-done | bytes 1835040 | tf_op jit(solution)/shard_map/all_to_all | solution.py:282
  78.7 3.9 %hidden_units.1 = bf16[4,256,256]{2,1,0:T(8,128)(2,1)S(1)} custom-call(bf16[256,3584]{1,0:T(8,128)(2,1)} %bitcast.4.rows_ref, bf16[3584,256]{1,0:T(8,128)(2,1)S(1)} %pad_maximum_fusion.own_ref, bf16[3584,256]{1,0:T(8,128)(2,1)} %collective-permute-done.peer_ref), custom_call_target="tpu_custom_call" | custom-call | tf_op jit(solution)/shard_map/hidden_units/pallas_call | solution.py:224
  82.6 17.4 %all_to_all.25.h_ref = bf16[4,256,256]{2,1,0:T(8,128)(2,1)S(1)} all-to-all(bf16[4,256,256]{2,1,0:T(8,128)(2,1)S(1)} %hidden_units.1), channel_id=1, replica_groups=mesh['yh'=4,'c'=2,'yl'=2,'x'=4,'z'=8] {'yh'}, dimensions={0} | all-to-all | bytes 1048576 | tf_op jit(solution)/shard_map/all_to_all | solution.py:282
  100.0 0.0 collective-permute-done.5.peer_ref
  100.0 2.7 %down.1 = bf16[256,896]{1,0:T(8,128)(2,1)} custom-call(s32[1]{0:T(128)} %bitcast.13.yh_ref, bf16[4,256,256]{2,1,0:T(8,128)(2,1)S(1)} %all_to_all.25.h_ref, bf16[4,128,896]{2,1,0:T(8,128)(2,1)S(1)} %pad_maximum_fusion.1.own_ref, bf16[4,128,896]{2,1,0:T(8,128)(2,1)} %collective-permute-done.5.peer_ref), custom_call_target="tpu_custom_call" | custom-call | tf_op jit(solution)/shard_map/down/pallas_call | solution.py:246
  102.8 9.1 %all-to-all-start.3 = ((bf16[32,8,896]{2,1,0:T(8,128)(2,1)}), bf16[32,8,896]{2,1,0:T(8,128)(2,1)S(1)}, u32[]{:S(2)}, u32[]{:S(2)}) async-start(bf16[32,8,896]{2,1,0:T(8,128)(2,1)} %bitcast.14), calls=%async_computation.3 | async-start | bytes 917504 | tf_op jit(solution)/shard_map/all_to_all | solution.py:282
  111.9 6.4 %collective-permute-start.6 = (bf16[2,128,512]{2,1,0:T(8,128)(2,1)S(1)}, bf16[2,128,512]{2,1,0:T(8,128)(2,1)S(1)}, u32[]{:S(2)}, u32[]{:S(2)}) collective-permute-start(bf16[2,128,512]{2,1,0:T(8,128)(2,1)S(1)} %get-tuple-element.30), channel_id=1, source_target_pairs={{0,63},{1,0},{2,1},{3,2},{4,3},{5,4},{6,5},{7,6},{8,7},{9,8},{10,9... | collective-permute-start | bytes 786440 | tf_op jit(solution)/shard_map/ppermute | solution.py:287
  118.3 1.9 %collective-permute-start.7 = (bf16[2,128,512]{2,1,0:T(8,128)(2,1)S(1)}, bf16[2,128,512]{2,1,0:T(8,128)(2,1)S(1)}, u32[]{:S(2)}, u32[]{:S(2)}) collective-permute-start(bf16[2,128,512]{2,1,0:T(8,128)(2,1)S(1)} %get-tuple-element.30), channel_id=1, source_target_pairs={{0,1},{1,2},{2,3},{3,4},{4,5},{5,6},{6,7},{7,8},{8,9},{9,10},{10,1... | collective-permute-start | bytes 786440 | tf_op jit(solution)/shard_map/ppermute | solution.py:287
  120.2 0.5 fusion.1
  122.6 0.3 all-to-all-done.3
  122.8 0.8 combine.1
  123.7 11.9 %all-to-all-start.4 = ((bf16[16,2,896]{2,1,0:T(2,128)(2,1)}), bf16[16,2,896]{2,1,0:T(2,128)(2,1)S(1)}, u32[]{:S(2)}, u32[]{:S(2)}) async-start(bf16[16,2,896]{2,1,0:T(2,128)(2,1)} %combine.1), calls=%async_computation.4 | async-start | bytes 114688 | tf_op jit(solution)/shard_map/all_to_all | solution.py:282
  135.6 0.0 collective-permute-done.6
  135.6 0.0 collective-permute-done.7
  135.7 0.1 maximum_bitcast_fusion
  135.7 0.8 copy.22
  136.6 6.6 %all-to-all-done.4 = bf16[16,2,896]{2,1,0:T(2,128)(2,1)S(1)} async-done(((bf16[16,2,896]{2,1,0:T(2,128)(2,1)}), bf16[16,2,896]{2,1,0:T(2,128)(2,1)S(1)}, u32[]{:S(2)}, u32[]{:S(2)}) %all-to-all-start.4) | async-done | bytes 57376 | tf_op jit(solution)/shard_map/all_to_all | solution.py:282
  143.2 0.1 bitcast_reduce_fusion
  143.2 0.6 reshape.44
  (12 shorter events, 0.1 us)
Async XLA Ops:
  2.2 19.9 %all-to-all-start = ((bf16[16,2,3600]{2,1,0:T(2,128)(2,1)}), bf16[16,2,3600]{2,1,0:T(2,128)(2,1)S(1)}, u32[]{:S(2)}, u32[]{:S(2)}) async-start(bf16[16,2,3600]{2,1,0:T(2,128)(2,1)} %pack.1), calls=%async_computation | async-start | bytes 475136 | tf_op jit(solution)/shard_map/all_to_all | solution.py:282
  12.4 3.1 %copy-start.4 = (s32[64,2]{0,1:T(2,128)S(1)}, s32[64,2]{0,1:T(2,128)}, u32[]{:S(2)}) copy-start(s32[64,2]{0,1:T(2,128)} %param.13) | copy-start | bytes 1540
  12.4 3.1 %copy-start.5 = (s32[64,2]{0,1:T(2,128)S(1)}, s32[64,2]{0,1:T(2,128)}, u32[]{:S(2)}) copy-start(s32[64,2]{0,1:T(2,128)} %param.12) | copy-start | bytes 1540
  12.4 3.3 %copy-start = (bf16[2,1,2,576]{3,2,1,0:T(2,128)(2,1)S(1)}, bf16[2,1,2,576]{3,2,1,0:T(2,128)(2,1)}, u32[]{:S(2)}) copy-start(bf16[2,1,2,576]{3,2,1,0:T(2,128)(2,1)} %fresh_ref.1) | copy-start | bytes 13828
  24.2 14.1 %copy-start.1 = (bf16[1,128,3584]{2,1,0:T(8,128)(2,1)S(1)}, bf16[1,128,3584]{2,1,0:T(8,128)(2,1)}, u32[]{:S(2)}) copy-start(bf16[1,128,3584]{2,1,0:T(8,128)(2,1)} %param.21) | copy-start | bytes 2752516
  24.2 54.5 %all-to-all-start.1 = ((bf16[32,8,3584]{2,1,0:T(8,128)(2,1)}), bf16[32,8,3584]{2,1,0:T(8,128)(2,1)}, u32[]{:S(2)}, u32[]{:S(2)}) async-start(bf16[32,8,3584]{2,1,0:T(8,128)(2,1)} %dispatch.1), calls=%async_computation.1 | async-start | bytes 3670016 | tf_op jit(solution)/shard_map/all_to_all | solution.py:282
  35.7 34.8 %collective-permute-start = (bf16[3584,256]{1,0:T(8,128)(2,1)S(1)}, bf16[3584,256]{1,0:T(8,128)(2,1)}, u32[]{:S(2)}, u32[]{:S(2)}) collective-permute-start(bf16[3584,256]{1,0:T(8,128)(2,1)S(1)} %pad_maximum_fusion.own_ref), channel_id=1, source_target_pairs={{0,64},{64,0},{1,65},{65,1},{2,66},{66,2},{3,67},{67,3},{4,68},{68... | collective-permute-start | bytes 5505032 | tf_op jit(solution)/shard_map/ppermute | solution.py:287
  38.4 15.1 %collective-permute-start.3 = (bf16[128,896]{1,0:T(8,128)(2,1)S(1)}, bf16[128,896]{1,0:T(8,128)(2,1)S(1)}, u32[]{:S(2)}, u32[]{:S(2)}) collective-permute-start(bf16[128,896]{1,0:T(8,128)(2,1)S(1)} %get-tuple-element.40), channel_id=1, source_target_pairs={{0,384},{128,0},{256,128},{384,256},{1,385},{129,1},{257,129},{385... | collective-permute-start | bytes 688136 | tf_op jit(solution)/shard_map/ppermute | solution.py:287
  42.0 12.1 %collective-permute-start.1 = (bf16[128,896]{1,0:T(8,128)(2,1)S(1)}, bf16[128,896]{1,0:T(8,128)(2,1)S(1)}, u32[]{:S(2)}, u32[]{:S(2)}) collective-permute-start(bf16[128,896]{1,0:T(8,128)(2,1)S(1)} %get-tuple-element.39), channel_id=1, source_target_pairs={{0,128},{128,256},{256,384},{384,0},{1,129},{129,257},{257,385},{3... | collective-permute-start | bytes 688136 | tf_op jit(solution)/shard_map/ppermute | solution.py:287
  44.6 14.3 %collective-permute-start.2 = (bf16[128,896]{1,0:T(8,128)(2,1)S(1)}, bf16[128,896]{1,0:T(8,128)(2,1)S(1)}, u32[]{:S(2)}, u32[]{:S(2)}) collective-permute-start(bf16[128,896]{1,0:T(8,128)(2,1)S(1)} %get-tuple-element.41), channel_id=1, source_target_pairs={{0,256},{128,384},{256,0},{384,128},{1,257},{129,385},{257,1},{385... | collective-permute-start | bytes 688136 | tf_op jit(solution)/shard_map/ppermute | solution.py:287
  49.6 20.1 %collective-permute-start.4 = (bf16[2,128,512]{2,1,0:T(8,128)(2,1)S(1)}, bf16[2,128,512]{2,1,0:T(8,128)(2,1)S(1)}, u32[]{:S(2)}, u32[]{:S(2)}) collective-permute-start(bf16[2,128,512]{2,1,0:T(8,128)(2,1)S(1)} %get-tuple-element.19), channel_id=1, source_target_pairs={{0,32},{1,33},{2,34},{3,35},{4,36},{5,37},{6,38},{7,39},{8,40},{9,... | collective-permute-start | bytes 786440 | tf_op jit(solution)/shard_map/ppermute | solution.py:287
  59.1 40.9 %collective-permute-start.5 = (bf16[4,128,896]{2,1,0:T(8,128)(2,1)S(1)}, bf16[4,128,896]{2,1,0:T(8,128)(2,1)}, u32[]{:S(2)}, u32[]{:S(2)}) collective-permute-start(bf16[4,128,896]{2,1,0:T(8,128)(2,1)S(1)} %pad_maximum_fusion.1.own_ref), channel_id=1, source_target_pairs={{0,64},{64,0},{1,65},{65,1},{2,66},{66,2},{3,67},{67,3},{4,68},{68... | collective-permute-start | bytes 2752520 | tf_op jit(solution)/shard_map/ppermute | solution.py:287
  69.7 0.7 copy-start.2
  100.0 22.5 %copy-start.3 = (bf16[2,128,512]{2,1,0:T(8,128)(2,1)S(1)}, bf16[2,128,512]{2,1,0:T(8,128)(2,1)}, u32[]{:S(2)}) copy-start(bf16[2,128,512]{2,1,0:T(8,128)(2,1)} %copy-done.2) | copy-start | bytes 786436
  102.8 20.1 %all-to-all-start.3 = ((bf16[32,8,896]{2,1,0:T(8,128)(2,1)}), bf16[32,8,896]{2,1,0:T(8,128)(2,1)S(1)}, u32[]{:S(2)}, u32[]{:S(2)}) async-start(bf16[32,8,896]{2,1,0:T(8,128)(2,1)} %bitcast.14), calls=%async_computation.3 | async-start | bytes 917504 | tf_op jit(solution)/shard_map/all_to_all | solution.py:282
  111.9 23.7 %collective-permute-start.6 = (bf16[2,128,512]{2,1,0:T(8,128)(2,1)S(1)}, bf16[2,128,512]{2,1,0:T(8,128)(2,1)S(1)}, u32[]{:S(2)}, u32[]{:S(2)}) collective-permute-start(bf16[2,128,512]{2,1,0:T(8,128)(2,1)S(1)} %get-tuple-element.30), channel_id=1, source_target_pairs={{0,63},{1,0},{2,1},{3,2},{4,3},{5,4},{6,5},{7,6},{8,7},{9,8},{10,9... | collective-permute-start | bytes 786440 | tf_op jit(solution)/shard_map/ppermute | solution.py:287
  118.3 17.3 %collective-permute-start.7 = (bf16[2,128,512]{2,1,0:T(8,128)(2,1)S(1)}, bf16[2,128,512]{2,1,0:T(8,128)(2,1)S(1)}, u32[]{:S(2)}, u32[]{:S(2)}) collective-permute-start(bf16[2,128,512]{2,1,0:T(8,128)(2,1)S(1)} %get-tuple-element.30), channel_id=1, source_target_pairs={{0,1},{1,2},{2,3},{3,4},{4,5},{5,6},{6,7},{7,8},{8,9},{9,10},{10,1... | collective-permute-start | bytes 786440 | tf_op jit(solution)/shard_map/ppermute | solution.py:287
  123.7 19.5 %all-to-all-start.4 = ((bf16[16,2,896]{2,1,0:T(2,128)(2,1)}), bf16[16,2,896]{2,1,0:T(2,128)(2,1)S(1)}, u32[]{:S(2)}, u32[]{:S(2)}) async-start(bf16[16,2,896]{2,1,0:T(2,128)(2,1)} %combine.1), calls=%async_computation.4 | async-start | bytes 114688 | tf_op jit(solution)/shard_map/all_to_all | solution.py:282

commit v9 on v8

--- a/solution.py
+++ b/solution.py
@@ -14,7 +14,7 @@
 EP = ("yl", "x", "z")
 DP = ("yh", "c")
 COLUMN = ("yh", "c", "yl")
-PLANE = ("x", "z")
+PLANE = ("z", "x")
 BF = jnp.bfloat16
 F32 = jnp.float32
 ALL_VMEM = pltpu.CompilerParams(vmem_limit_bytes=60 * 1024 * 1024)
@@ -127,10 +127,13 @@
     )(hidden, routes, logits)
 
 
-def chosen_slots(yl, tail, slots):
+def chosen_slots(columns, yl, tail, slots):
     rows, top = tail.shape
     slot = iota((rows, slots), 1)
-    expert = (slot // (2 * CAP) + yl * (slots // (2 * CAP))).astype(F32)
+    peers = slots // (2 * CAP)
+    peer = slot // (2 * CAP)
+    expert = yl * peers + peer % columns * (peers // columns) + peer // columns
+    expert = expert.astype(F32)
     named = jnp.zeros((rows, slots), F32)
     for k in range(top):
         named = jnp.where(tail[:, k : k + 1] == expert, 1.0, named)
@@ -141,10 +144,10 @@
     return chosen & (slot % (2 * CAP) // CAP == iota((rows, slots), 0) // 2 % 2), expert
 
 
-def dispatch_kernel(top, yl_ref, tokens_ref, send_ref, held_ref, done):
+def dispatch_kernel(columns, top, yl_ref, tokens_ref, send_ref, held_ref, done):
     peers, block, width = send_ref.shape
     tail = tokens_ref[:, width : width + top].astype(F32)
-    chosen, _ = chosen_slots(yl_ref[0], tail, peers * block)
+    chosen, _ = chosen_slots(columns, yl_ref[0], tail, peers * block)
     pick = chosen.astype(F32).astype(BF)
     copies = []
     group = 128 // block
@@ -160,9 +163,9 @@
         copy.wait()
 
 
-def dispatch(yl, top, tokens, peers, block, width):
-    return pl.pallas_call(
-        functools.partial(dispatch_kernel, top),
+def dispatch(columns, yl, top, tokens, peers, block, width):
+    return pl.pallas_call(
+        functools.partial(dispatch_kernel, columns, top),
         out_shape=jax.ShapeDtypeStruct((peers, block, width), BF),
         in_specs=[pl.BlockSpec(memory_space=pltpu.SMEM), *vmem(1)],
         out_specs=hbm(),
@@ -175,13 +178,13 @@
     )(yl, tokens)
 
 
-def mix_kernel(yl_ref, tail_ref, mix_ref):
+def mix_kernel(columns, yl_ref, tail_ref, mix_ref):
     slots = mix_ref.shape[1]
     tail = tail_ref[...].astype(F32)
     top = tail.shape[1] // 2
     sigmoid = jax.nn.sigmoid(tail[:, top:])
     gates = 2.5 * sigmoid / jnp.sum(sigmoid, 1, keepdims=True)
-    chosen, expert = chosen_slots(yl_ref[0], tail[:, :top], slots)
+    chosen, expert = chosen_slots(columns, yl_ref[0], tail[:, :top], slots)
     gate = jnp.zeros(chosen.shape, F32)
     for k in range(top):
         gate = jnp.where(tail[:, k : k + 1] == expert, gates[:, k : k + 1], gate)
@@ -190,9 +193,9 @@
     mix_ref[...] = jnp.concatenate(mix, 0).astype(BF)
 
 
-def mixing(yl, tail, slots):
-    return pl.pallas_call(
-        mix_kernel,
+def mixing(columns, yl, tail, slots):
+    return pl.pallas_call(
+        functools.partial(mix_kernel, columns),
         out_shape=jax.ShapeDtypeStruct((2 * tail.shape[0], slots), BF),
         in_specs=[pl.BlockSpec(memory_space=pltpu.SMEM), *vmem(1)],
         out_specs=vmem(1)[0],
@@ -311,6 +314,7 @@
 
     top = routes.shape[3]
     yl = lax.axis_index("yl").reshape(1)
+    columns = lax.axis_size("x")
 
     packed = pack(hidden, routes, route_logits, yh_size, yl_size)
     tokens = exchange(packed, COLUMN)
@@ -318,11 +322,11 @@
     served = attend(lengths[own_rank], queries, latent_cache, new_latent)
     tokens, own_w, served0, served1 = lax.optimization_barrier((tokens, own_w, *served))
     tokens = tokens.reshape(-1, tokens.shape[-1])
-    send = dispatch(yl, top, tokens, peers, block, width)
+    send = dispatch(columns, yl, top, tokens, peers, block, width)
     arrived = exchange(send, PLANE).reshape(slots, width)
 
     far = shifted(served0, EP, experts // 2)
-    mix = mixing(yl, tokens[:, width:], slots)
+    mix = mixing(columns, yl, tokens[:, width:], slots)
     peer_w = shifted(own_w, "c", 1)
     yh = lax.axis_index("yh")
     sent = [

time: 145 us -> 145 us (level)
  starting transfers between devices: 74.1 us -> 71.5 us
  waiting for transfers between devices: 27.8 us -> 29.6 us
    all_to_all x4, starting transfers between devices: 42.8 us -> 40.3 us  [exchange(): return lax.all_to_all(x, axes, split_axis=0, concat_axis=0, tiled=True)]
    all_to_all x4, waiting for transfers between devices: 17.4 us -> 19.3 us  [exchange(): return lax.all_to_all(x, axes, split_axis=0, concat_axis=0, tiled=True)]
where the time goes in v9:
time: 145 us; the launch traced here: 144 us
  starting transfers between devices  71.5 us (49%)
  waiting for transfers between devices  29.6 us (20%)
  blocking collectives  17.9 us (12%)
  Pallas kernels  13.7 us (9%)
  local copies, waits for them, and re-layouts  6.21 us (4%)
  between operations  2.75 us (2%)
  other arithmetic  1.98 us (1%)
    all_to_all x4, starting transfers between devices, exchange(): return lax.all_to_all(x, axes, split_axis=0, concat_axis=0, tiled=True)  40.3 us
    ppermute x8, starting transfers between devices, shifted(): return lax.ppermute(x, axes, [(i, (i + by) % size) for i in range(size)])  31.2 us
    all_to_all x4, waiting for transfers between devices, exchange(): return lax.all_to_all(x, axes, split_axis=0, concat_axis=0, tiled=True)  19.3 us
    all_to_all x1, blocking collectives, exchange(): return lax.all_to_all(x, axes, split_axis=0, concat_axis=0, tiled=True)  17.9 us
    ppermute x8, waiting for transfers between devices, shifted(): return lax.ppermute(x, axes, [(i, (i + by) % size) for i in range(size)])  10.3 us
    unnamed x15, local copies, waits for them, and re-layouts  4.6 us
    pallas_call x1, Pallas kernels, hidden_units(): pl.pallas_call(hidden_kernel, out_shape=jax.ShapeDtypeStruct((peers, *sha...  3.9 us
  transfers between devices with their start and end apart: 12, of which 8 were waited for; matrix products, arithmetic and copies ran while one was open for 5% of the time, Pallas kernels for 5%

profile of v9, /device:TPU:1, one launch (start us, length us, event | category | flops | bytes accessed | tf_op | source)
XLA Modules:
  0.0 143.6 jit_solution(9090477929335218180)
XLA Ops:
  0.6 1.5 %pack.1 = bf16[16,2,3600]{2,1,0:T(2,128)(2,1)} custom-call(bf16[2,1,2,3584]{3,2,1,0:T(2,128)(2,1)} %hidden_ref.1, s32[2,1,2,8]{3,2,1,0:T(2,128)} %routes_ref.1, bf16[2,1,2,8]{3,2,1,0:T(2,128)(2,1)} %logits_ref.1), custom_call_target="tpu_custom_call" | custom-call | tf_op jit(solution)/shard_map/pack/pallas_call | solution.py:113
  2.2 10.2 %all-to-all-start = ((bf16[16,2,3600]{2,1,0:T(2,128)(2,1)}), bf16[16,2,3600]{2,1,0:T(2,128)(2,1)S(1)}, u32[]{:S(2)}, u32[]{:S(2)}) async-start(bf16[16,2,3600]{2,1,0:T(2,128)(2,1)} %pack.1), calls=%async_computation | async-start | bytes 475136 | tf_op jit(solution)/shard_map/all_to_all | solution.py:285
  12.4 0.0 copy-start.5
  12.4 0.0 copy-start
  12.4 1.7 %copy.20.cache_ref = bf16[1,2,512,576]{3,2,1,0:T(8,128)(2,1)S(1)} copy(bf16[1,2,512,576]{2,3,1,0:T(8,128)(2,1)} %param.11) | data formatting | bytes 2359296 | tf_op args[0]
  14.1 1.4 copy.19.query_ref
  15.5 0.2 constant_dynamic-slice_fusion.2
  15.7 2.5 %attend.1 = (bf16[2,128,512]{2,1,0:T(8,128)(2,1)S(1)}, bf16[2,128,512]{2,1,0:T(8,128)(2,1)S(1)}) custom-call(s32[2]{0:T(128)S(1)} %get-tuple-element.45.len_ref, bf16[2,1,2,128,576]{4,3,2,1,0:T(8,128)(2,1)S(1)} %copy.19.query_ref, bf16[1,2,512,576]{3,2,1,0:T(8,128)(2,1)S(1)} %copy.20.cache_ref, bf16[2,1,2,576]{3,2,1,0:T(2,128)(2,1)S(1)} %copy-done), custom_call_target="tpu_custom_call" | custom-call | tf_op jit(solution)/shard_map/attend/pallas_call | solution.py:66
  18.2 1.7 %pad_maximum_fusion.own_ref = bf16[3584,256]{1,0:T(8,128)(2,1)S(1)} fusion(bf16[3584,128]{1,0:T(8,128)(2,1)} %bitcast.29, bf16[3584,128]{1,0:T(8,128)(2,1)} %bitcast.30), kind=kLoop, calls=%fused_computation | loop fusion | flops 3670016 | bytes 3670016 | tf_op jit(solution)/shard_map/concatenate | solution.py:321
  19.8 2.3 %all-to-all-done = bf16[16,2,3600]{2,1,0:T(2,128)(2,1)S(1)} async-done(((bf16[16,2,3600]{2,1,0:T(2,128)(2,1)}), bf16[16,2,3600]{2,1,0:T(2,128)(2,1)S(1)}, u32[]{:S(2)}, u32[]{:S(2)}) %all-to-all-start) | async-done | bytes 230432 | tf_op jit(solution)/shard_map/all_to_all | solution.py:285
  22.1 0.2 reshape.38.tokens_ref
  22.3 1.9 %dispatch.1 = bf16[32,8,3584]{2,1,0:T(8,128)(2,1)} custom-call(s32[1]{0:T(128)} %bitcast.3.yl_ref, bf16[32,3600]{1,0:T(8,128)(2,1)S(1)} %reshape.38.tokens_ref), custom_call_target="tpu_custom_call" | custom-call | tf_op jit(solution)/shard_map/dispatch/pallas_call | solution.py:167
  24.2 0.0 copy-start.1
  24.2 11.5 %all-to-all-start.1 = ((bf16[32,8,3584]{2,1,0:T(8,128)(2,1)}), bf16[32,8,3584]{2,1,0:T(8,128)(2,1)}, u32[]{:S(2)}, u32[]{:S(2)}) async-start(bf16[32,8,3584]{2,1,0:T(8,128)(2,1)} %dispatch.1), calls=%async_computation.1 | async-start | bytes 3670016 | tf_op jit(solution)/shard_map/all_to_all | solution.py:285
  35.7 2.6 %collective-permute-start = (bf16[3584,256]{1,0:T(8,128)(2,1)S(1)}, bf16[3584,256]{1,0:T(8,128)(2,1)}, u32[]{:S(2)}, u32[]{:S(2)}) collective-permute-start(bf16[3584,256]{1,0:T(8,128)(2,1)S(1)} %pad_maximum_fusion.own_ref), channel_id=1, source_target_pairs={{0,64},{64,0},{1,65},{65,1},{2,66},{66,2},{3,67},{67,3},{4,68},{68... | collective-permute-start | bytes 5505032 | tf_op jit(solution)/shard_map/ppermute | solution.py:290
  38.3 0.1 constant_dynamic-slice_fusion
  38.4 3.6 %collective-permute-start.3 = (bf16[128,896]{1,0:T(8,128)(2,1)S(1)}, bf16[128,896]{1,0:T(8,128)(2,1)S(1)}, u32[]{:S(2)}, u32[]{:S(2)}) collective-permute-start(bf16[128,896]{1,0:T(8,128)(2,1)S(1)} %get-tuple-element.40), channel_id=1, source_target_pairs={{0,384},{128,0},{256,128},{384,256},{1,385},{129,1},{257,129},{385... | collective-permute-start | bytes 688136 | tf_op jit(solution)/shard_map/ppermute | solution.py:290
  42.0 2.6 %collective-permute-start.1 = (bf16[128,896]{1,0:T(8,128)(2,1)S(1)}, bf16[128,896]{1,0:T(8,128)(2,1)S(1)}, u32[]{:S(2)}, u32[]{:S(2)}) collective-permute-start(bf16[128,896]{1,0:T(8,128)(2,1)S(1)} %get-tuple-element.39), channel_id=1, source_target_pairs={{0,128},{128,256},{256,384},{384,0},{1,129},{129,257},{257,385},{3... | collective-permute-start | bytes 688136 | tf_op jit(solution)/shard_map/ppermute | solution.py:290
  44.6 5.0 %collective-permute-start.2 = (bf16[128,896]{1,0:T(8,128)(2,1)S(1)}, bf16[128,896]{1,0:T(8,128)(2,1)S(1)}, u32[]{:S(2)}, u32[]{:S(2)}) collective-permute-start(bf16[128,896]{1,0:T(8,128)(2,1)S(1)} %get-tuple-element.41), channel_id=1, source_target_pairs={{0,256},{128,384},{256,0},{384,128},{1,257},{129,385},{257,1},{385... | collective-permute-start | bytes 688136 | tf_op jit(solution)/shard_map/ppermute | solution.py:290
  49.6 2.4 %collective-permute-start.4 = (bf16[2,128,512]{2,1,0:T(8,128)(2,1)S(1)}, bf16[2,128,512]{2,1,0:T(8,128)(2,1)S(1)}, u32[]{:S(2)}, u32[]{:S(2)}) collective-permute-start(bf16[2,128,512]{2,1,0:T(8,128)(2,1)S(1)} %get-tuple-element.19), channel_id=1, source_target_pairs={{0,32},{1,33},{2,34},{3,35},{4,36},{5,37},{6,38},{7,39},{8,40},{9,... | collective-permute-start | bytes 786440 | tf_op jit(solution)/shard_map/ppermute | solution.py:290
  52.0 1.5 %collective-permute-done.3 = bf16[128,896]{1,0:T(8,128)(2,1)S(1)} collective-permute-done((bf16[128,896]{1,0:T(8,128)(2,1)S(1)}, bf16[128,896]{1,0:T(8,128)(2,1)S(1)}, u32[]{:S(2)}, u32[]{:S(2)}) %collective-permute-start.3) | collective-permute-done | bytes 229408 | tf_op jit(solution)/shard_map/ppermute | solution.py:290
  53.6 0.6 collective-permute-done.1
  54.2 4.8 %collective-permute-done.2 = bf16[128,896]{1,0:T(8,128)(2,1)S(1)} collective-permute-done((bf16[128,896]{1,0:T(8,128)(2,1)S(1)}, bf16[128,896]{1,0:T(8,128)(2,1)S(1)}, u32[]{:S(2)}, u32[]{:S(2)}) %collective-permute-start.2) | collective-permute-done | bytes 229408 | tf_op jit(solution)/shard_map/ppermute | solution.py:290
  59.0 0.1 pad_maximum_fusion.1.own_ref
  59.1 6.9 %collective-permute-start.5 = (bf16[4,128,896]{2,1,0:T(8,128)(2,1)S(1)}, bf16[4,128,896]{2,1,0:T(8,128)(2,1)}, u32[]{:S(2)}, u32[]{:S(2)}) collective-permute-start(bf16[4,128,896]{2,1,0:T(8,128)(2,1)S(1)} %pad_maximum_fusion.1.own_ref), channel_id=1, source_target_pairs={{0,64},{64,0},{1,65},{65,1},{2,66},{66,2},{3,67},{67,3},{4,68},{68... | collective-permute-start | bytes 2752520 | tf_op jit(solution)/shard_map/ppermute | solution.py:290
  66.0 0.3 mixing.1.mix_ref
  66.4 3.4 %collective-permute-done.4 = bf16[2,128,512]{2,1,0:T(8,128)(2,1)S(1)} collective-permute-done((bf16[2,128,512]{2,1,0:T(8,128)(2,1)S(1)}, bf16[2,128,512]{2,1,0:T(8,128)(2,1)S(1)}, u32[]{:S(2)}, u32[]{:S(2)}) %collective-permute-start.4) | collective-permute-done | bytes 262176 | tf_op jit(solution)/shard_map/ppermute | solution.py:290
  69.7 0.7 copy-done.2
  70.4 0.0 collective-permute-done.peer_ref
  70.4 8.3 %all-to-all-done.1 = bf16[32,8,3584]{2,1,0:T(8,128)(2,1)} async-done(((bf16[32,8,3584]{2,1,0:T(8,128)(2,1)}), bf16[32,8,3584]{2,1,0:T(8,128)(2,1)}, u32[]{:S(2)}, u32[]{:S(2)}) %all-to-all-start.1) | async-done | bytes 1835040 | tf_op jit(solution)/shard_map/all_to_all | solution.py:285
  78.7 3.9 %hidden_units.1 = bf16[4,256,256]{2,1,0:T(8,128)(2,1)S(1)} custom-call(bf16[256,3584]{1,0:T(8,128)(2,1)} %bitcast.4.rows_ref, bf16[3584,256]{1,0:T(8,128)(2,1)S(1)} %pad_maximum_fusion.own_ref, bf16[3584,256]{1,0:T(8,128)(2,1)} %collective-permute-done.peer_ref), custom_call_target="tpu_custom_call" | custom-call | tf_op jit(solution)/shard_map/hidden_units/pallas_call | solution.py:227
  82.6 17.9 %all_to_all.25.h_ref = bf16[4,256,256]{2,1,0:T(8,128)(2,1)S(1)} all-to-all(bf16[4,256,256]{2,1,0:T(8,128)(2,1)S(1)} %hidden_units.1), channel_id=1, replica_groups=mesh['yh'=4,'c'=2,'yl'=2,'x'=4,'z'=8] {'yh'}, dimensions={0} | all-to-all | bytes 1048576 | tf_op jit(solution)/shard_map/all_to_all | solution.py:285
  100.6 0.0 collective-permute-done.5.peer_ref
  100.6 2.7 %down.1 = bf16[256,896]{1,0:T(8,128)(2,1)} custom-call(s32[1]{0:T(128)} %bitcast.13.yh_ref, bf16[4,256,256]{2,1,0:T(8,128)(2,1)S(1)} %all_to_all.25.h_ref, bf16[4,128,896]{2,1,0:T(8,128)(2,1)S(1)} %pad_maximum_fusion.1.own_ref, bf16[4,128,896]{2,1,0:T(8,128)(2,1)} %collective-permute-done.5.peer_ref), custom_call_target="tpu_custom_call" | custom-call | tf_op jit(solution)/shard_map/down/pallas_call | solution.py:249
  103.3 7.7 %all-to-all-start.3 = ((bf16[32,8,896]{2,1,0:T(8,128)(2,1)}), bf16[32,8,896]{2,1,0:T(8,128)(2,1)S(1)}, u32[]{:S(2)}, u32[]{:S(2)}) async-start(bf16[32,8,896]{2,1,0:T(8,128)(2,1)} %bitcast.14), calls=%async_computation.3 | async-start | bytes 917504 | tf_op jit(solution)/shard_map/all_to_all | solution.py:285
  111.0 6.2 %collective-permute-start.6 = (bf16[2,128,512]{2,1,0:T(8,128)(2,1)S(1)}, bf16[2,128,512]{2,1,0:T(8,128)(2,1)S(1)}, u32[]{:S(2)}, u32[]{:S(2)}) collective-permute-start(bf16[2,128,512]{2,1,0:T(8,128)(2,1)S(1)} %get-tuple-element.30), channel_id=1, source_target_pairs={{0,63},{1,0},{2,1},{3,2},{4,3},{5,4},{6,5},{7,6},{8,7},{9,8},{10,9... | collective-permute-start | bytes 786440 | tf_op jit(solution)/shard_map/ppermute | solution.py:290
  117.2 1.9 %collective-permute-start.7 = (bf16[2,128,512]{2,1,0:T(8,128)(2,1)S(1)}, bf16[2,128,512]{2,1,0:T(8,128)(2,1)S(1)}, u32[]{:S(2)}, u32[]{:S(2)}) collective-permute-start(bf16[2,128,512]{2,1,0:T(8,128)(2,1)S(1)} %get-tuple-element.30), channel_id=1, source_target_pairs={{0,1},{1,2},{2,3},{3,4},{4,5},{5,6},{6,7},{7,8},{8,9},{9,10},{10,1... | collective-permute-start | bytes 786440 | tf_op jit(solution)/shard_map/ppermute | solution.py:290
  119.2 0.5 fusion.1
  121.5 2.1 %all-to-all-done.3 = bf16[32,8,896]{2,1,0:T(8,128)(2,1)S(1)} async-done(((bf16[32,8,896]{2,1,0:T(8,128)(2,1)}), bf16[32,8,896]{2,1,0:T(8,128)(2,1)S(1)}, u32[]{:S(2)}, u32[]{:S(2)}) %all-to-all-start.3) | async-done | bytes 458784 | tf_op jit(solution)/shard_map/all_to_all | solution.py:285
  123.6 0.8 combine.1
  124.4 10.9 %all-to-all-start.4 = ((bf16[16,2,896]{2,1,0:T(2,128)(2,1)}), bf16[16,2,896]{2,1,0:T(2,128)(2,1)S(1)}, u32[]{:S(2)}, u32[]{:S(2)}) async-start(bf16[16,2,896]{2,1,0:T(2,128)(2,1)} %combine.1), calls=%async_computation.4 | async-start | bytes 114688 | tf_op jit(solution)/shard_map/all_to_all | solution.py:285
  135.3 0.0 collective-permute-done.6
  135.3 0.0 collective-permute-done.7
  135.4 0.1 maximum_bitcast_fusion
  135.5 0.8 copy.22
  136.3 6.6 %all-to-all-done.4 = bf16[16,2,896]{2,1,0:T(2,128)(2,1)S(1)} async-done(((bf16[16,2,896]{2,1,0:T(2,128)(2,1)}), bf16[16,2,896]{2,1,0:T(2,128)(2,1)S(1)}, u32[]{:S(2)}, u32[]{:S(2)}) %all-to-all-start.4) | async-done | bytes 57376 | tf_op jit(solution)/shard_map/all_to_all | solution.py:285
  142.9 0.1 bitcast_reduce_fusion
  143.0 0.6 reshape.44
  (12 shorter events, 0.1 us)
Async XLA Ops:
  2.2 19.9 %all-to-all-start = ((bf16[16,2,3600]{2,1,0:T(2,128)(2,1)}), bf16[16,2,3600]{2,1,0:T(2,128)(2,1)S(1)}, u32[]{:S(2)}, u32[]{:S(2)}) async-start(bf16[16,2,3600]{2,1,0:T(2,128)(2,1)} %pack.1), calls=%async_computation | async-start | bytes 475136 | tf_op jit(solution)/shard_map/all_to_all | solution.py:285
  12.4 3.1 %copy-start.4 = (s32[64,2]{0,1:T(2,128)S(1)}, s32[64,2]{0,1:T(2,128)}, u32[]{:S(2)}) copy-start(s32[64,2]{0,1:T(2,128)} %param.13) | copy-start | bytes 1540
  12.4 3.1 %copy-start.5 = (s32[64,2]{0,1:T(2,128)S(1)}, s32[64,2]{0,1:T(2,128)}, u32[]{:S(2)}) copy-start(s32[64,2]{0,1:T(2,128)} %param.12) | copy-start | bytes 1540
  12.4 3.3 %copy-start = (bf16[2,1,2,576]{3,2,1,0:T(2,128)(2,1)S(1)}, bf16[2,1,2,576]{3,2,1,0:T(2,128)(2,1)}, u32[]{:S(2)}) copy-start(bf16[2,1,2,576]{3,2,1,0:T(2,128)(2,1)} %fresh_ref.1) | copy-start | bytes 13828
  24.2 14.1 %copy-start.1 = (bf16[1,128,3584]{2,1,0:T(8,128)(2,1)S(1)}, bf16[1,128,3584]{2,1,0:T(8,128)(2,1)}, u32[]{:S(2)}) copy-start(bf16[1,128,3584]{2,1,0:T(8,128)(2,1)} %param.21) | copy-start | bytes 2752516
  24.2 54.5 %all-to-all-start.1 = ((bf16[32,8,3584]{2,1,0:T(8,128)(2,1)}), bf16[32,8,3584]{2,1,0:T(8,128)(2,1)}, u32[]{:S(2)}, u32[]{:S(2)}) async-start(bf16[32,8,3584]{2,1,0:T(8,128)(2,1)} %dispatch.1), calls=%async_computation.1 | async-start | bytes 3670016 | tf_op jit(solution)/shard_map/all_to_all | solution.py:285
  35.7 34.8 %collective-permute-start = (bf16[3584,256]{1,0:T(8,128)(2,1)S(1)}, bf16[3584,256]{1,0:T(8,128)(2,1)}, u32[]{:S(2)}, u32[]{:S(2)}) collective-permute-start(bf16[3584,256]{1,0:T(8,128)(2,1)S(1)} %pad_maximum_fusion.own_ref), channel_id=1, source_target_pairs={{0,64},{64,0},{1,65},{65,1},{2,66},{66,2},{3,67},{67,3},{4,68},{68... | collective-permute-start | bytes 5505032 | tf_op jit(solution)/shard_map/ppermute | solution.py:290
  38.4 15.1 %collective-permute-start.3 = (bf16[128,896]{1,0:T(8,128)(2,1)S(1)}, bf16[128,896]{1,0:T(8,128)(2,1)S(1)}, u32[]{:S(2)}, u32[]{:S(2)}) collective-permute-start(bf16[128,896]{1,0:T(8,128)(2,1)S(1)} %get-tuple-element.40), channel_id=1, source_target_pairs={{0,384},{128,0},{256,128},{384,256},{1,385},{129,1},{257,129},{385... | collective-permute-start | bytes 688136 | tf_op jit(solution)/shard_map/ppermute | solution.py:290
  42.0 12.1 %collective-permute-start.1 = (bf16[128,896]{1,0:T(8,128)(2,1)S(1)}, bf16[128,896]{1,0:T(8,128)(2,1)S(1)}, u32[]{:S(2)}, u32[]{:S(2)}) collective-permute-start(bf16[128,896]{1,0:T(8,128)(2,1)S(1)} %get-tuple-element.39), channel_id=1, source_target_pairs={{0,128},{128,256},{256,384},{384,0},{1,129},{129,257},{257,385},{3... | collective-permute-start | bytes 688136 | tf_op jit(solution)/shard_map/ppermute | solution.py:290
  44.6 14.3 %collective-permute-start.2 = (bf16[128,896]{1,0:T(8,128)(2,1)S(1)}, bf16[128,896]{1,0:T(8,128)(2,1)S(1)}, u32[]{:S(2)}, u32[]{:S(2)}) collective-permute-start(bf16[128,896]{1,0:T(8,128)(2,1)S(1)} %get-tuple-element.41), channel_id=1, source_target_pairs={{0,256},{128,384},{256,0},{384,128},{1,257},{129,385},{257,1},{385... | collective-permute-start | bytes 688136 | tf_op jit(solution)/shard_map/ppermute | solution.py:290
  49.6 20.1 %collective-permute-start.4 = (bf16[2,128,512]{2,1,0:T(8,128)(2,1)S(1)}, bf16[2,128,512]{2,1,0:T(8,128)(2,1)S(1)}, u32[]{:S(2)}, u32[]{:S(2)}) collective-permute-start(bf16[2,128,512]{2,1,0:T(8,128)(2,1)S(1)} %get-tuple-element.19), channel_id=1, source_target_pairs={{0,32},{1,33},{2,34},{3,35},{4,36},{5,37},{6,38},{7,39},{8,40},{9,... | collective-permute-start | bytes 786440 | tf_op jit(solution)/shard_map/ppermute | solution.py:290
  59.1 41.5 %collective-permute-start.5 = (bf16[4,128,896]{2,1,0:T(8,128)(2,1)S(1)}, bf16[4,128,896]{2,1,0:T(8,128)(2,1)}, u32[]{:S(2)}, u32[]{:S(2)}) collective-permute-start(bf16[4,128,896]{2,1,0:T(8,128)(2,1)S(1)} %pad_maximum_fusion.1.own_ref), channel_id=1, source_target_pairs={{0,64},{64,0},{1,65},{65,1},{2,66},{66,2},{3,67},{67,3},{4,68},{68... | collective-permute-start | bytes 2752520 | tf_op jit(solution)/shard_map/ppermute | solution.py:290
  69.7 0.7 copy-start.2
  100.6 20.9 %copy-start.3 = (bf16[2,128,512]{2,1,0:T(8,128)(2,1)S(1)}, bf16[2,128,512]{2,1,0:T(8,128)(2,1)}, u32[]{:S(2)}) copy-start(bf16[2,128,512]{2,1,0:T(8,128)(2,1)} %copy-done.2) | copy-start | bytes 786436
  103.3 20.3 %all-to-all-start.3 = ((bf16[32,8,896]{2,1,0:T(8,128)(2,1)}), bf16[32,8,896]{2,1,0:T(8,128)(2,1)S(1)}, u32[]{:S(2)}, u32[]{:S(2)}) async-start(bf16[32,8,896]{2,1,0:T(8,128)(2,1)} %bitcast.14), calls=%async_computation.3 | async-start | bytes 917504 | tf_op jit(solution)/shard_map/all_to_all | solution.py:285
  111.0 24.3 %collective-permute-start.6 = (bf16[2,128,512]{2,1,0:T(8,128)(2,1)S(1)}, bf16[2,128,512]{2,1,0:T(8,128)(2,1)S(1)}, u32[]{:S(2)}, u32[]{:S(2)}) collective-permute-start(bf16[2,128,512]{2,1,0:T(8,128)(2,1)S(1)} %get-tuple-element.30), channel_id=1, source_target_pairs={{0,63},{1,0},{2,1},{3,2},{4,3},{5,4},{6,5},{7,6},{8,7},{9,8},{10,9... | collective-permute-start | bytes 786440 | tf_op jit(solution)/shard_map/ppermute | solution.py:290
  117.2 18.1 %collective-permute-start.7 = (bf16[2,128,512]{2,1,0:T(8,128)(2,1)S(1)}, bf16[2,128,512]{2,1,0:T(8,128)(2,1)S(1)}, u32[]{:S(2)}, u32[]{:S(2)}) collective-permute-start(bf16[2,128,512]{2,1,0:T(8,128)(2,1)S(1)} %get-tuple-element.30), channel_id=1, source_target_pairs={{0,1},{1,2},{2,3},{3,4},{4,5},{5,6},{6,7},{7,8},{8,9},{9,10},{10,1... | collective-permute-start | bytes 786440 | tf_op jit(solution)/shard_map/ppermute | solution.py:290
  124.4 18.5 %all-to-all-start.4 = ((bf16[16,2,896]{2,1,0:T(2,128)(2,1)}), bf16[16,2,896]{2,1,0:T(2,128)(2,1)S(1)}, u32[]{:S(2)}, u32[]{:S(2)}) async-start(bf16[16,2,896]{2,1,0:T(2,128)(2,1)} %combine.1), calls=%async_computation.4 | async-start | bytes 114688 | tf_op jit(solution)/shard_map/all_to_all | solution.py:285

commit v10 on v9

--- a/solution.py
+++ b/solution.py
@@ -338,11 +338,13 @@
     arrived, peer_w, own_down, mix, far = lax.optimization_barrier(
         (arrived, peer_w, own_down, mix, far)
     )
-    h = exchange(hidden_units(arrived, own_w, peer_w, yh_size), "yh")
+    h = hidden_units(arrived, own_w, peer_w, yh_size)
     h, served1 = lax.optimization_barrier((h, served1))
+    h = exchange(h, "yh")
     lower = shifted(served1, EP, 1)
     upper = shifted(served1, EP, -1)
     out = down(yh, h, own_down, peer_down)
+    out, lower, upper = lax.optimization_barrier((out, lower, upper))
     back = exchange(out.reshape(peers, block, chunk), PLANE).reshape(slots, chunk)
     mixed, served1 = lax.optimization_barrier((combine(mix, back, requests), served1))
     final = exchange(mixed, COLUMN)

time: 145 us -> 144 us (level)
  blocking collectives: 17.9 us -> 0 us
  waiting for transfers between devices: 29.6 us -> 47.2 us
    all_to_all x1 -> x0, blocking collectives: 17.9 us -> none  [exchange(): return lax.all_to_all(x, axes, split_axis=0, concat_axis=0, tiled=True)]
    all_to_all x4 -> x5, waiting for transfers between devices: 19.3 us -> 28.3 us  [exchange(): return lax.all_to_all(x, axes, split_axis=0, concat_axis=0, tiled=True)]
    ppermute x8, waiting for transfers between devices: 10.3 us -> 18.9 us  [shifted(): return lax.ppermute(x, axes, [(i, (i + by) % size) for i in range(size)])]
    all_to_all x4 -> x5, starting transfers between devices: 40.3 us -> 39.2 us  [exchange(): return lax.all_to_all(x, axes, split_axis=0, concat_axis=0, tiled=True)]
  transfers between devices with their start and end apart: 12 -> 13, of which waited for: 8 -> 8; matrix products, arithmetic and copies ran while one was open for 5% -> 5% of each run, Pallas kernels for 5% -> 7%
where the time goes in v10:
time: 144 us; the launch traced here: 143 us
  starting transfers between devices  71.5 us (50%)
  waiting for transfers between devices  47.2 us (33%)
  Pallas kernels  13.8 us (10%)
  local copies, waits for them, and re-layouts  5.16 us (4%)
  other arithmetic  2.93 us (2%)
  between operations  2.78 us (2%)
    all_to_all x5, starting transfers between devices, exchange(): return lax.all_to_all(x, axes, split_axis=0, concat_axis=0, tiled=True)  39.2 us
    ppermute x8, starting transfers between devices, shifted(): return lax.ppermute(x, axes, [(i, (i + by) % size) for i in range(size)])  32.3 us
    all_to_all x5, waiting for transfers between devices, exchange(): return lax.all_to_all(x, axes, split_axis=0, concat_axis=0, tiled=True)  28.3 us
    ppermute x8, waiting for transfers between devices, shifted(): return lax.ppermute(x, axes, [(i, (i + by) % size) for i in range(size)])  18.9 us
    pallas_call x1, Pallas kernels, hidden_units(): pl.pallas_call(hidden_kernel, out_shape=jax.ShapeDtypeStruct((peers, *sha...  4 us
    unnamed x15, local copies, waits for them, and re-layouts  3.55 us
  transfers between devices with their start and end apart: 13, of which 8 were waited for; matrix products, arithmetic and copies ran while one was open for 5% of the time, Pallas kernels for 7%

profile of v10, /device:TPU:1, one launch (start us, length us, event | category | flops | bytes accessed | tf_op | source)
XLA Modules:
  0.0 143.3 jit_solution(14997686148404418215)
XLA Ops:
  0.6 1.6 %pack.1 = bf16[16,2,3600]{2,1,0:T(2,128)(2,1)} custom-call(bf16[2,1,2,3584]{3,2,1,0:T(2,128)(2,1)} %hidden_ref.1, s32[2,1,2,8]{3,2,1,0:T(2,128)} %routes_ref.1, bf16[2,1,2,8]{3,2,1,0:T(2,128)(2,1)} %logits_ref.1), custom_call_target="tpu_custom_call" | custom-call | tf_op jit(solution)/shard_map/pack/pallas_call | solution.py:113
  2.3 10.2 %all-to-all-start = ((bf16[16,2,3600]{2,1,0:T(2,128)(2,1)}), bf16[16,2,3600]{2,1,0:T(2,128)(2,1)S(1)}, u32[]{:S(2)}, u32[]{:S(2)}) async-start(bf16[16,2,3600]{2,1,0:T(2,128)(2,1)} %pack.1), calls=%async_computation | async-start | bytes 475136 | tf_op jit(solution)/shard_map/all_to_all | solution.py:285
  12.5 0.0 copy-start.5
  12.5 0.0 copy-start
  12.5 1.7 %copy.20.cache_ref = bf16[1,2,512,576]{3,2,1,0:T(8,128)(2,1)S(1)} copy(bf16[1,2,512,576]{2,3,1,0:T(8,128)(2,1)} %param.11) | data formatting | bytes 2359296 | tf_op args[0]
  14.2 0.3 copy.19.query_ref
  14.5 0.2 constant_dynamic-slice_fusion.2
  14.7 2.5 %attend.1 = (bf16[2,128,512]{2,1,0:T(8,128)(2,1)S(1)}, bf16[2,128,512]{2,1,0:T(8,128)(2,1)S(1)}) custom-call(s32[2]{0:T(128)S(1)} %get-tuple-element.51.len_ref, bf16[2,1,2,128,576]{4,3,2,1,0:T(8,128)(2,1)S(1)} %copy.19.query_ref, bf16[1,2,512,576]{3,2,1,0:T(8,128)(2,1)S(1)} %copy.20.cache_ref, bf16[2,1,2,576]{3,2,1,0:T(2,128)(2,1)S(1)} %copy-done), custom_call_target="tpu_custom_call" | custom-call | tf_op jit(solution)/shard_map/attend/pallas_call | solution.py:66
  17.2 1.7 %pad_maximum_fusion.own_ref = bf16[3584,256]{1,0:T(8,128)(2,1)S(1)} fusion(bf16[3584,128]{1,0:T(8,128)(2,1)} %bitcast.29, bf16[3584,128]{1,0:T(8,128)(2,1)} %bitcast.30), kind=kLoop, calls=%fused_computation | loop fusion | flops 3670016 | bytes 3670016 | tf_op jit(solution)/shard_map/concatenate | solution.py:321
  18.8 3.4 %all-to-all-done = bf16[16,2,3600]{2,1,0:T(2,128)(2,1)S(1)} async-done(((bf16[16,2,3600]{2,1,0:T(2,128)(2,1)}), bf16[16,2,3600]{2,1,0:T(2,128)(2,1)S(1)}, u32[]{:S(2)}, u32[]{:S(2)}) %all-to-all-start) | async-done | bytes 230432 | tf_op jit(solution)/shard_map/all_to_all | solution.py:285
  22.2 0.2 reshape.38.tokens_ref
  22.4 1.9 %dispatch.1 = bf16[32,8,3584]{2,1,0:T(8,128)(2,1)} custom-call(s32[1]{0:T(128)} %bitcast.3.yl_ref, bf16[32,3600]{1,0:T(8,128)(2,1)S(1)} %reshape.38.tokens_ref), custom_call_target="tpu_custom_call" | custom-call | tf_op jit(solution)/shard_map/dispatch/pallas_call | solution.py:167
  24.3 0.0 copy-start.1
  24.3 11.5 %all-to-all-start.1 = ((bf16[32,8,3584]{2,1,0:T(8,128)(2,1)}), bf16[32,8,3584]{2,1,0:T(8,128)(2,1)}, u32[]{:S(2)}, u32[]{:S(2)}) async-start(bf16[32,8,3584]{2,1,0:T(8,128)(2,1)} %dispatch.1), calls=%async_computation.1 | async-start | bytes 3670016 | tf_op jit(solution)/shard_map/all_to_all | solution.py:285
  35.8 2.6 %collective-permute-start = (bf16[3584,256]{1,0:T(8,128)(2,1)S(1)}, bf16[3584,256]{1,0:T(8,128)(2,1)}, u32[]{:S(2)}, u32[]{:S(2)}) collective-permute-start(bf16[3584,256]{1,0:T(8,128)(2,1)S(1)} %pad_maximum_fusion.own_ref), channel_id=1, source_target_pairs={{0,64},{64,0},{1,65},{65,1},{2,66},{66,2},{3,67},{67,3},{4,68},{68... | collective-permute-start | bytes 5505032 | tf_op jit(solution)/shard_map/ppermute | solution.py:290
  38.4 0.1 constant_dynamic-slice_fusion
  38.5 3.6 %collective-permute-start.3 = (bf16[128,896]{1,0:T(8,128)(2,1)S(1)}, bf16[128,896]{1,0:T(8,128)(2,1)S(1)}, u32[]{:S(2)}, u32[]{:S(2)}) collective-permute-start(bf16[128,896]{1,0:T(8,128)(2,1)S(1)} %get-tuple-element.46), channel_id=1, source_target_pairs={{0,384},{128,0},{256,128},{384,256},{1,385},{129,1},{257,129},{385... | collective-permute-start | bytes 688136 | tf_op jit(solution)/shard_map/ppermute | solution.py:290
  42.1 2.6 %collective-permute-start.1 = (bf16[128,896]{1,0:T(8,128)(2,1)S(1)}, bf16[128,896]{1,0:T(8,128)(2,1)S(1)}, u32[]{:S(2)}, u32[]{:S(2)}) collective-permute-start(bf16[128,896]{1,0:T(8,128)(2,1)S(1)} %get-tuple-element.45), channel_id=1, source_target_pairs={{0,128},{128,256},{256,384},{384,0},{1,129},{129,257},{257,385},{3... | collective-permute-start | bytes 688136 | tf_op jit(solution)/shard_map/ppermute | solution.py:290
  44.7 4.6 %collective-permute-start.2 = (bf16[128,896]{1,0:T(8,128)(2,1)S(1)}, bf16[128,896]{1,0:T(8,128)(2,1)S(1)}, u32[]{:S(2)}, u32[]{:S(2)}) collective-permute-start(bf16[128,896]{1,0:T(8,128)(2,1)S(1)} %get-tuple-element.47), channel_id=1, source_target_pairs={{0,256},{128,384},{256,0},{384,128},{1,257},{129,385},{257,1},{385... | collective-permute-start | bytes 688136 | tf_op jit(solution)/shard_map/ppermute | solution.py:290
  49.4 2.7 %collective-permute-start.4 = (bf16[2,128,512]{2,1,0:T(8,128)(2,1)S(1)}, bf16[2,128,512]{2,1,0:T(8,128)(2,1)S(1)}, u32[]{:S(2)}, u32[]{:S(2)}) collective-permute-start(bf16[2,128,512]{2,1,0:T(8,128)(2,1)S(1)} %get-tuple-element.22), channel_id=1, source_target_pairs={{0,32},{1,33},{2,34},{3,35},{4,36},{5,37},{6,38},{7,39},{8,40},{9,... | collective-permute-start | bytes 786440 | tf_op jit(solution)/shard_map/ppermute | solution.py:290
  52.1 1.5 %collective-permute-done.3 = bf16[128,896]{1,0:T(8,128)(2,1)S(1)} collective-permute-done((bf16[128,896]{1,0:T(8,128)(2,1)S(1)}, bf16[128,896]{1,0:T(8,128)(2,1)S(1)}, u32[]{:S(2)}, u32[]{:S(2)}) %collective-permute-start.3) | collective-permute-done | bytes 229408 | tf_op jit(solution)/shard_map/ppermute | solution.py:290
  53.6 0.0 collective-permute-done.1
  53.6 5.4 %collective-permute-done.2 = bf16[128,896]{1,0:T(8,128)(2,1)S(1)} collective-permute-done((bf16[128,896]{1,0:T(8,128)(2,1)S(1)}, bf16[128,896]{1,0:T(8,128)(2,1)S(1)}, u32[]{:S(2)}, u32[]{:S(2)}) %collective-permute-start.2) | collective-permute-done | bytes 229408 | tf_op jit(solution)/shard_map/ppermute | solution.py:290
  59.1 0.1 pad_maximum_fusion.1.own_ref
  59.2 6.7 %collective-permute-start.5 = (bf16[4,128,896]{2,1,0:T(8,128)(2,1)S(1)}, bf16[4,128,896]{2,1,0:T(8,128)(2,1)}, u32[]{:S(2)}, u32[]{:S(2)}) collective-permute-start(bf16[4,128,896]{2,1,0:T(8,128)(2,1)S(1)} %pad_maximum_fusion.1.own_ref), channel_id=1, source_target_pairs={{0,64},{64,0},{1,65},{65,1},{2,66},{66,2},{3,67},{67,3},{4,68},{68... | collective-permute-start | bytes 2752520 | tf_op jit(solution)/shard_map/ppermute | solution.py:290
  65.9 0.3 mixing.1.mix_ref
  66.3 3.9 %collective-permute-done.4 = bf16[2,128,512]{2,1,0:T(8,128)(2,1)S(1)} collective-permute-done((bf16[2,128,512]{2,1,0:T(8,128)(2,1)S(1)}, bf16[2,128,512]{2,1,0:T(8,128)(2,1)S(1)}, u32[]{:S(2)}, u32[]{:S(2)}) %collective-permute-start.4) | collective-permute-done | bytes 262176 | tf_op jit(solution)/shard_map/ppermute | solution.py:290
  70.2 0.7 copy-done.3
  70.9 7.9 %all-to-all-done.1 = bf16[32,8,3584]{2,1,0:T(8,128)(2,1)} async-done(((bf16[32,8,3584]{2,1,0:T(8,128)(2,1)}), bf16[32,8,3584]{2,1,0:T(8,128)(2,1)}, u32[]{:S(2)}, u32[]{:S(2)}) %all-to-all-start.1) | async-done | bytes 1835040 | tf_op jit(solution)/shard_map/all_to_all | solution.py:285
  78.8 4.0 %hidden_units.1 = bf16[4,256,256]{2,1,0:T(8,128)(2,1)} custom-call(bf16[256,3584]{1,0:T(8,128)(2,1)} %bitcast.4.rows_ref, bf16[3584,256]{1,0:T(8,128)(2,1)S(1)} %pad_maximum_fusion.own_ref, bf16[3584,256]{1,0:T(8,128)(2,1)} %collective-permute-done.peer_ref), custom_call_target="tpu_custom_call" | custom-call | tf_op jit(solution)/shard_map/hidden_units/pallas_call | solution.py:227
  82.8 3.7 %all-to-all-start.2 = ((bf16[4,256,256]{2,1,0:T(8,128)(2,1)}), bf16[4,256,256]{2,1,0:T(8,128)(2,1)S(1)}, u32[]{:S(2)}, u32[]{:S(2)}) async-start(bf16[4,256,256]{2,1,0:T(8,128)(2,1)} %hidden_units.1), calls=%async_computation.2 | async-start | bytes 1048576 | tf_op jit(solution)/shard_map/all_to_all | solution.py:285
  86.5 3.5 %collective-permute-start.6 = (bf16[2,128,512]{2,1,0:T(8,128)(2,1)S(1)}, bf16[2,128,512]{2,1,0:T(8,128)(2,1)S(1)}, u32[]{:S(2)}, u32[]{:S(2)}) collective-permute-start(bf16[2,128,512]{2,1,0:T(8,128)(2,1)S(1)} %get-tuple-element.34), channel_id=1, source_target_pairs={{0,1},{1,2},{2,3},{3,4},{4,5},{5,6},{6,7},{7,8},{8,9},{9,10},{10,1... | collective-permute-start | bytes 786440 | tf_op jit(solution)/shard_map/ppermute | solution.py:290
  90.0 6.0 %collective-permute-start.7 = (bf16[2,128,512]{2,1,0:T(8,128)(2,1)S(1)}, bf16[2,128,512]{2,1,0:T(8,128)(2,1)}, u32[]{:S(2)}, u32[]{:S(2)}) collective-permute-start(bf16[2,128,512]{2,1,0:T(8,128)(2,1)S(1)} %get-tuple-element.34), channel_id=1, source_target_pairs={{0,63},{1,0},{2,1},{3,2},{4,3},{5,4},{6,5},{7,6},{8,7},{9,8},{10,9... | collective-permute-start | bytes 786440 | tf_op jit(solution)/shard_map/ppermute | solution.py:290
  96.0 0.0 all-to-all-done.2.h_ref
  96.1 2.7 %down.1 = bf16[256,896]{1,0:T(8,128)(2,1)} custom-call(s32[1]{0:T(128)} %bitcast.13.yh_ref, bf16[4,256,256]{2,1,0:T(8,128)(2,1)S(1)} %all-to-all-done.2.h_ref, bf16[4,128,896]{2,1,0:T(8,128)(2,1)S(1)} %pad_maximum_fusion.1.own_ref, bf16[4,128,896]{2,1,0:T(8,128)(2,1)} %collective-permute-done.5.peer_ref), custom_call_target="tpu_custom_call" | custom-call | tf_op jit(solution)/shard_map/down/pallas_call | solution.py:249
  98.7 8.0 %collective-permute-done.6 = bf16[2,128,512]{2,1,0:T(8,128)(2,1)S(1)} collective-permute-done((bf16[2,128,512]{2,1,0:T(8,128)(2,1)S(1)}, bf16[2,128,512]{2,1,0:T(8,128)(2,1)S(1)}, u32[]{:S(2)}, u32[]{:S(2)}) %collective-permute-start.6) | collective-permute-done | bytes 262176 | tf_op jit(solution)/shard_map/ppermute | solution.py:290
  106.7 0.0 collective-permute-done.7
  106.7 4.3 %all-to-all-start.3 = ((bf16[32,8,896]{2,1,0:T(8,128)(2,1)}), bf16[32,8,896]{2,1,0:T(8,128)(2,1)S(1)}, u32[]{:S(2)}, u32[]{:S(2)}) async-start(bf16[32,8,896]{2,1,0:T(8,128)(2,1)} %bitcast.14), calls=%async_computation.3 | async-start | bytes 917504 | tf_op jit(solution)/shard_map/all_to_all | solution.py:285
  111.0 0.5 fusion.1
  113.3 1.0 select_bitcast_fusion.1
  114.3 10.3 %all-to-all-done.3 = bf16[32,8,896]{2,1,0:T(8,128)(2,1)S(1)} async-done(((bf16[32,8,896]{2,1,0:T(8,128)(2,1)}), bf16[32,8,896]{2,1,0:T(8,128)(2,1)S(1)}, u32[]{:S(2)}, u32[]{:S(2)}) %all-to-all-start.3) | async-done | bytes 458784 | tf_op jit(solution)/shard_map/all_to_all | solution.py:285
  124.6 0.8 combine.1
  125.5 9.6 %all-to-all-start.4 = ((bf16[16,2,896]{2,1,0:T(2,128)(2,1)}), bf16[16,2,896]{2,1,0:T(2,128)(2,1)S(1)}, u32[]{:S(2)}, u32[]{:S(2)}) async-start(bf16[16,2,896]{2,1,0:T(2,128)(2,1)} %combine.1), calls=%async_computation.4 | async-start | bytes 114688 | tf_op jit(solution)/shard_map/all_to_all | solution.py:285
  135.1 0.1 maximum_bitcast_fusion
  135.2 0.8 copy.22
  136.0 6.6 %all-to-all-done.4 = bf16[16,2,896]{2,1,0:T(2,128)(2,1)S(1)} async-done(((bf16[16,2,896]{2,1,0:T(2,128)(2,1)}), bf16[16,2,896]{2,1,0:T(2,128)(2,1)S(1)}, u32[]{:S(2)}, u32[]{:S(2)}) %all-to-all-start.4) | async-done | bytes 57376 | tf_op jit(solution)/shard_map/all_to_all | solution.py:285
  142.6 0.1 bitcast_reduce_fusion
  142.7 0.6 reshape.44
  (13 shorter events, 0.1 us)
Async XLA Ops:
  0.6 13.6 %copy-start.2 = (bf16[2,1,2,128,576]{3,4,2,1,0:T(8,128)(2,1)S(1)}, bf16[2,1,2,128,576]{3,4,2,1,0:T(8,128)(2,1)}, u32[]{:S(2)}) copy-start(bf16[2,1,2,128,576]{3,4,2,1,0:T(8,128)(2,1)} %param.14) | copy-start | bytes 1769476
  2.3 19.9 %all-to-all-start = ((bf16[16,2,3600]{2,1,0:T(2,128)(2,1)}), bf16[16,2,3600]{2,1,0:T(2,128)(2,1)S(1)}, u32[]{:S(2)}, u32[]{:S(2)}) async-start(bf16[16,2,3600]{2,1,0:T(2,128)(2,1)} %pack.1), calls=%async_computation | async-start | bytes 475136 | tf_op jit(solution)/shard_map/all_to_all | solution.py:285
  12.5 2.0 %copy-start.4 = (s32[64,2]{0,1:T(2,128)S(1)}, s32[64,2]{0,1:T(2,128)}, u32[]{:S(2)}) copy-start(s32[64,2]{0,1:T(2,128)} %param.13) | copy-start | bytes 1540
  12.5 2.0 %copy-start.5 = (s32[64,2]{0,1:T(2,128)S(1)}, s32[64,2]{0,1:T(2,128)}, u32[]{:S(2)}) copy-start(s32[64,2]{0,1:T(2,128)} %param.12) | copy-start | bytes 1540
  12.5 2.2 %copy-start = (bf16[2,1,2,576]{3,2,1,0:T(2,128)(2,1)S(1)}, bf16[2,1,2,576]{3,2,1,0:T(2,128)(2,1)}, u32[]{:S(2)}) copy-start(bf16[2,1,2,576]{3,2,1,0:T(2,128)(2,1)} %fresh_ref.1) | copy-start | bytes 13828
  24.3 14.1 %copy-start.1 = (bf16[1,128,3584]{2,1,0:T(8,128)(2,1)S(1)}, bf16[1,128,3584]{2,1,0:T(8,128)(2,1)}, u32[]{:S(2)}) copy-start(bf16[1,128,3584]{2,1,0:T(8,128)(2,1)} %param.21) | copy-start | bytes 2752516
  24.3 54.5 %all-to-all-start.1 = ((bf16[32,8,3584]{2,1,0:T(8,128)(2,1)}), bf16[32,8,3584]{2,1,0:T(8,128)(2,1)}, u32[]{:S(2)}, u32[]{:S(2)}) async-start(bf16[32,8,3584]{2,1,0:T(8,128)(2,1)} %dispatch.1), calls=%async_computation.1 | async-start | bytes 3670016 | tf_op jit(solution)/shard_map/all_to_all | solution.py:285
  35.8 35.1 %collective-permute-start = (bf16[3584,256]{1,0:T(8,128)(2,1)S(1)}, bf16[3584,256]{1,0:T(8,128)(2,1)}, u32[]{:S(2)}, u32[]{:S(2)}) collective-permute-start(bf16[3584,256]{1,0:T(8,128)(2,1)S(1)} %pad_maximum_fusion.own_ref), channel_id=1, source_target_pairs={{0,64},{64,0},{1,65},{65,1},{2,66},{66,2},{3,67},{67,3},{4,68},{68... | collective-permute-start | bytes 5505032 | tf_op jit(solution)/shard_map/ppermute | solution.py:290
  38.5 15.1 %collective-permute-start.3 = (bf16[128,896]{1,0:T(8,128)(2,1)S(1)}, bf16[128,896]{1,0:T(8,128)(2,1)S(1)}, u32[]{:S(2)}, u32[]{:S(2)}) collective-permute-start(bf16[128,896]{1,0:T(8,128)(2,1)S(1)} %get-tuple-element.46), channel_id=1, source_target_pairs={{0,384},{128,0},{256,128},{384,256},{1,385},{129,1},{257,129},{385... | collective-permute-start | bytes 688136 | tf_op jit(solution)/shard_map/ppermute | solution.py:290
  42.1 11.5 %collective-permute-start.1 = (bf16[128,896]{1,0:T(8,128)(2,1)S(1)}, bf16[128,896]{1,0:T(8,128)(2,1)S(1)}, u32[]{:S(2)}, u32[]{:S(2)}) collective-permute-start(bf16[128,896]{1,0:T(8,128)(2,1)S(1)} %get-tuple-element.45), channel_id=1, source_target_pairs={{0,128},{128,256},{256,384},{384,0},{1,129},{129,257},{257,385},{3... | collective-permute-start | bytes 688136 | tf_op jit(solution)/shard_map/ppermute | solution.py:290
  44.7 14.4 %collective-permute-start.2 = (bf16[128,896]{1,0:T(8,128)(2,1)S(1)}, bf16[128,896]{1,0:T(8,128)(2,1)S(1)}, u32[]{:S(2)}, u32[]{:S(2)}) collective-permute-start(bf16[128,896]{1,0:T(8,128)(2,1)S(1)} %get-tuple-element.47), channel_id=1, source_target_pairs={{0,256},{128,384},{256,0},{384,128},{1,257},{129,385},{257,1},{385... | collective-permute-start | bytes 688136 | tf_op jit(solution)/shard_map/ppermute | solution.py:290
  49.4 20.8 %collective-permute-start.4 = (bf16[2,128,512]{2,1,0:T(8,128)(2,1)S(1)}, bf16[2,128,512]{2,1,0:T(8,128)(2,1)S(1)}, u32[]{:S(2)}, u32[]{:S(2)}) collective-permute-start(bf16[2,128,512]{2,1,0:T(8,128)(2,1)S(1)} %get-tuple-element.22), channel_id=1, source_target_pairs={{0,32},{1,33},{2,34},{3,35},{4,36},{5,37},{6,38},{7,39},{8,40},{9,... | collective-permute-start | bytes 786440 | tf_op jit(solution)/shard_map/ppermute | solution.py:290
  59.2 36.8 %collective-permute-start.5 = (bf16[4,128,896]{2,1,0:T(8,128)(2,1)S(1)}, bf16[4,128,896]{2,1,0:T(8,128)(2,1)}, u32[]{:S(2)}, u32[]{:S(2)}) collective-permute-start(bf16[4,128,896]{2,1,0:T(8,128)(2,1)S(1)} %pad_maximum_fusion.1.own_ref), channel_id=1, source_target_pairs={{0,64},{64,0},{1,65},{65,1},{2,66},{66,2},{3,67},{67,3},{4,68},{68... | collective-permute-start | bytes 2752520 | tf_op jit(solution)/shard_map/ppermute | solution.py:290
  70.2 0.7 copy-start.3
  82.8 13.2 %all-to-all-start.2 = ((bf16[4,256,256]{2,1,0:T(8,128)(2,1)}), bf16[4,256,256]{2,1,0:T(8,128)(2,1)S(1)}, u32[]{:S(2)}, u32[]{:S(2)}) async-start(bf16[4,256,256]{2,1,0:T(8,128)(2,1)} %hidden_units.1), calls=%async_computation.2 | async-start | bytes 1048576 | tf_op jit(solution)/shard_map/all_to_all | solution.py:285
  86.5 20.2 %collective-permute-start.6 = (bf16[2,128,512]{2,1,0:T(8,128)(2,1)S(1)}, bf16[2,128,512]{2,1,0:T(8,128)(2,1)S(1)}, u32[]{:S(2)}, u32[]{:S(2)}) collective-permute-start(bf16[2,128,512]{2,1,0:T(8,128)(2,1)S(1)} %get-tuple-element.34), channel_id=1, source_target_pairs={{0,1},{1,2},{2,3},{3,4},{4,5},{5,6},{6,7},{7,8},{8,9},{9,10},{10,1... | collective-permute-start | bytes 786440 | tf_op jit(solution)/shard_map/ppermute | solution.py:290
  90.0 16.7 %collective-permute-start.7 = (bf16[2,128,512]{2,1,0:T(8,128)(2,1)S(1)}, bf16[2,128,512]{2,1,0:T(8,128)(2,1)}, u32[]{:S(2)}, u32[]{:S(2)}) collective-permute-start(bf16[2,128,512]{2,1,0:T(8,128)(2,1)S(1)} %get-tuple-element.34), channel_id=1, source_target_pairs={{0,63},{1,0},{2,1},{3,2},{4,3},{5,4},{6,5},{7,6},{8,7},{9,8},{10,9... | collective-permute-start | bytes 786440 | tf_op jit(solution)/shard_map/ppermute | solution.py:290
  106.7 17.9 %all-to-all-start.3 = ((bf16[32,8,896]{2,1,0:T(8,128)(2,1)}), bf16[32,8,896]{2,1,0:T(8,128)(2,1)S(1)}, u32[]{:S(2)}, u32[]{:S(2)}) async-start(bf16[32,8,896]{2,1,0:T(8,128)(2,1)} %bitcast.14), calls=%async_computation.3 | async-start | bytes 917504 | tf_op jit(solution)/shard_map/all_to_all | solution.py:285
  125.5 17.1 %all-to-all-start.4 = ((bf16[16,2,896]{2,1,0:T(2,128)(2,1)}), bf16[16,2,896]{2,1,0:T(2,128)(2,1)S(1)}, u32[]{:S(2)}, u32[]{:S(2)}) async-start(bf16[16,2,896]{2,1,0:T(2,128)(2,1)} %combine.1), calls=%async_computation.4 | async-start | bytes 114688 | tf_op jit(solution)/shard_map/all_to_all | solution.py:285
